TPU v7x, 512 devices: a whole 4x8x8 slice. The times are simulated.
512 devices in a mesh: px: 32 (over z, x), py: 16 (over y, core).
Axes of the slice: x: 4, y: 8, z: 8, core: 2. Of those that a mesh axis runs over, the one named last changes fastest.
Arguments:
- node_latents: bfloat16 [32, 16, 2048, 128], P('px', 'py'), may hold values from -6 to 6
- edge_latents: bfloat16 [32, 16, 1024, 128], P('px', 'py'), may hold values from -6 to 6
- edge_senders: int32 [32, 16, 1024], P('px', 'py'), may hold values from 0 to 3071
- edge_receivers: int32 [32, 16, 1024], P('px', 'py'), may hold values from 0 to 2047
- send_rows: int32 [32, 16, 256], P('px', 'py'), may hold values from 0 to 2047
- clusters: int32 [32, 16, 2048], P('px', 'py'), may hold values from 0 to 4095, as said below
- coarse_senders: int32 [32, 16, 1024], P('px', 'py'), may hold values from 0 to 1279
- coarse_receivers: int32 [32, 16, 1024], P('px', 'py'), may hold values from 0 to 255
- fine_edge_in: bfloat16 [384, 128], replicated, may hold values from -0.3125 to 0.3125
- fine_edge_out: bfloat16 [128, 128], replicated, may hold values from -0.5 to 0.5
- fine_node_in: bfloat16 [256, 128], replicated, may hold values from -0.375 to 0.375
- fine_node_out: bfloat16 [128, 128], replicated, may hold values from -0.5 to 0.5
- coarse_edge_in: bfloat16 [256, 128], replicated, may hold values from -0.375 to 0.375
- coarse_edge_out: bfloat16 [128, 128], replicated, may hold values from -0.5 to 0.5
- coarse_node_in: bfloat16 [256, 128], replicated, may hold values from -0.375 to 0.375
- coarse_node_out: bfloat16 [128, 128], replicated, may hold values from -0.5 to 0.5
- prolong_in: bfloat16 [256, 128], replicated, may hold values from -0.375 to 0.375
- prolong_out: bfloat16 [128, 128], replicated, may hold values from -0.5 to 0.5
Outputs:
- node_out: bfloat16 [32, 16, 2048, 128], P('px', 'py')
- edge_out: bfloat16 [32, 16, 1024, 128], P('px', 'py')
Inputs may be any that keep to these rules, and one draw needn't show every extreme that they name: `clusters`: A cell of partition (i, j) belongs to a cluster of partition (i, j-1), (i, j) or (i, j+1) of the same row.
All inputs are finite; a program needn't handle non-finite values.
Results may differ from a plain program's by a relative error of at most 0.0095.
Values may be sent and summed in bfloat16 or wider, within the bound.
No kernel may reach another device: no remote copies, remote signals or barrier semaphores. Data moves between devices by JAX's collectives and lax.ppermute only.
A program may use at most 64 MiB of HBM per device.

v0:
```python
import jax
import jax.numpy as jnp
from jax import lax
from jax.sharding import PartitionSpec as P

CLUS_DEV = 256
FAN = 8


def with_halo(cells, sides, width):
    for axis, dim in sides:
        count = lax.axis_size(axis)
        ends = count - 1
        head = lax.slice_in_dim(cells, 0, width, axis=dim)
        tail = lax.slice_in_dim(cells, cells.shape[dim] - width, cells.shape[dim], axis=dim)
        cells = jnp.concatenate(
            [
                lax.ppermute(tail, axis, [(i, (i + 1) % count) for i in range(ends)]),
                cells,
                lax.ppermute(head, axis, [((i + 1) % count, i) for i in range(ends)]),
            ],
            axis=dim,
        )
    return cells


def layer_norm(values):
    mean = jnp.mean(values, axis=-1, keepdims=True)
    centred = values - mean
    spread = jnp.mean(centred * centred, axis=-1, keepdims=True)
    return centred * lax.rsqrt(spread + 1e-05)


def perceptron(inputs, first, second):
    hidden = jnp.maximum(jnp.dot(inputs, first, preferred_element_type=jnp.float32), 0.0).astype(
        jnp.bfloat16
    )
    return layer_norm(jnp.dot(hidden, second, preferred_element_type=jnp.float32))


def fine_layer(nodes, edges, senders, receivers, send_rows, weights):
    edge_in, edge_out, node_in, node_out = weights
    outgoing = jnp.take(nodes, send_rows, axis=0)[None, None]
    beside_all = with_halo(outgoing, (("px", 0), ("py", 1)), 1)
    parts_list = [beside_all[0, 1], beside_all[2, 1], beside_all[1, 0], beside_all[1, 2]]
    table = jnp.concatenate([nodes] + parts_list, axis=0)
    inputs = jnp.concatenate(
        [edges, jnp.take(table, senders, axis=0), jnp.take(nodes, receivers, axis=0)], axis=1
    )
    message = perceptron(inputs, edge_in, edge_out)
    new_edges = (edges.astype(jnp.float32) + message).astype(jnp.bfloat16)
    gathered = jax.ops.segment_sum(message, receivers, num_segments=nodes.shape[0]).astype(
        jnp.bfloat16
    )
    update = perceptron(jnp.concatenate([nodes, gathered], axis=1), node_in, node_out)
    new_nodes = (nodes.astype(jnp.float32) + update).astype(jnp.bfloat16)
    return (new_nodes, new_edges)


def on_device(
    node_latents,
    edge_latents,
    edge_senders,
    edge_receivers,
    send_rows,
    clusters,
    coarse_senders,
    coarse_receivers,
    fine_edge_in,
    fine_edge_out,
    fine_node_in,
    fine_node_out,
    coarse_edge_in,
    coarse_edge_out,
    coarse_node_in,
    coarse_node_out,
    prolong_in,
    prolong_out,
):
    width = node_latents.shape[3]
    owned = CLUS_DEV
    column = lax.axis_index("py")
    nodes = node_latents[0, 0]
    edges = edge_latents[0, 0]
    senders = edge_senders[0, 0]
    receivers = edge_receivers[0, 0]
    outgoing_rows = send_rows[0, 0]
    local_labels = clusters[0, 0] - (column - 1) * owned
    weights = (fine_edge_in, fine_edge_out, fine_node_in, fine_node_out)
    cells_one, edges_one = fine_layer(nodes, edges, senders, receivers, outgoing_rows, weights)
    partial_sums = jax.ops.segment_sum(
        cells_one.astype(jnp.float32), local_labels, num_segments=3 * owned
    )
    blocks = partial_sums.reshape(3, owned, width)
    sides = jnp.stack([blocks[0], blocks[2]], axis=0)[None]
    beside = with_halo(sides.astype(jnp.bfloat16), (("py", 0),), 1).astype(sides.dtype)
    sums = blocks[1] + beside[0, 1] + beside[2, 0]
    pooled = (sums / FAN).astype(jnp.bfloat16)
    beside_all = with_halo(pooled[None, None], (("px", 0), ("py", 1)), 1)
    coarse_table = jnp.concatenate(
        [pooled, beside_all[0, 1], beside_all[2, 1], beside_all[1, 0], beside_all[1, 2]], axis=0
    )
    coarse_targets = coarse_receivers[0, 0]
    inputs = jnp.concatenate(
        [
            jnp.take(coarse_table, coarse_senders[0, 0], axis=0),
            jnp.take(pooled, coarse_targets, axis=0),
        ],
        axis=1,
    )
    message = perceptron(inputs, coarse_edge_in, coarse_edge_out)
    gathered = jax.ops.segment_sum(message, coarse_targets, num_segments=owned).astype(jnp.bfloat16)
    update = perceptron(
        jnp.concatenate([pooled, gathered], axis=1), coarse_node_in, coarse_node_out
    )
    coarse = (pooled.astype(jnp.float32) + update).astype(jnp.bfloat16)
    coarse_near = with_halo(coarse[None], (("py", 0),), 1)
    coarse_local = coarse_near.reshape(3 * owned, width)
    looked = jnp.take(coarse_local, local_labels, axis=0)
    lifted = perceptron(jnp.concatenate([cells_one, looked], axis=1), prolong_in, prolong_out)
    cells_two = (cells_one.astype(jnp.float32) + lifted).astype(jnp.bfloat16)
    node_final, edge_final = fine_layer(
        cells_two, edges_one, senders, receivers, outgoing_rows, weights
    )
    return (node_final[None, None], edge_final[None, None])


def solution(mesh):
    return jax.shard_map(
        on_device,
        mesh=mesh,
        in_specs=(
            P("px", "py", None, None),
            P("px", "py", None, None),
            P("px", "py", None),
            P("px", "py", None),
            P("px", "py", None),
            P("px", "py", None),
            P("px", "py", None),
            P("px", "py", None),
            P(),
            P(),
            P(),
            P(),
            P(),
            P(),
            P(),
            P(),
            P(),
            P(),
        ),
        out_specs=(P("px", "py", None, None), P("px", "py", None, None)),
        check_vma=False,
    )
```

profile of v0, /device:TPU:223, one launch (start us, length us, event | category | flops | bytes accessed | tf_op | source)
XLA Modules:
  0.0 170.0 jit_solution(18342704604936600191)
XLA Ops:
  0.7 0.7 compare_select_fusion.8
  1.4 0.7 compare_and_fusion.5
  2.1 0.7 pad_clamp_fusion
  2.8 1.8 %gather_fusion.3 = bf16[256,128]{1,0:T(8,128)(2,1)S(1)} fusion(bf16[2048,128]{1,0:T(8,128)(2,1)} %bitcast.106, s32[1024]{0:T(1024)S(1)} %get-tuple-element.38), kind=kCustom, calls=%fused_computation.clone | custom fusion | bytes 132096 | tf_op jit(solution)/shard_map/jit(_take)/gather | solution.py:43
  4.8 5.1 %collective-permute-start = (bf16[1,1,256,128]{2,3,1,0:T(8,128)(2,1)S(1)}, bf16[1,1,256,128]{2,3,1,0:T(8,128)(2,1)S(1)}, u32[]{:S(2)}, u32[]{:S(2)}) collective-permute-start(bf16[1,1,256,128]{2,3,1,0:T(8,128)(2,1)S(1)} %select_bitcast_fusion.1), channel_id=1, source_target_pairs={{0,16},{16,32},{32,48},{48,64},{64,80},{80,96},{96,112},{112,128},... | collective-permute-start | bytes 196616 | tf_op jit(solution)/shard_map/ppermute | solution.py:18
  9.9 1.9 %collective-permute-start.1 = (bf16[1,1,256,128]{2,3,1,0:T(8,128)(2,1)S(1)}, bf16[1,1,256,128]{2,3,1,0:T(8,128)(2,1)S(1)}, u32[]{:S(2)}, u32[]{:S(2)}) collective-permute-start(bf16[1,1,256,128]{2,3,1,0:T(8,128)(2,1)S(1)} %select_bitcast_fusion.1), channel_id=1, source_target_pairs={{16,0},{32,16},{48,32},{64,48},{80,64},{96,80},{112,96},{128,112},... | collective-permute-start | bytes 196616 | tf_op jit(solution)/shard_map/ppermute | solution.py:20
  11.8 0.7 compare_and_fusion.1
  12.8 3.2 %gather_fusion.5 = bf16[1024,128]{1,0:T(8,128)(2,1)S(1)} fusion(bf16[2048,128]{1,0:T(8,128)(2,1)S(1)} %bitcast.107, s32[1024]{0:T(1024)S(1)} %get-tuple-element.39), kind=kCustom, calls=%fused_computation.2.clone | custom fusion | bytes 528384 | tf_op jit(solution)/shard_map/jit(_take)/gather | solution.py:48
  16.2 0.4 copy-done.6
  17.2 1.1 collective-permute-done.1
  18.3 6.4 %collective-permute-start.2 = (bf16[3,1,256,128]{2,3,1,0:T(8,128)(2,1)S(1)}, bf16[3,1,256,128]{2,3,1,0:T(8,128)(2,1)S(1)}, u32[]{:S(2)}, u32[]{:S(2)}) collective-permute-start(bf16[3,1,256,128]{2,3,1,0:T(8,128)(2,1)S(1)} %pad_maximum_fusion), channel_id=1, source_target_pairs={{0,1},{1,2},{2,3},{3,4},{4,5},{5,6},{6,7},{7,8},{8,9},{9,10},{10,1... | collective-permute-start | bytes 589832 | tf_op jit(solution)/shard_map/ppermute | solution.py:18
  24.7 1.9 %collective-permute-start.3 = (bf16[3,1,256,128]{2,3,1,0:T(8,128)(2,1)S(1)}, bf16[3,1,256,128]{2,3,1,0:T(8,128)(2,1)S(1)}, u32[]{:S(2)}, u32[]{:S(2)}) collective-permute-start(bf16[3,1,256,128]{2,3,1,0:T(8,128)(2,1)S(1)} %pad_maximum_fusion), channel_id=1, source_target_pairs={{1,0},{2,1},{3,2},{4,3},{5,4},{6,5},{7,6},{8,7},{9,8},{10,9},{11,1... | collective-permute-start | bytes 589832 | tf_op jit(solution)/shard_map/ppermute | solution.py:20
  26.6 0.6 collective-permute-done.2
  27.3 5.6 %collective-permute-done.3 = bf16[3,1,256,128]{2,3,1,0:T(8,128)(2,1)S(1)} collective-permute-done((bf16[3,1,256,128]{2,3,1,0:T(8,128)(2,1)S(1)}, bf16[3,1,256,128]{2,3,1,0:T(8,128)(2,1)S(1)}, u32[]{:S(2)}, u32[]{:S(2)}) %collective-permute-start.3) | collective-permute-done | bytes 196640 | tf_op jit(solution)/shard_map/ppermute | solution.py:20
  32.9 0.4 copy.41
  33.2 3.2 %gather_fusion.4 = bf16[1024,128]{1,0:T(8,128)(2,1)S(1)} fusion(bf16[3072,128]{1,0:T(8,128)(2,1)S(1)} %copy.41, s32[1024]{0:T(1024)S(1)} %fusion.94), kind=kCustom, calls=%fused_computation.1.clone | custom fusion | bytes 528384 | tf_op jit(solution)/shard_map/jit(_take)/gather | solution.py:48
  36.7 0.6 copy-done.15
  37.2 0.6 fusion.118
  37.9 0.8 add_convert_fusion.4
  38.9 6.4 %scatter_custom_fusion = f32[2048,128]{1,0:T(8,128)S(1)} fusion(s32[1024]{0:T(1024)} %bitcast.120, f32[1024,128]{1,0:T(8,128)S(1)} %copy.45, f32[]{:T(128)} %constant.77.clone.1), kind=kCustom, calls=%fused_computation.73 | custom fusion | flops 131072 | bytes 1049088 | tf_op jit(solution)/shard_map/scatter-add | solution.py:52
  45.6 0.6 copy-done.11
  46.2 0.8 fusion.121
  47.6 11.6 %scatter_custom_fusion.1 = f32[768,128]{1,0:T(8,128)S(1)} fusion(s32[2048]{0:T(1024)S(1)} %bitcast.110, f32[2048,128]{1,0:T(8,128)S(1)} %copy.47, f32[]{:T(128)} %constant.77.clone.1), kind=kCustom, calls=%fused_computation.93 | custom fusion | flops 262144 | bytes 393220 | tf_op jit(solution)/shard_map/scatter-add | solution.py:91
  59.2 1.9 %collective-permute-start.5 = (bf16[1,2,256,128]{3,2,1,0:T(8,128)(2,1)S(1)}, bf16[1,2,256,128]{3,2,1,0:T(8,128)(2,1)S(1)}, u32[]{:S(2)}, u32[]{:S(2)}) collective-permute-start(bf16[1,2,256,128]{3,2,1,0:T(8,128)(2,1)S(1)} %pad_maximum_fusion.4), channel_id=1, source_target_pairs={{1,0},{2,1},{3,2},{4,3},{5,4},{6,5},{7,6},{8,7},{9,8},{10,9},{11,1... | collective-permute-start | bytes 393224 | tf_op jit(solution)/shard_map/ppermute | solution.py:20
  61.1 4.9 %collective-permute-start.4 = (bf16[1,2,256,128]{3,2,1,0:T(8,128)(2,1)S(1)}, bf16[1,2,256,128]{3,2,1,0:T(8,128)(2,1)S(1)}, u32[]{:S(2)}, u32[]{:S(2)}) collective-permute-start(bf16[1,2,256,128]{3,2,1,0:T(8,128)(2,1)S(1)} %pad_maximum_fusion.4), channel_id=1, source_target_pairs={{0,1},{1,2},{2,3},{3,4},{4,5},{5,6},{6,7},{7,8},{8,9},{9,10},{10,1... | collective-permute-start | bytes 393224 | tf_op jit(solution)/shard_map/ppermute | solution.py:18
  66.0 0.7 collective-permute-done.5
  66.7 1.2 collective-permute-done.4
  67.9 4.8 %collective-permute-start.6 = (bf16[1,1,256,128]{3,2,1,0:T(8,128)(2,1)S(1)}, bf16[1,1,256,128]{3,2,1,0:T(8,128)(2,1)S(1)}, u32[]{:S(2)}, u32[]{:S(2)}) collective-permute-start(bf16[1,1,256,128]{3,2,1,0:T(8,128)(2,1)S(1)} %get-tuple-element.17), channel_id=1, source_target_pairs={{0,16},{16,32},{32,48},{48,64},{64,80},{80,96},{96,112},{112,128},... | collective-permute-start | bytes 196616 | tf_op jit(solution)/shard_map/ppermute | solution.py:18
  72.7 1.9 %collective-permute-start.7 = (bf16[1,1,256,128]{3,2,1,0:T(8,128)(2,1)S(1)}, bf16[1,1,256,128]{3,2,1,0:T(8,128)(2,1)S(1)}, u32[]{:S(2)}, u32[]{:S(2)}) collective-permute-start(bf16[1,1,256,128]{3,2,1,0:T(8,128)(2,1)S(1)} %get-tuple-element.17), channel_id=1, source_target_pairs={{16,0},{32,16},{48,32},{64,48},{80,64},{96,80},{112,96},{128,112},... | collective-permute-start | bytes 196616 | tf_op jit(solution)/shard_map/ppermute | solution.py:20
  74.7 3.2 %gather_fusion.1 = bf16[1024,128]{1,0:T(8,128)(2,1)S(1)} fusion(bf16[256,128]{1,0:T(8,128)(2,1)S(1)} %get-tuple-element.21, s32[1024]{0:T(1024)S(1)} %broadcast_clamp_fusion.1), kind=kCustom, calls=%fused_computation.7 | custom fusion | bytes 528384 | tf_op jit(solution)/shard_map/jit(_take)/gather | solution.py:107
  78.1 2.9 %collective-permute-done.7 = bf16[1,1,256,128]{3,2,1,0:T(8,128)(2,1)S(1)} collective-permute-done((bf16[1,1,256,128]{3,2,1,0:T(8,128)(2,1)S(1)}, bf16[1,1,256,128]{3,2,1,0:T(8,128)(2,1)S(1)}, u32[]{:S(2)}, u32[]{:S(2)}) %collective-permute-start.7) | collective-permute-done | bytes 65568 | tf_op jit(solution)/shard_map/ppermute | solution.py:20
  81.1 7.0 %collective-permute-start.8 = (bf16[3,1,256,128]{3,2,1,0:T(8,128)(2,1)S(1)}, bf16[3,1,256,128]{3,2,1,0:T(8,128)(2,1)S(1)}, u32[]{:S(2)}, u32[]{:S(2)}) collective-permute-start(bf16[3,1,256,128]{3,2,1,0:T(8,128)(2,1)S(1)} %pad_maximum_fusion.1), channel_id=1, source_target_pairs={{0,1},{1,2},{2,3},{3,4},{4,5},{5,6},{6,7},{7,8},{8,9},{9,10},{10,1... | collective-permute-start | bytes 589832 | tf_op jit(solution)/shard_map/ppermute | solution.py:18
  88.1 2.1 %collective-permute-start.9 = (bf16[3,1,256,128]{3,2,1,0:T(8,128)(2,1)S(1)}, bf16[3,1,256,128]{3,2,1,0:T(8,128)(2,1)S(1)}, u32[]{:S(2)}, u32[]{:S(2)}) collective-permute-start(bf16[3,1,256,128]{3,2,1,0:T(8,128)(2,1)S(1)} %pad_maximum_fusion.1), channel_id=1, source_target_pairs={{1,0},{2,1},{3,2},{4,3},{5,4},{6,5},{7,6},{8,7},{9,8},{10,9},{11,1... | collective-permute-start | bytes 589832 | tf_op jit(solution)/shard_map/ppermute | solution.py:20
  90.2 0.4 collective-permute-done.8
  90.7 5.6 %collective-permute-done.9 = bf16[3,1,256,128]{3,2,1,0:T(8,128)(2,1)S(1)} collective-permute-done((bf16[3,1,256,128]{3,2,1,0:T(8,128)(2,1)S(1)}, bf16[3,1,256,128]{3,2,1,0:T(8,128)(2,1)S(1)}, u32[]{:S(2)}, u32[]{:S(2)}) %collective-permute-start.9) | collective-permute-done | bytes 196640 | tf_op jit(solution)/shard_map/ppermute | solution.py:20
  96.3 3.2 %gather_fusion = bf16[1024,128]{1,0:T(8,128)(2,1)S(1)} fusion(bf16[1280,128]{1,0:T(8,128)(2,1)S(1)} %fusion.87, s32[1024]{0:T(1024)S(1)} %broadcast_clamp_fusion.2), kind=kCustom, calls=%fused_computation.6 | custom fusion | bytes 528384 | tf_op jit(solution)/shard_map/jit(_take)/gather | solution.py:106
  99.8 0.6 fusion.124
  100.7 6.1 %scatter_custom_fusion.2 = f32[256,128]{1,0:T(8,128)S(1)} fusion(s32[1024]{0:T(1024)S(1)} %bitcast.117, f32[1024,128]{1,0:T(8,128)S(1)} %copy.48, f32[]{:T(128)} %constant.77.clone.1), kind=kCustom, calls=%fused_computation.139 | custom fusion | flops 131072 | bytes 131076 | tf_op jit(solution)/shard_map/scatter-add | solution.py:112
  106.8 0.4 fusion.127
  107.6 1.9 %collective-permute-start.11 = (bf16[1,256,128]{2,1,0:T(8,128)(2,1)S(1)}, bf16[1,256,128]{2,1,0:T(8,128)(2,1)S(1)}, u32[]{:S(2)}, u32[]{:S(2)}) collective-permute-start(bf16[1,256,128]{2,1,0:T(8,128)(2,1)S(1)} %fusion.84), channel_id=1, source_target_pairs={{1,0},{2,1},{3,2},{4,3},{5,4},{6,5},{7,6},{8,7},{9,8},{10,9},{11,1... | collective-permute-start | bytes 196616 | tf_op jit(solution)/shard_map/ppermute | solution.py:20
  109.5 4.9 %collective-permute-start.10 = (bf16[1,256,128]{2,1,0:T(8,128)(2,1)S(1)}, bf16[1,256,128]{2,1,0:T(8,128)(2,1)S(1)}, u32[]{:S(2)}, u32[]{:S(2)}) collective-permute-start(bf16[1,256,128]{2,1,0:T(8,128)(2,1)S(1)} %fusion.84), channel_id=1, source_target_pairs={{0,1},{1,2},{2,3},{3,4},{4,5},{5,6},{6,7},{7,8},{8,9},{9,10},{10,1... | collective-permute-start | bytes 196616 | tf_op jit(solution)/shard_map/ppermute | solution.py:18
  114.4 1.3 collective-permute-done.10
  115.7 6.2 %gather_fusion.2 = bf16[2048,128]{1,0:T(8,128)(2,1)S(1)} fusion(bf16[768,128]{1,0:T(8,128)(2,1)S(1)} %bitcast.105, s32[2048]{0:T(1024)S(1)} %broadcast_clamp_fusion), kind=kCustom, calls=%fused_computation.8 | custom fusion | bytes 1056768 | tf_op jit(solution)/shard_map/jit(_take)/gather | solution.py:119
  121.9 0.2 copy.49
  122.2 0.5 copy-done.10
  122.7 0.8 fusion.130
  123.9 0.3 copy.50
  124.2 3.2 %gather_fusion.8 = bf16[1024,128]{1,0:T(8,128)(2,1)S(1)} fusion(bf16[2048,128]{1,0:T(8,128)(2,1)S(1)} %copy.50, s32[1024]{0:T(1024)S(1)} %get-tuple-element.39), kind=kCustom, calls=%fused_computation.5.clone | custom fusion | bytes 528384 | tf_op jit(solution)/shard_map/jit(_take)/gather | solution.py:48
  127.4 0.9 gather_fusion.6
  128.4 2.9 %collective-permute-start.12 = (bf16[1,1,256,128]{2,3,1,0:T(8,128)(2,1)S(1)}, bf16[1,1,256,128]{2,3,1,0:T(8,128)(2,1)S(1)}, u32[]{:S(2)}, u32[]{:S(2)}) collective-permute-start(bf16[1,1,256,128]{2,3,1,0:T(8,128)(2,1)S(1)} %select_bitcast_fusion), channel_id=1, source_target_pairs={{0,16},{16,32},{32,48},{48,64},{64,80},{80,96},{96,112},{112,128},... | collective-permute-start | bytes 196616 | tf_op jit(solution)/shard_map/ppermute | solution.py:18
  131.3 2.4 %collective-permute-start.13 = (bf16[1,1,256,128]{2,3,1,0:T(8,128)(2,1)S(1)}, bf16[1,1,256,128]{2,3,1,0:T(8,128)(2,1)S(1)}, u32[]{:S(2)}, u32[]{:S(2)}) collective-permute-start(bf16[1,1,256,128]{2,3,1,0:T(8,128)(2,1)S(1)} %select_bitcast_fusion), channel_id=1, source_target_pairs={{16,0},{32,16},{48,32},{64,48},{80,64},{96,80},{112,96},{128,112},... | collective-permute-start | bytes 196616 | tf_op jit(solution)/shard_map/ppermute | solution.py:20
  133.9 5.7 %collective-permute-done.13 = bf16[1,1,256,128]{2,3,1,0:T(8,128)(2,1)S(1)} collective-permute-done((bf16[1,1,256,128]{2,3,1,0:T(8,128)(2,1)S(1)}, bf16[1,1,256,128]{2,3,1,0:T(8,128)(2,1)S(1)}, u32[]{:S(2)}, u32[]{:S(2)}) %collective-permute-start.13) | collective-permute-done | bytes 65568 | tf_op jit(solution)/shard_map/ppermute | solution.py:20
  139.7 6.9 %collective-permute-start.14 = (bf16[3,1,256,128]{2,3,1,0:T(8,128)(2,1)S(1)}, bf16[3,1,256,128]{2,3,1,0:T(8,128)(2,1)S(1)}, u32[]{:S(2)}, u32[]{:S(2)}) collective-permute-start(bf16[3,1,256,128]{2,3,1,0:T(8,128)(2,1)S(1)} %pad_maximum_fusion.3), channel_id=1, source_target_pairs={{0,1},{1,2},{2,3},{3,4},{4,5},{5,6},{6,7},{7,8},{8,9},{9,10},{10,1... | collective-permute-start | bytes 589832 | tf_op jit(solution)/shard_map/ppermute | solution.py:18
  146.6 1.9 %collective-permute-start.15 = (bf16[3,1,256,128]{2,3,1,0:T(8,128)(2,1)S(1)}, bf16[3,1,256,128]{2,3,1,0:T(8,128)(2,1)S(1)}, u32[]{:S(2)}, u32[]{:S(2)}) collective-permute-start(bf16[3,1,256,128]{2,3,1,0:T(8,128)(2,1)S(1)} %pad_maximum_fusion.3), channel_id=1, source_target_pairs={{1,0},{2,1},{3,2},{4,3},{5,4},{6,5},{7,6},{8,7},{9,8},{10,9},{11,1... | collective-permute-start | bytes 589832 | tf_op jit(solution)/shard_map/ppermute | solution.py:20
  148.6 0.6 collective-permute-done.14
  149.2 5.6 %collective-permute-done.15 = bf16[3,1,256,128]{2,3,1,0:T(8,128)(2,1)S(1)} collective-permute-done((bf16[3,1,256,128]{2,3,1,0:T(8,128)(2,1)S(1)}, bf16[3,1,256,128]{2,3,1,0:T(8,128)(2,1)S(1)}, u32[]{:S(2)}, u32[]{:S(2)}) %collective-permute-start.15) | collective-permute-done | bytes 196640 | tf_op jit(solution)/shard_map/ppermute | solution.py:20
  154.8 0.4 copy.52
  155.2 3.2 %gather_fusion.7 = bf16[1024,128]{1,0:T(8,128)(2,1)S(1)} fusion(bf16[3072,128]{1,0:T(8,128)(2,1)S(1)} %copy.52, s32[1024]{0:T(1024)S(1)} %fusion.94), kind=kCustom, calls=%fused_computation.4.clone | custom fusion | bytes 528384 | tf_op jit(solution)/shard_map/jit(_take)/gather | solution.py:48
  158.6 0.8 copy-done.2
  159.4 0.6 fusion.133
  160.4 6.4 %scatter_custom_fusion.3 = f32[2048,128]{1,0:T(8,128)S(1)} fusion(s32[1024]{0:T(1024)} %bitcast.121, f32[1024,128]{1,0:T(8,128)S(1)} %copy.56, f32[]{:T(128)} %constant.77.clone.1), kind=kCustom, calls=%fused_computation.69 | custom fusion | flops 131072 | bytes 1049088 | tf_op jit(solution)/shard_map/scatter-add | solution.py:52
  167.0 0.8 fusion.136
  168.1 1.0 copy.58
  169.1 0.8 copy.59
  (117 shorter events, 5.3 us)
Async XLA Ops:
  0.6 36.0 %copy-start = (bf16[384,128]{1,0:T(8,128)(2,1)S(1)}, bf16[384,128]{1,0:T(8,128)(2,1)}, u32[]{:S(2)}) copy-start(bf16[384,128]{1,0:T(8,128)(2,1)} %param.32) | copy-start | bytes 294916
  0.6 11.9 %copy-start.1 = (bf16[1,1,2048,128]{3,2,1,0:T(8,128)(2,1)S(1)}, bf16[1,1,2048,128]{3,2,1,0:T(8,128)(2,1)}, u32[]{:S(2)}) copy-start(bf16[1,1,2048,128]{3,2,1,0:T(8,128)(2,1)} %param.24) | copy-start | bytes 1572868
  0.7 12.1 %copy-start.4 = (s32[1,1,1024]{2,1,0:T(1,128)S(1)}, s32[1,1,1024]{2,1,0:T(1,128)}, u32[]{:S(2)}) copy-start(s32[1,1,1024]{2,1,0:T(1,128)} %param.26) | copy-start | bytes 12292
  4.8 12.4 %collective-permute-start = (bf16[1,1,256,128]{2,3,1,0:T(8,128)(2,1)S(1)}, bf16[1,1,256,128]{2,3,1,0:T(8,128)(2,1)S(1)}, u32[]{:S(2)}, u32[]{:S(2)}) collective-permute-start(bf16[1,1,256,128]{2,3,1,0:T(8,128)(2,1)S(1)} %select_bitcast_fusion.1), channel_id=1, source_target_pairs={{0,16},{16,32},{32,48},{48,64},{64,80},{80,96},{96,112},{112,128},... | collective-permute-start | bytes 196616 | tf_op jit(solution)/shard_map/ppermute | solution.py:18
  9.9 8.3 %collective-permute-start.1 = (bf16[1,1,256,128]{2,3,1,0:T(8,128)(2,1)S(1)}, bf16[1,1,256,128]{2,3,1,0:T(8,128)(2,1)S(1)}, u32[]{:S(2)}, u32[]{:S(2)}) collective-permute-start(bf16[1,1,256,128]{2,3,1,0:T(8,128)(2,1)S(1)} %select_bitcast_fusion.1), channel_id=1, source_target_pairs={{16,0},{32,16},{48,32},{64,48},{80,64},{96,80},{112,96},{128,112},... | collective-permute-start | bytes 196616 | tf_op jit(solution)/shard_map/ppermute | solution.py:20
  16.0 0.7 copy-start.6
  16.0 0.7 copy-start.5
  16.0 0.7 copy-start.7
  16.0 1.0 copy-start.3
  18.3 9.0 %collective-permute-start.2 = (bf16[3,1,256,128]{2,3,1,0:T(8,128)(2,1)S(1)}, bf16[3,1,256,128]{2,3,1,0:T(8,128)(2,1)S(1)}, u32[]{:S(2)}, u32[]{:S(2)}) collective-permute-start(bf16[3,1,256,128]{2,3,1,0:T(8,128)(2,1)S(1)} %pad_maximum_fusion), channel_id=1, source_target_pairs={{0,1},{1,2},{2,3},{3,4},{4,5},{5,6},{6,7},{7,8},{8,9},{9,10},{10,1... | collective-permute-start | bytes 589832 | tf_op jit(solution)/shard_map/ppermute | solution.py:18
  24.7 8.2 %collective-permute-start.3 = (bf16[3,1,256,128]{2,3,1,0:T(8,128)(2,1)S(1)}, bf16[3,1,256,128]{2,3,1,0:T(8,128)(2,1)S(1)}, u32[]{:S(2)}, u32[]{:S(2)}) collective-permute-start(bf16[3,1,256,128]{2,3,1,0:T(8,128)(2,1)S(1)} %pad_maximum_fusion), channel_id=1, source_target_pairs={{1,0},{2,1},{3,2},{4,3},{5,4},{6,5},{7,6},{8,7},{9,8},{10,9},{11,1... | collective-permute-start | bytes 589832 | tf_op jit(solution)/shard_map/ppermute | solution.py:20
  36.5 0.8 copy-start.15
  45.3 0.8 copy-start.11
  45.4 0.8 copy-start.16
  59.2 7.5 %collective-permute-start.5 = (bf16[1,2,256,128]{3,2,1,0:T(8,128)(2,1)S(1)}, bf16[1,2,256,128]{3,2,1,0:T(8,128)(2,1)S(1)}, u32[]{:S(2)}, u32[]{:S(2)}) collective-permute-start(bf16[1,2,256,128]{3,2,1,0:T(8,128)(2,1)S(1)} %pad_maximum_fusion.4), channel_id=1, source_target_pairs={{1,0},{2,1},{3,2},{4,3},{5,4},{6,5},{7,6},{8,7},{9,8},{10,9},{11,1... | collective-permute-start | bytes 393224 | tf_op jit(solution)/shard_map/ppermute | solution.py:20
  61.1 6.8 %collective-permute-start.4 = (bf16[1,2,256,128]{3,2,1,0:T(8,128)(2,1)S(1)}, bf16[1,2,256,128]{3,2,1,0:T(8,128)(2,1)S(1)}, u32[]{:S(2)}, u32[]{:S(2)}) collective-permute-start(bf16[1,2,256,128]{3,2,1,0:T(8,128)(2,1)S(1)} %pad_maximum_fusion.4), channel_id=1, source_target_pairs={{0,1},{1,2},{2,3},{3,4},{4,5},{5,6},{6,7},{7,8},{8,9},{9,10},{10,1... | collective-permute-start | bytes 393224 | tf_op jit(solution)/shard_map/ppermute | solution.py:18
  67.9 10.2 %collective-permute-start.6 = (bf16[1,1,256,128]{3,2,1,0:T(8,128)(2,1)S(1)}, bf16[1,1,256,128]{3,2,1,0:T(8,128)(2,1)S(1)}, u32[]{:S(2)}, u32[]{:S(2)}) collective-permute-start(bf16[1,1,256,128]{3,2,1,0:T(8,128)(2,1)S(1)} %get-tuple-element.17), channel_id=1, source_target_pairs={{0,16},{16,32},{32,48},{48,64},{64,80},{80,96},{96,112},{112,128},... | collective-permute-start | bytes 196616 | tf_op jit(solution)/shard_map/ppermute | solution.py:18
  72.7 8.3 %collective-permute-start.7 = (bf16[1,1,256,128]{3,2,1,0:T(8,128)(2,1)S(1)}, bf16[1,1,256,128]{3,2,1,0:T(8,128)(2,1)S(1)}, u32[]{:S(2)}, u32[]{:S(2)}) collective-permute-start(bf16[1,1,256,128]{3,2,1,0:T(8,128)(2,1)S(1)} %get-tuple-element.17), channel_id=1, source_target_pairs={{16,0},{32,16},{48,32},{64,48},{80,64},{96,80},{112,96},{128,112},... | collective-permute-start | bytes 196616 | tf_op jit(solution)/shard_map/ppermute | solution.py:20
  81.1 9.6 %collective-permute-start.8 = (bf16[3,1,256,128]{3,2,1,0:T(8,128)(2,1)S(1)}, bf16[3,1,256,128]{3,2,1,0:T(8,128)(2,1)S(1)}, u32[]{:S(2)}, u32[]{:S(2)}) collective-permute-start(bf16[3,1,256,128]{3,2,1,0:T(8,128)(2,1)S(1)} %pad_maximum_fusion.1), channel_id=1, source_target_pairs={{0,1},{1,2},{2,3},{3,4},{4,5},{5,6},{6,7},{7,8},{8,9},{9,10},{10,1... | collective-permute-start | bytes 589832 | tf_op jit(solution)/shard_map/ppermute | solution.py:18
  88.1 8.2 %collective-permute-start.9 = (bf16[3,1,256,128]{3,2,1,0:T(8,128)(2,1)S(1)}, bf16[3,1,256,128]{3,2,1,0:T(8,128)(2,1)S(1)}, u32[]{:S(2)}, u32[]{:S(2)}) collective-permute-start(bf16[3,1,256,128]{3,2,1,0:T(8,128)(2,1)S(1)} %pad_maximum_fusion.1), channel_id=1, source_target_pairs={{1,0},{2,1},{3,2},{4,3},{5,4},{6,5},{7,6},{8,7},{9,8},{10,9},{11,1... | collective-permute-start | bytes 589832 | tf_op jit(solution)/shard_map/ppermute | solution.py:20
  96.3 3.5 %copy-start.8 = (bf16[256,128]{1,0:T(8,128)(2,1)S(1)}, bf16[256,128]{1,0:T(8,128)(2,1)}, u32[]{:S(2)}) copy-start(bf16[256,128]{1,0:T(8,128)(2,1)} %param.36) | copy-start | bytes 196612
  96.3 3.5 %copy-start.12 = (bf16[128,128]{1,0:T(8,128)(2,1)S(1)}, bf16[128,128]{1,0:T(8,128)(2,1)}, u32[]{:S(2)}) copy-start(bf16[128,128]{1,0:T(8,128)(2,1)} %param.37) | copy-start | bytes 98308
  100.4 6.4 %copy-start.9 = (bf16[256,128]{1,0:T(8,128)(2,1)S(1)}, bf16[256,128]{1,0:T(8,128)(2,1)}, u32[]{:S(2)}) copy-start(bf16[256,128]{1,0:T(8,128)(2,1)} %param.38) | copy-start | bytes 196612
  100.4 6.4 %copy-start.13 = (bf16[128,128]{1,0:T(8,128)(2,1)S(1)}, bf16[128,128]{1,0:T(8,128)(2,1)}, u32[]{:S(2)}) copy-start(bf16[128,128]{1,0:T(8,128)(2,1)} %param.39) | copy-start | bytes 98308
  107.6 6.8 %collective-permute-start.11 = (bf16[1,256,128]{2,1,0:T(8,128)(2,1)S(1)}, bf16[1,256,128]{2,1,0:T(8,128)(2,1)S(1)}, u32[]{:S(2)}, u32[]{:S(2)}) collective-permute-start(bf16[1,256,128]{2,1,0:T(8,128)(2,1)S(1)} %fusion.84), channel_id=1, source_target_pairs={{1,0},{2,1},{3,2},{4,3},{5,4},{6,5},{7,6},{8,7},{9,8},{10,9},{11,1... | collective-permute-start | bytes 196616 | tf_op jit(solution)/shard_map/ppermute | solution.py:20
  109.5 6.2 %collective-permute-start.10 = (bf16[1,256,128]{2,1,0:T(8,128)(2,1)S(1)}, bf16[1,256,128]{2,1,0:T(8,128)(2,1)S(1)}, u32[]{:S(2)}, u32[]{:S(2)}) collective-permute-start(bf16[1,256,128]{2,1,0:T(8,128)(2,1)S(1)} %fusion.84), channel_id=1, source_target_pairs={{0,1},{1,2},{2,3},{3,4},{4,5},{5,6},{6,7},{7,8},{8,9},{9,10},{10,1... | collective-permute-start | bytes 196616 | tf_op jit(solution)/shard_map/ppermute | solution.py:18
  121.9 0.8 copy-start.10
  121.9 0.8 copy-start.14
  128.4 5.5 %collective-permute-start.12 = (bf16[1,1,256,128]{2,3,1,0:T(8,128)(2,1)S(1)}, bf16[1,1,256,128]{2,3,1,0:T(8,128)(2,1)S(1)}, u32[]{:S(2)}, u32[]{:S(2)}) collective-permute-start(bf16[1,1,256,128]{2,3,1,0:T(8,128)(2,1)S(1)} %select_bitcast_fusion), channel_id=1, source_target_pairs={{0,16},{16,32},{32,48},{48,64},{64,80},{80,96},{96,112},{112,128},... | collective-permute-start | bytes 196616 | tf_op jit(solution)/shard_map/ppermute | solution.py:18
  131.3 8.3 %collective-permute-start.13 = (bf16[1,1,256,128]{2,3,1,0:T(8,128)(2,1)S(1)}, bf16[1,1,256,128]{2,3,1,0:T(8,128)(2,1)S(1)}, u32[]{:S(2)}, u32[]{:S(2)}) collective-permute-start(bf16[1,1,256,128]{2,3,1,0:T(8,128)(2,1)S(1)} %select_bitcast_fusion), channel_id=1, source_target_pairs={{16,0},{32,16},{48,32},{64,48},{80,64},{96,80},{112,96},{128,112},... | collective-permute-start | bytes 196616 | tf_op jit(solution)/shard_map/ppermute | solution.py:20
  139.7 9.5 %collective-permute-start.14 = (bf16[3,1,256,128]{2,3,1,0:T(8,128)(2,1)S(1)}, bf16[3,1,256,128]{2,3,1,0:T(8,128)(2,1)S(1)}, u32[]{:S(2)}, u32[]{:S(2)}) collective-permute-start(bf16[3,1,256,128]{2,3,1,0:T(8,128)(2,1)S(1)} %pad_maximum_fusion.3), channel_id=1, source_target_pairs={{0,1},{1,2},{2,3},{3,4},{4,5},{5,6},{6,7},{7,8},{8,9},{9,10},{10,1... | collective-permute-start | bytes 589832 | tf_op jit(solution)/shard_map/ppermute | solution.py:18
  146.6 8.2 %collective-permute-start.15 = (bf16[3,1,256,128]{2,3,1,0:T(8,128)(2,1)S(1)}, bf16[3,1,256,128]{2,3,1,0:T(8,128)(2,1)S(1)}, u32[]{:S(2)}, u32[]{:S(2)}) collective-permute-start(bf16[3,1,256,128]{2,3,1,0:T(8,128)(2,1)S(1)} %pad_maximum_fusion.3), channel_id=1, source_target_pairs={{1,0},{2,1},{3,2},{4,3},{5,4},{6,5},{7,6},{8,7},{9,8},{10,9},{11,1... | collective-permute-start | bytes 589832 | tf_op jit(solution)/shard_map/ppermute | solution.py:20
  158.4 1.0 copy-start.2
where the time goes:
time: 171 us; the launch traced here: 170 us
  starting transfers between devices  58.8 us (34%)
  local copies, waits for them, and re-layouts  36.8 us (22%)
  other arithmetic  36.6 us (21%)
  waiting for transfers between devices  31.4 us (18%)
  matrix products  4.63 us (3%)
    ppermute x8, starting transfers between devices, with_halo(): lax.ppermute(tail, axis, [(i, (i + 1) % count) for i in range(ends)])  42.8 us
    ppermute x8, waiting for transfers between devices, with_halo(): lax.ppermute(head, axis, [((i + 1) % count, i) for i in range(ends)])  27.2 us
    ppermute x8, starting transfers between devices, with_halo(): lax.ppermute(head, axis, [((i + 1) % count, i) for i in range(ends)])  16 us
    scatter-add x2, other arithmetic, fine_layer(): jax.ops.segment_sum(message, receivers, num_segments=nodes.shape[0])  12.8 us
    scatter-add x1, other arithmetic, on_device(): jax.ops.segment_sum(cells_one.astype(jnp.float32), local_labels, num_segm...  11.6 us
    gather x4, local copies, waits for them, and re-layouts, fine_layer(): jnp.take(table, senders, axis=0)  6.71 us
    gather x4, local copies, waits for them, and re-layouts, fine_layer(): jnp.take(nodes, receivers, axis=0)  6.71 us
    gather x2, local copies, waits for them, and re-layouts, on_device(): looked = jnp.take(coarse_local, local_labels, axis=0)  6.4 us
  transfers between devices with their start and end apart: 16, of which 12 were waited for; matrix products, arithmetic and copies ran while one was open for 5% of the time, Pallas kernels for 0%

commit v1 on v0

v1 whole, which is shorter than its diff:
```python
import functools

import jax
import jax.numpy as jnp
from jax import lax
from jax.experimental import pallas as pl
from jax.experimental.pallas import tpu as pltpu
from jax.sharding import PartitionSpec as P

LATENT = 128
CELLS = 2048
EDGES = 1024
RIM = 256
CLUS = 256
CEDGES = 1024
FAN = 8
ROWS = 4
BF16 = jnp.bfloat16
F32 = jnp.float32
VMEM = pl.BlockSpec(memory_space=pltpu.VMEM)
SMEM = pl.BlockSpec(memory_space=pltpu.SMEM)
PARAMS = pltpu.CompilerParams(vmem_limit_bytes=24 * 1024 * 1024)


def cost(flops, moved):
    return pl.CostEstimate(flops=flops, bytes_accessed=moved, transcendentals=0)


def dot(a, b):
    return jnp.dot(a, b, preferred_element_type=F32)


def column(ref, start, count):
    parts = []
    for k in range(count):
        row = ref[pl.ds(start + k, 1), :]
        parts.append(jnp.transpose(jnp.broadcast_to(row, (128, 128))))
    return jnp.concatenate(parts, axis=0)


def pick_rows(code, depth, low):
    code = code.astype(F32).astype(BF16)
    blocks = []
    for b in range(depth // 128):
        lane = lax.broadcasted_iota(jnp.int32, code.shape, 1) + (low + 128 * b)
        hit = code == lane.astype(F32).astype(BF16)
        blocks.append(jnp.where(hit, jnp.ones_like(code), jnp.zeros_like(code)))
    return jnp.concatenate(blocks, axis=1)


def pick_columns(ref, code_of, depth, low, count):
    row = lax.broadcasted_iota(jnp.int32, (depth, 128), 0) + low
    row = row.astype(F32).astype(BF16)
    blocks = []
    for c in range(count):
        code = code_of(ref[pl.ds(c, 1), :]).astype(F32).astype(BF16)
        hit = jnp.broadcast_to(code, (depth, 128)) == row
        blocks.append(jnp.where(hit, jnp.ones_like(row), jnp.zeros_like(row)))
    return jnp.concatenate(blocks, axis=1)


def side_by_side(table, folds):
    depth = table.shape[0] // folds
    return jnp.concatenate([table[f * depth : (f + 1) * depth] for f in range(folds)], axis=1)


def choose(wide, which, folds):
    out = wide[:, :LATENT]
    for f in range(1, folds):
        out = jnp.where(which == f, wide[:, f * LATENT : (f + 1) * LATENT], out)
    return out


def layer_norm(values):
    mean = jnp.mean(values, axis=-1, keepdims=True)
    centred = values - mean
    spread = jnp.mean(centred * centred, axis=-1, keepdims=True)
    return centred * lax.rsqrt(spread + 1e-05)


def finish(pre, second):
    return layer_norm(dot(jnp.maximum(pre, 0.0).astype(BF16), second))


def from_cells(table, index):
    code = jnp.where(index < CELLS, (index & 511) - 256, 512)
    wide = dot(pick_rows(code, 512, -256), table)
    return choose(wide, index >> 9, 4).astype(BF16)


def from_halo(table, index):
    code = jnp.where(index >= 0, index & 255, 512)
    wide = dot(pick_rows(code, 256, 0), table)
    return choose(wide, index >> 8, 4).astype(BF16)


def halo_table(flags, left, right, first, second, cross):
    a, b, c = first[...], second[...], cross[...]
    zero = jnp.zeros_like(a)
    up = jnp.where(flags[0] == 0, a, jnp.where(flags[0] == 1, b, jnp.where(flags[0] == 2, c, zero)))
    down = jnp.where(flags[1] == 0, a, jnp.where(flags[1] == 1, b, jnp.where(flags[1] == 2, c, zero)))
    west = jnp.where(flags[2] == 0, zero, left[...])
    east = jnp.where(flags[3] == 0, zero, right[...])
    return jnp.concatenate([up, down, west, east], axis=1)


def outgoing_kernel(nodes, rows, out):
    table = side_by_side(nodes[...], 4)
    out[...] = from_cells(table, column(rows, 0, 2))


def fine_local_kernel(nodes, edges, senders, receivers, first, out):
    table = side_by_side(nodes[...], 4)

    def body(i, carry):
        index = jnp.concatenate([column(senders, 2 * i, 2), column(receivers, 2 * i, 2)], axis=0)
        near = from_cells(table, index)
        at = pl.ds(pl.multiple_of(i * 256, 256), 256)
        inputs = jnp.concatenate([edges[at, :], near[:256], near[256:]], axis=1)
        out[at, :] = dot(inputs, first[...])
        return carry

    lax.fori_loop(0, 4, body, 0)


def fine_rest(
    flags, pre, edges, nodes, senders, receivers, halo, edge_in, edge_out, node_in, node_out, new_edges, wide, sums
):
    table = halo_table(flags, *halo)

    def edge_body(i, carry):
        at = pl.ds(pl.multiple_of(i * 256, 256), 256)
        far = from_halo(table, column(senders, 2 * i, 2) - CELLS)
        message = finish(pre[at, :] + dot(far, edge_in[LATENT : 2 * LATENT, :]), edge_out[...])
        new_edges[at, :] = (edges[at, :].astype(F32) + message).astype(BF16)
        quarter = column(receivers, 2 * i, 2) >> 9
        wide[at, :] = jnp.concatenate(
            [jnp.where(quarter == f, message, 0.0) for f in range(4)], axis=1
        ).astype(BF16)
        return carry

    lax.fori_loop(0, 4, edge_body, 0)
    spread = pick_columns(receivers, lambda r: (r & 511) - 256, 512, -256, 8)
    total = dot(spread, wide[...]).astype(BF16)
    for f in range(4):
        sums[f] = total[:, f * LATENT : (f + 1) * LATENT]


def node_update(f, nodes, sums, node_in, node_out):
    at = pl.ds(pl.multiple_of(f * 512, 512), 512)
    cells = nodes[at, :]
    inputs = jnp.concatenate([cells, sums[f]], axis=1)
    return at, (cells.astype(F32) + finish(dot(inputs, node_in[...]), node_out[...])).astype(BF16)


def fine_pool_kernel(
    flags, pre, edges, nodes, senders, receivers, left, right, first, second, cross,
    edge_in, edge_out, node_in, node_out, labels,
    new_nodes, new_edges, own, to_left, to_right, wide, sums, masked,
):
    fine_rest(
        flags, pre, edges, nodes, senders, receivers, (left, right, first, second, cross),
        edge_in, edge_out, node_in, node_out, new_edges, wide, sums,
    )
    base = flags[4]

    def node_body(f, carry):
        at, cells = node_update(f, nodes, sums, node_in, node_out)
        new_nodes[at, :] = cells
        block = (column(labels, 4 * f, 4) - base) >> 8
        masked[at, :] = jnp.concatenate(
            [jnp.where(block == b, cells.astype(F32), 0.0) for b in range(3)], axis=1
        ).astype(BF16)
        return carry

    lax.fori_loop(0, 4, node_body, 0)
    spread = pick_columns(labels, lambda r: r & 255, 256, 0, 16)
    total = dot(spread, masked[...])
    to_left[...] = total[:, :LATENT].astype(BF16)
    own[...] = total[:, LATENT : 2 * LATENT]
    to_right[...] = total[:, 2 * LATENT :].astype(BF16)


def fine_last_kernel(
    flags, pre, edges, nodes, senders, receivers, left, right, first, second, cross,
    edge_in, edge_out, node_in, node_out,
    new_nodes, new_edges, wide, sums,
):
    fine_rest(
        flags, pre, edges, nodes, senders, receivers, (left, right, first, second, cross),
        edge_in, edge_out, node_in, node_out, new_edges, wide, sums,
    )

    def node_body(f, carry):
        at, cells = node_update(f, nodes, sums, node_in, node_out)
        new_nodes[at, :] = cells
        return carry

    lax.fori_loop(0, 4, node_body, 0)


def coarse_local_kernel(pooled, senders, receivers, first, out):
    table = pooled[...]

    def body(i, carry):
        index = jnp.concatenate([column(senders, 2 * i, 2), column(receivers, 2 * i, 2)], axis=0)
        code = jnp.where(index < CLUS, index, 512)
        near = dot(pick_rows(code, 256, 0), table).astype(BF16)
        at = pl.ds(pl.multiple_of(i * 256, 256), 256)
        out[at, :] = dot(jnp.concatenate([near[:256], near[256:]], axis=1), first[...])
        return carry

    lax.fori_loop(0, 4, body, 0)


def coarse_kernel(
    flags, pre, pooled, senders, receivers, left, right, first, second, cross,
    edge_in, edge_out, node_in, node_out, out, messages,
):
    table = halo_table(flags, left, right, first, second, cross)

    def body(i, carry):
        at = pl.ds(pl.multiple_of(i * 256, 256), 256)
        far = from_halo(table, column(senders, 2 * i, 2) - CLUS)
        message = finish(pre[at, :] + dot(far, edge_in[:LATENT, :]), edge_out[...])
        messages[at, :] = message.astype(BF16)
        return carry

    lax.fori_loop(0, 4, body, 0)
    spread = pick_columns(receivers, lambda r: r, 256, 0, 8)
    gathered = dot(spread, messages[...]).astype(BF16)
    own = pooled[...]
    update = finish(dot(jnp.concatenate([own, gathered], axis=1), node_in[...]), node_out[...])
    out[...] = (own.astype(F32) + update).astype(BF16)


def prolong_kernel(flags, cells, labels, own, left, right, rows, first, second, new_cells, outgoing):
    table = jnp.concatenate([left[...], own[...], right[...]], axis=1)
    base = flags[4]

    def body(f, carry):
        at = pl.ds(pl.multiple_of(f * 512, 512), 512)
        index = column(labels, 4 * f, 4) - base
        wide = dot(pick_rows(index & 255, 256, 0), table)
        looked = choose(wide, index >> 8, 3).astype(BF16)
        old = cells[at, :]
        update = finish(dot(jnp.concatenate([old, looked], axis=1), first[...]), second[...])
        new_cells[at, :] = (old.astype(F32) + update).astype(BF16)
        return carry

    lax.fori_loop(0, 4, body, 0)
    outgoing[...] = from_cells(side_by_side(new_cells[...], 4), column(rows, 0, 2))


def shape(*dims, dtype=BF16):
    return jax.ShapeDtypeStruct(dims, dtype)


def call(kernel, outs, ins, args, name, estimate, scratch=()):
    return pl.pallas_call(
        kernel,
        out_shape=outs,
        in_specs=ins,
        out_specs=jax.tree.map(lambda _: VMEM, outs),
        scratch_shapes=scratch,
        compiler_params=PARAMS,
        cost_estimate=estimate,
        name=name,
    )(*args)


def snake(count_x, count_y):
    pairs = []
    for i in range(count_x):
        for j in range(count_y):
            if j % 2 == 0:
                to = (i + 1, j) if i % ROWS < ROWS - 1 else (i, j + 1)
            else:
                to = (i - 1, j) if i % ROWS > 0 else (i, j - 1)
            pairs.append((i * count_y + j, to[0] * count_y + to[1]))
    return pairs


def exchange(block):
    count_x, count_y = lax.axis_size("px"), lax.axis_size("py")
    ring = snake(count_x, count_y)
    crossing = []
    for k in range(ROWS - 1, count_x - 1, ROWS):
        crossing += [(k, k + 1), (k + 1, k)]
    left, right = exchange_row(block, block)
    first = lax.ppermute(block, ("px", "py"), ring)
    second = lax.ppermute(block, ("px", "py"), [(b, a) for a, b in ring])
    cross = lax.ppermute(block, "px", crossing)
    return left, right, first, second, cross


def exchange_row(to_left, to_right):
    count = lax.axis_size("py")
    from_left = lax.ppermute(to_right, "py", [(i, (i + 1) % count) for i in range(count)])
    from_right = lax.ppermute(to_left, "py", [((i + 1) % count, i) for i in range(count)])
    return from_left, from_right


def on_device(
    node_latents, edge_latents, edge_senders, edge_receivers, send_rows, clusters, coarse_senders, coarse_receivers,
    fine_edge_in, fine_edge_out, fine_node_in, fine_node_out,
    coarse_edge_in, coarse_edge_out, coarse_node_in, coarse_node_out, prolong_in, prolong_out,
):
    nodes, edges = node_latents[0, 0], edge_latents[0, 0]
    senders, receivers = edge_senders.reshape(8, 128), edge_receivers.reshape(8, 128)
    rows, labels = send_rows.reshape(2, 128), clusters.reshape(16, 128)
    csenders, creceivers = coarse_senders.reshape(8, 128), coarse_receivers.reshape(8, 128)
    i, j = lax.axis_index("px"), lax.axis_index("py")
    last_i, last_j = lax.axis_size("px") - 1, lax.axis_size("py") - 1
    core, along = j % 2, i % ROWS
    up = jnp.where(along > 0, core, jnp.where(i > 0, 2, 3))
    down = jnp.where(along < ROWS - 1, 1 - core, jnp.where(i < last_i, 2, 3))
    flags = jnp.stack([up, down, j > 0, j < last_j, (j - 1) * CLUS]).astype(jnp.int32)

    def fine_local(nodes, edges):
        return call(
            fine_local_kernel, shape(EDGES, LATENT, dtype=F32), [VMEM] * 5,
            (nodes, edges, senders, receivers, fine_edge_in), "fine_local", cost(4_000_000_000, 2_000_000),
        )

    weights = (fine_edge_in, fine_edge_out, fine_node_in, fine_node_out)
    scratch = [pltpu.VMEM((EDGES, 512), BF16), pltpu.VMEM((4, 512, LATENT), BF16)]

    outgoing = call(outgoing_kernel, shape(RIM, LATENT), [VMEM] * 2, (nodes, rows), "outgoing", cost(10**9, 10**6))
    halo = exchange(outgoing)
    pre = fine_local(nodes, edges)
    cells, edges_one, own, to_left, to_right = call(
        fine_pool_kernel,
        [shape(CELLS, LATENT), shape(EDGES, LATENT), shape(CLUS, LATENT, dtype=F32)] + [shape(CLUS, LATENT)] * 2,
        [SMEM] + [VMEM] * 15,
        (flags, pre, edges, nodes, senders, receivers, *halo, *weights, labels),
        "fine_pool", cost(4_000_000_000, 2_000_000), scratch + [pltpu.VMEM((CELLS, 384), BF16)],
    )
    from_left, from_right = exchange_row(to_left, to_right)
    pooled = ((own + from_left + from_right) / FAN).astype(BF16)
    halo = exchange(pooled)
    pre = call(
        coarse_local_kernel, shape(CEDGES, LATENT, dtype=F32), [VMEM] * 4,
        (pooled, csenders, creceivers, coarse_edge_in), "coarse_local", cost(10**9, 10**6),
    )
    coarse = call(
        coarse_kernel, shape(CLUS, LATENT), [SMEM] + [VMEM] * 13,
        (flags, pre, pooled, csenders, creceivers, *halo,
         coarse_edge_in, coarse_edge_out, coarse_node_in, coarse_node_out),
        "coarse", cost(2 * 10**9, 10**6), [pltpu.VMEM((CEDGES, LATENT), BF16)],
    )
    left, right = exchange_row(coarse, coarse)
    cells_two, outgoing = call(
        prolong_kernel, [shape(CELLS, LATENT), shape(RIM, LATENT)], [SMEM] + [VMEM] * 8,
        (flags, cells, labels, coarse, left, right, rows, prolong_in, prolong_out),
        "prolong", cost(2 * 10**9, 10**6),
    )
    halo = exchange(outgoing)
    pre = fine_local(cells_two, edges_one)
    node_out, edge_out = call(
        fine_last_kernel, [shape(CELLS, LATENT), shape(EDGES, LATENT)], [SMEM] + [VMEM] * 14,
        (flags, pre, edges_one, cells_two, senders, receivers, *halo, *weights),
        "fine_last", cost(4_000_000_000, 2_000_000), scratch,
    )
    return node_out[None, None], edge_out[None, None]


def solution(mesh):
    split = P("px", "py", None)
    cells = P("px", "py", None, None)
    return jax.shard_map(
        on_device,
        mesh=mesh,
        in_specs=(cells, cells) + (split,) * 6 + (P(),) * 10,
        out_specs=(cells, cells),
        check_vma=False,
    )
```

time: 171 us -> 74 us (0.43)
  the two profiles are of different devices: /device:TPU:223 before, /device:TPU:196 now
where the time goes in v1:
time: 74 us; the launch traced here: 73.7 us
  Pallas kernels  30.2 us (41%)
  starting transfers between devices  27.2 us (37%)
  waiting for transfers between devices  13.3 us (18%)
  local copies, waits for them, and re-layouts  1.89 us (3%)
  between operations  1.01 us (1%)
    pallas_call x8, Pallas kernels, call(): pl.pallas_call(kernel, out_shape=outs, in_specs=ins, out_specs=jax.tree.m...  30.2 us
    ppermute x3, starting transfers between devices, exchange(): first = lax.ppermute(block, ('px', 'py'), ring)  15.8 us
    ppermute x5, waiting for transfers between devices, exchange_row(): lax.ppermute(to_right, 'py', [(i, (i + 1) % count) for i in range(count)])  11.9 us
    ppermute x5, starting transfers between devices, exchange_row(): lax.ppermute(to_left, 'py', [((i + 1) % count, i) for i in range(count)])  7.66 us
    ppermute x3, starting transfers between devices, exchange(): cross = lax.ppermute(block, 'px', crossing)  2.13 us
    unnamed x38, local copies, waits for them, and re-layouts  1.8 us
  transfers between devices with their start and end apart: 19, of which 6 were waited for; matrix products, arithmetic and copies ran while one was open for 0% of the time, Pallas kernels for 9%

profile of v1, /device:TPU:196, one launch (start us, length us, event | category | flops | bytes accessed | tf_op | source)
XLA Modules:
  0.0 73.7 jit_solution(3121837965603217064)
XLA Ops:
  0.6 0.7 copy-done.18
  1.3 1.0 %copy-done = bf16[1,1,2048,128]{3,2,1,0:T(8,128)(2,1)S(1)} copy-done((bf16[1,1,2048,128]{3,2,1,0:T(8,128)(2,1)S(1)}, bf16[1,1,2048,128]{3,2,1,0:T(8,128)(2,1)}, u32[]{:S(2)}) %copy-start) | copy-done | bytes 524312
  2.4 0.3 outgoing.1
  2.7 0.0 copy-start.16
  2.7 0.7 collective-permute-start.4
  3.4 0.5 collective-permute-start.3
  3.9 5.4 %collective-permute-start.2 = (bf16[256,128]{1,0:T(8,128)(2,1)S(1)}, bf16[256,128]{1,0:T(8,128)(2,1)S(1)}, u32[]{:S(2)}, u32[]{:S(2)}) collective-permute-start(bf16[256,128]{1,0:T(8,128)(2,1)S(1)} %outgoing.1), channel_id=1, source_target_pairs={{0,16},{1,0},{2,18},{3,2},{4,20},{5,4},{6,22},{7,6},{8,24},{9,8},{... | collective-permute-start | bytes 196616 | tf_op jit(solution)/shard_map/ppermute | solution.py:291
  9.4 2.3 %collective-permute-start.1 = (bf16[256,128]{1,0:T(8,128)(2,1)S(1)}, bf16[256,128]{1,0:T(8,128)(2,1)S(1)}, u32[]{:S(2)}, u32[]{:S(2)}) collective-permute-start(bf16[256,128]{1,0:T(8,128)(2,1)S(1)} %outgoing.1), channel_id=1, source_target_pairs={{1,0},{2,1},{3,2},{4,3},{5,4},{6,5},{7,6},{8,7},{9,8},{10,9},{11,1... | collective-permute-start | bytes 196616 | tf_op jit(solution)/shard_map/ppermute | solution.py:300
  11.7 0.0 collective-permute-start
  11.7 0.0 copy-done.2
  11.7 0.0 copy-start.1
  11.7 0.0 copy-start.12
  11.8 0.0 copy-start.13
  11.8 2.5 %fine_local.2.pre = f32[1024,128]{1,0:T(8,128)S(1)} custom-call(bf16[2048,128]{1,0:T(8,128)(2,1)S(1)} %bitcast.16, bf16[1024,128]{1,0:T(8,128)(2,1)S(1)} %bitcast.18, s32[8,128]{1,0:T(8,128)S(1)} %bitcast.26, s32[8,128]{1,0:T(8,128)S(1)} %bitcast.30, bf16[384,128]{1,0:T(8,128)(2,1)S(1)} %copy-done.3), custom_call_target="tpu_custom_call" | custom-call | flops 4000000000 | bytes 2000000 | tf_op jit(solution)/shard_map/fine_local/pallas_call | solution.py:260
  14.3 0.0 copy-start.7
  14.3 0.0 copy-start.11
  14.3 0.1 stack.31.flags
  14.4 0.0 collective-permute-done.4.cross
  14.4 0.0 collective-permute-done.3.second
  14.4 0.0 collective-permute-done.2.first
  14.4 0.0 collective-permute-done.1.right
  14.5 2.1 %collective-permute-done.left = bf16[256,128]{1,0:T(8,128)(2,1)S(1)} collective-permute-done((bf16[256,128]{1,0:T(8,128)(2,1)S(1)}, bf16[256,128]{1,0:T(8,128)(2,1)S(1)}, u32[]{:S(2)}, u32[]{:S(2)}) %collective-permute-start) | collective-permute-done | bytes 65568 | tf_op jit(solution)/shard_map/ppermute | solution.py:299
  16.6 7.5 %fine_pool.1 = (bf16[2048,128]{1,0:T(8,128)(2,1)S(1)}, bf16[1024,128]{1,0:T(8,128)(2,1)S(1)}, f32[256,128]{1,0:T(8,128)S(1)}, bf16[256,128]{1,0:T(8,128)(2,1)S(1)}, bf16[256,128]{1,0:T(8,128)(2,1)S(1)}) custom-call(s32[5]{0:T(128)S(1)} %stack.31.flags, f32[1024,128]{1,0:T(8,128)S(1)} %fine_local.2.pre, bf16[1024,128]{1,0:T(8,128)(2,1)S(1)} %bitcast.19, ...), custom_call_target="tpu_custom_call" | custom-call | flops 4000000000 | bytes 2000000 | tf_op jit(solution)/shard_map/fine_pool/pallas_call | solution.py:260
  24.2 0.0 collective-permute-start.5
  24.2 2.9 %collective-permute-start.6 = (bf16[256,128]{1,0:T(8,128)(2,1)S(1)}, bf16[256,128]{1,0:T(8,128)(2,1)S(1)}, u32[]{:S(2)}, u32[]{:S(2)}) collective-permute-start(bf16[256,128]{1,0:T(8,128)(2,1)S(1)} %get-tuple-element.14), channel_id=1, source_target_pairs={{1,0},{2,1},{3,2},{4,3},{5,4},{6,5},{7,6},{8,7},{9,8},{10,9},{11,1... | collective-permute-start | bytes 196616 | tf_op jit(solution)/shard_map/ppermute | solution.py:300
  27.1 1.9 %collective-permute-done.5 = bf16[256,128]{1,0:T(8,128)(2,1)S(1)} collective-permute-done((bf16[256,128]{1,0:T(8,128)(2,1)S(1)}, bf16[256,128]{1,0:T(8,128)(2,1)S(1)}, u32[]{:S(2)}, u32[]{:S(2)}) %collective-permute-start.5) | collective-permute-done | bytes 65568 | tf_op jit(solution)/shard_map/ppermute | solution.py:299
  29.1 0.0 collective-permute-done.6
  29.1 0.8 %collective-permute-start.11 = (bf16[256,128]{1,0:T(8,128)(2,1)S(1)}, bf16[256,128]{1,0:T(8,128)(2,1)S(1)}, u32[]{:S(2)}, u32[]{:S(2)}) collective-permute-start(bf16[256,128]{1,0:T(8,128)(2,1)S(1)} %multiply_convert_fusion.pooled), channel_id=1, source_target_pairs={{48,64},{64,48},{112,128},{128,112},{176,192},{192,176},{240,256},... | collective-permute-start | bytes 196616 | tf_op jit(solution)/shard_map/ppermute | solution.py:293
  29.9 0.0 collective-permute-start.10
  30.0 4.4 %collective-permute-start.9 = (bf16[256,128]{1,0:T(8,128)(2,1)S(1)}, bf16[256,128]{1,0:T(8,128)(2,1)S(1)}, u32[]{:S(2)}, u32[]{:S(2)}) collective-permute-start(bf16[256,128]{1,0:T(8,128)(2,1)S(1)} %multiply_convert_fusion.pooled), channel_id=1, source_target_pairs={{0,16},{1,0},{2,18},{3,2},{4,20},{5,4},{6,22},{7,6},{8,24},{9,8},{... | collective-permute-start | bytes 196616 | tf_op jit(solution)/shard_map/ppermute | solution.py:291
  34.4 2.4 %collective-permute-start.8 = (bf16[256,128]{1,0:T(8,128)(2,1)S(1)}, bf16[256,128]{1,0:T(8,128)(2,1)S(1)}, u32[]{:S(2)}, u32[]{:S(2)}) collective-permute-start(bf16[256,128]{1,0:T(8,128)(2,1)S(1)} %multiply_convert_fusion.pooled), channel_id=1, source_target_pairs={{1,0},{2,1},{3,2},{4,3},{5,4},{6,5},{7,6},{8,7},{9,8},{10,9},{11,1... | collective-permute-start | bytes 196616 | tf_op jit(solution)/shard_map/ppermute | solution.py:300
  36.7 0.0 collective-permute-start.7
  36.7 0.0 copy-done.14
  36.7 0.0 copy-done.15
  36.7 0.0 copy-start.5
  36.7 0.0 copy-start.8
  36.8 0.0 copy-start.9
  36.8 1.8 %coarse_local.1.pre = f32[1024,128]{1,0:T(8,128)S(1)} custom-call(bf16[256,128]{1,0:T(8,128)(2,1)S(1)} %multiply_convert_fusion.pooled, s32[8,128]{1,0:T(8,128)S(1)} %bitcast.22, s32[8,128]{1,0:T(8,128)S(1)} %bitcast.24, bf16[256,128]{1,0:T(8,128)(2,1)S(1)} %copy-done.4), custom_call_target="tpu_custom_call" | custom-call | flops 1000000000 | bytes 1000000 | tf_op jit(solution)/shard_map/coarse_local/pallas_call | solution.py:260
  38.6 0.0 copy-start.6
  38.6 0.0 copy-start.10
  38.6 0.0 collective-permute-done.11.cross
  38.6 0.0 collective-permute-done.10.second
  38.6 0.0 collective-permute-done.9.first
  38.7 0.0 collective-permute-done.8.right
  38.7 2.9 %collective-permute-done.7.left = bf16[256,128]{1,0:T(8,128)(2,1)S(1)} collective-permute-done((bf16[256,128]{1,0:T(8,128)(2,1)S(1)}, bf16[256,128]{1,0:T(8,128)(2,1)S(1)}, u32[]{:S(2)}, u32[]{:S(2)}) %collective-permute-start.7) | collective-permute-done | bytes 65568 | tf_op jit(solution)/shard_map/ppermute | solution.py:299
  41.6 4.1 %coarse.1.own = bf16[256,128]{1,0:T(8,128)(2,1)S(1)} custom-call(s32[5]{0:T(128)S(1)} %stack.31.flags, f32[1024,128]{1,0:T(8,128)S(1)} %coarse_local.1.pre, bf16[256,128]{1,0:T(8,128)(2,1)S(1)} %multiply_convert_fusion.pooled, s32[8,128]{1,0:T(8,128)S(1)} %bitcast.23, s32[8,128]{1,0:T(8,128)S(1)} %bitcast.25, ...), custom_call_target="tpu_custom_call" | custom-call | flops 2000000000 | bytes 1000000 | tf_op jit(solution)/shard_map/coarse/pallas_call | solution.py:260
  45.7 0.0 collective-permute-start.13
  45.7 0.5 collective-permute-start.12
  46.2 1.4 %collective-permute-done.13.right = bf16[256,128]{1,0:T(8,128)(2,1)S(1)} collective-permute-done((bf16[256,128]{1,0:T(8,128)(2,1)S(1)}, bf16[256,128]{1,0:T(8,128)(2,1)S(1)}, u32[]{:S(2)}, u32[]{:S(2)}) %collective-permute-start.13) | collective-permute-done | bytes 65568 | tf_op jit(solution)/shard_map/ppermute | solution.py:300
  47.6 3.0 %collective-permute-done.12.left = bf16[256,128]{1,0:T(8,128)(2,1)S(1)} collective-permute-done((bf16[256,128]{1,0:T(8,128)(2,1)S(1)}, bf16[256,128]{1,0:T(8,128)(2,1)S(1)}, u32[]{:S(2)}, u32[]{:S(2)}) %collective-permute-start.12) | collective-permute-done | bytes 65568 | tf_op jit(solution)/shard_map/ppermute | solution.py:299
  50.6 0.0 copy-done.10
  50.6 4.1 %prolong.1 = (bf16[2048,128]{1,0:T(8,128)(2,1)S(1)}, bf16[256,128]{1,0:T(8,128)(2,1)S(1)}) custom-call(s32[5]{0:T(128)S(1)} %stack.31.flags, bf16[2048,128]{1,0:T(8,128)(2,1)S(1)} %get-tuple-element.11.cells, s32[16,128]{1,0:T(8,128)S(1)} %bitcast.21, bf16[256,128]{1,0:T(8,128)(2,1)S(1)} %coarse.1.own, bf16[256,128]{1,0:T(8,128)(2,1)S(1)} %collective-permute-done.12.left, ...), custom_call_target="tpu_custom_call" | custom-call | flops 2000000000 | bytes 1000000 | tf_op jit(solution)/shard_map/prolong/pallas_call | solution.py:260
  54.7 0.7 collective-permute-start.18
  55.4 0.0 collective-permute-start.17
  55.4 6.0 %collective-permute-start.16 = (bf16[256,128]{1,0:T(8,128)(2,1)S(1)}, bf16[256,128]{1,0:T(8,128)(2,1)S(1)}, u32[]{:S(2)}, u32[]{:S(2)}) collective-permute-start(bf16[256,128]{1,0:T(8,128)(2,1)S(1)} %get-tuple-element.17), channel_id=1, source_target_pairs={{0,16},{1,0},{2,18},{3,2},{4,20},{5,4},{6,22},{7,6},{8,24},{9,8},{... | collective-permute-start | bytes 196616 | tf_op jit(solution)/shard_map/ppermute | solution.py:291
  61.4 0.0 collective-permute-start.15
  61.4 0.5 collective-permute-start.14
  61.9 2.5 %fine_local.3.pre = f32[1024,128]{1,0:T(8,128)S(1)} custom-call(bf16[2048,128]{1,0:T(8,128)(2,1)S(1)} %get-tuple-element.15.nodes, bf16[1024,128]{1,0:T(8,128)(2,1)S(1)} %get-tuple-element.16.edges, s32[8,128]{1,0:T(8,128)S(1)} %bitcast.28, s32[8,128]{1,0:T(8,128)S(1)} %bitcast.32, bf16[384,128]{1,0:T(8,128)(2,1)S(1)} %copy-done.3), custom_call_target="tpu_custom_call" | custom-call | flops 4000000000 | bytes 2000000 | tf_op jit(solution)/shard_map/fine_local/pallas_call | solution.py:260
  64.5 0.0 collective-permute-done.18.cross
  64.5 0.0 collective-permute-done.17.second
  64.5 0.0 collective-permute-done.16.first
  64.5 0.0 collective-permute-done.15.right
  64.5 1.8 %collective-permute-done.14.left = bf16[256,128]{1,0:T(8,128)(2,1)S(1)} collective-permute-done((bf16[256,128]{1,0:T(8,128)(2,1)S(1)}, bf16[256,128]{1,0:T(8,128)(2,1)S(1)}, u32[]{:S(2)}, u32[]{:S(2)}) %collective-permute-start.14) | collective-permute-done | bytes 65568 | tf_op jit(solution)/shard_map/ppermute | solution.py:299
  66.3 7.4 %fine_last.1 = (bf16[2048,128]{1,0:T(8,128)(2,1)}, bf16[1024,128]{1,0:T(8,128)(2,1)}) custom-call(s32[5]{0:T(128)S(1)} %stack.31.flags, f32[1024,128]{1,0:T(8,128)S(1)} %fine_local.3.pre, bf16[1024,128]{1,0:T(8,128)(2,1)S(1)} %get-tuple-element.16.edges, bf16[2048,128]{1,0:T(8,128)(2,1)S(1)} %get-tuple-element.15.nodes, s32[8,128]{1,0:T(8,128)S(1)} %bitcast.29, ...), custom_call_target="tpu_custom_call" | custom-call | flops 4000000000 | bytes 2000000 | tf_op jit(solution)/shard_map/fine_last/pallas_call | solution.py:260
  (22 shorter events, 0.1 us)
Async XLA Ops:
  0.6 0.7 copy-start.18
  1.3 1.0 %copy-start = (bf16[1,1,2048,128]{3,2,1,0:T(8,128)(2,1)S(1)}, bf16[1,1,2048,128]{3,2,1,0:T(8,128)(2,1)}, u32[]{:S(2)}) copy-start(bf16[1,1,2048,128]{3,2,1,0:T(8,128)(2,1)} %param.18) | copy-start | bytes 1572868
  2.4 9.4 %copy-start.2 = (bf16[1,1,1024,128]{3,2,1,0:T(8,128)(2,1)S(1)}, bf16[1,1,1024,128]{3,2,1,0:T(8,128)(2,1)}, u32[]{:S(2)}) copy-start(bf16[1,1,1024,128]{3,2,1,0:T(8,128)(2,1)} %param.19) | copy-start | bytes 786436
  2.4 9.4 %copy-start.3 = (bf16[384,128]{1,0:T(8,128)(2,1)S(1)}, bf16[384,128]{1,0:T(8,128)(2,1)}, u32[]{:S(2)}) copy-start(bf16[384,128]{1,0:T(8,128)(2,1)} %edge_in.5) | copy-start | bytes 294916
  2.4 9.4 %copy-start.17 = (s32[1,1,1024]{2,1,0:T(1,128)S(1)}, s32[1,1,1024]{2,1,0:T(1,128)}, u32[]{:S(2)}) copy-start(s32[1,1,1024]{2,1,0:T(1,128)} %param.21) | copy-start | bytes 12292
  2.7 9.0 %copy-start.16 = (s32[1,1,1024]{2,1,0:T(1,128)S(1)}, s32[1,1,1024]{2,1,0:T(1,128)}, u32[]{:S(2)}) copy-start(s32[1,1,1024]{2,1,0:T(1,128)} %param.20) | copy-start | bytes 12292
  2.7 11.7 %collective-permute-start.4 = (bf16[256,128]{1,0:T(8,128)(2,1)S(1)}, bf16[256,128]{1,0:T(8,128)(2,1)S(1)}, u32[]{:S(2)}, u32[]{:S(2)}) collective-permute-start(bf16[256,128]{1,0:T(8,128)(2,1)S(1)} %outgoing.1), channel_id=1, source_target_pairs={{48,64},{64,48},{112,128},{128,112},{176,192},{192,176},{240,256},... | collective-permute-start | bytes 196616 | tf_op jit(solution)/shard_map/ppermute | solution.py:293
  3.4 11.0 %collective-permute-start.3 = (bf16[256,128]{1,0:T(8,128)(2,1)S(1)}, bf16[256,128]{1,0:T(8,128)(2,1)S(1)}, u32[]{:S(2)}, u32[]{:S(2)}) collective-permute-start(bf16[256,128]{1,0:T(8,128)(2,1)S(1)} %outgoing.1), channel_id=1, source_target_pairs={{16,0},{0,1},{18,2},{2,3},{20,4},{4,5},{22,6},{6,7},{24,8},{8,9},{... | collective-permute-start | bytes 196616 | tf_op jit(solution)/shard_map/ppermute | solution.py:292
  3.9 10.5 %collective-permute-start.2 = (bf16[256,128]{1,0:T(8,128)(2,1)S(1)}, bf16[256,128]{1,0:T(8,128)(2,1)S(1)}, u32[]{:S(2)}, u32[]{:S(2)}) collective-permute-start(bf16[256,128]{1,0:T(8,128)(2,1)S(1)} %outgoing.1), channel_id=1, source_target_pairs={{0,16},{1,0},{2,18},{3,2},{4,20},{5,4},{6,22},{7,6},{8,24},{9,8},{... | collective-permute-start | bytes 196616 | tf_op jit(solution)/shard_map/ppermute | solution.py:291
  9.4 5.1 %collective-permute-start.1 = (bf16[256,128]{1,0:T(8,128)(2,1)S(1)}, bf16[256,128]{1,0:T(8,128)(2,1)S(1)}, u32[]{:S(2)}, u32[]{:S(2)}) collective-permute-start(bf16[256,128]{1,0:T(8,128)(2,1)S(1)} %outgoing.1), channel_id=1, source_target_pairs={{1,0},{2,1},{3,2},{4,3},{5,4},{6,5},{7,6},{8,7},{9,8},{10,9},{11,1... | collective-permute-start | bytes 196616 | tf_op jit(solution)/shard_map/ppermute | solution.py:300
  11.7 4.9 %collective-permute-start = (bf16[256,128]{1,0:T(8,128)(2,1)S(1)}, bf16[256,128]{1,0:T(8,128)(2,1)S(1)}, u32[]{:S(2)}, u32[]{:S(2)}) collective-permute-start(bf16[256,128]{1,0:T(8,128)(2,1)S(1)} %outgoing.1), channel_id=1, source_target_pairs={{0,1},{1,2},{2,3},{3,4},{4,5},{5,6},{6,7},{7,8},{8,9},{9,10},{10,1... | collective-permute-start | bytes 196616 | tf_op jit(solution)/shard_map/ppermute | solution.py:299
  11.7 4.9 %copy-start.1 = (bf16[1,1,2048,128]{3,2,1,0:T(8,128)(2,1)S(1)}, bf16[1,1,2048,128]{3,2,1,0:T(8,128)(2,1)}, u32[]{:S(2)}) copy-start(bf16[1,1,2048,128]{3,2,1,0:T(8,128)(2,1)} %param.18) | copy-start | bytes 1572868
  11.7 4.9 %copy-start.12 = (bf16[128,128]{1,0:T(8,128)(2,1)S(1)}, bf16[128,128]{1,0:T(8,128)(2,1)}, u32[]{:S(2)}) copy-start(bf16[128,128]{1,0:T(8,128)(2,1)} %node_out.5) | copy-start | bytes 98308
  11.8 4.9 %copy-start.13 = (s32[1,1,2048]{2,1,0:T(1,128)S(1)}, s32[1,1,2048]{2,1,0:T(1,128)}, u32[]{:S(2)}) copy-start(s32[1,1,2048]{2,1,0:T(1,128)} %param.23) | copy-start | bytes 24580
  14.3 2.3 %copy-start.7 = (bf16[256,128]{1,0:T(8,128)(2,1)S(1)}, bf16[256,128]{1,0:T(8,128)(2,1)}, u32[]{:S(2)}) copy-start(bf16[256,128]{1,0:T(8,128)(2,1)} %node_in.5) | copy-start | bytes 196612
  14.3 2.3 %copy-start.11 = (bf16[128,128]{1,0:T(8,128)(2,1)S(1)}, bf16[128,128]{1,0:T(8,128)(2,1)}, u32[]{:S(2)}) copy-start(bf16[128,128]{1,0:T(8,128)(2,1)} %edge_out.5) | copy-start | bytes 98308
  24.2 4.9 %collective-permute-start.5 = (bf16[256,128]{1,0:T(8,128)(2,1)S(1)}, bf16[256,128]{1,0:T(8,128)(2,1)S(1)}, u32[]{:S(2)}, u32[]{:S(2)}) collective-permute-start(bf16[256,128]{1,0:T(8,128)(2,1)S(1)} %get-tuple-element.13), channel_id=1, source_target_pairs={{0,1},{1,2},{2,3},{3,4},{4,5},{5,6},{6,7},{7,8},{8,9},{9,10},{10,1... | collective-permute-start | bytes 196616 | tf_op jit(solution)/shard_map/ppermute | solution.py:299
  24.2 4.9 %collective-permute-start.6 = (bf16[256,128]{1,0:T(8,128)(2,1)S(1)}, bf16[256,128]{1,0:T(8,128)(2,1)S(1)}, u32[]{:S(2)}, u32[]{:S(2)}) collective-permute-start(bf16[256,128]{1,0:T(8,128)(2,1)S(1)} %get-tuple-element.14), channel_id=1, source_target_pairs={{1,0},{2,1},{3,2},{4,3},{5,4},{6,5},{7,6},{8,7},{9,8},{10,9},{11,1... | collective-permute-start | bytes 196616 | tf_op jit(solution)/shard_map/ppermute | solution.py:300
  29.1 7.6 %copy-start.4 = (bf16[256,128]{1,0:T(8,128)(2,1)S(1)}, bf16[256,128]{1,0:T(8,128)(2,1)}, u32[]{:S(2)}) copy-start(bf16[256,128]{1,0:T(8,128)(2,1)} %edge_in.4) | copy-start | bytes 196612
  29.1 7.6 %copy-start.14 = (s32[1,1,1024]{2,1,0:T(1,128)S(1)}, s32[1,1,1024]{2,1,0:T(1,128)}, u32[]{:S(2)}) copy-start(s32[1,1,1024]{2,1,0:T(1,128)} %param.24) | copy-start | bytes 12292
  29.1 7.6 %copy-start.15 = (s32[1,1,1024]{2,1,0:T(1,128)S(1)}, s32[1,1,1024]{2,1,0:T(1,128)}, u32[]{:S(2)}) copy-start(s32[1,1,1024]{2,1,0:T(1,128)} %param.25) | copy-start | bytes 12292
  29.1 9.5 %collective-permute-start.11 = (bf16[256,128]{1,0:T(8,128)(2,1)S(1)}, bf16[256,128]{1,0:T(8,128)(2,1)S(1)}, u32[]{:S(2)}, u32[]{:S(2)}) collective-permute-start(bf16[256,128]{1,0:T(8,128)(2,1)S(1)} %multiply_convert_fusion.pooled), channel_id=1, source_target_pairs={{48,64},{64,48},{112,128},{128,112},{176,192},{192,176},{240,256},... | collective-permute-start | bytes 196616 | tf_op jit(solution)/shard_map/ppermute | solution.py:293
  29.9 8.7 %collective-permute-start.10 = (bf16[256,128]{1,0:T(8,128)(2,1)S(1)}, bf16[256,128]{1,0:T(8,128)(2,1)S(1)}, u32[]{:S(2)}, u32[]{:S(2)}) collective-permute-start(bf16[256,128]{1,0:T(8,128)(2,1)S(1)} %multiply_convert_fusion.pooled), channel_id=1, source_target_pairs={{16,0},{0,1},{18,2},{2,3},{20,4},{4,5},{22,6},{6,7},{24,8},{8,9},{... | collective-permute-start | bytes 196616 | tf_op jit(solution)/shard_map/ppermute | solution.py:292
  30.0 8.7 %collective-permute-start.9 = (bf16[256,128]{1,0:T(8,128)(2,1)S(1)}, bf16[256,128]{1,0:T(8,128)(2,1)S(1)}, u32[]{:S(2)}, u32[]{:S(2)}) collective-permute-start(bf16[256,128]{1,0:T(8,128)(2,1)S(1)} %multiply_convert_fusion.pooled), channel_id=1, source_target_pairs={{0,16},{1,0},{2,18},{3,2},{4,20},{5,4},{6,22},{7,6},{8,24},{9,8},{... | collective-permute-start | bytes 196616 | tf_op jit(solution)/shard_map/ppermute | solution.py:291
  34.4 4.3 %collective-permute-start.8 = (bf16[256,128]{1,0:T(8,128)(2,1)S(1)}, bf16[256,128]{1,0:T(8,128)(2,1)S(1)}, u32[]{:S(2)}, u32[]{:S(2)}) collective-permute-start(bf16[256,128]{1,0:T(8,128)(2,1)S(1)} %multiply_convert_fusion.pooled), channel_id=1, source_target_pairs={{1,0},{2,1},{3,2},{4,3},{5,4},{6,5},{7,6},{8,7},{9,8},{10,9},{11,1... | collective-permute-start | bytes 196616 | tf_op jit(solution)/shard_map/ppermute | solution.py:300
  36.7 4.9 %collective-permute-start.7 = (bf16[256,128]{1,0:T(8,128)(2,1)S(1)}, bf16[256,128]{1,0:T(8,128)(2,1)S(1)}, u32[]{:S(2)}, u32[]{:S(2)}) collective-permute-start(bf16[256,128]{1,0:T(8,128)(2,1)S(1)} %multiply_convert_fusion.pooled), channel_id=1, source_target_pairs={{0,1},{1,2},{2,3},{3,4},{4,5},{5,6},{6,7},{7,8},{8,9},{9,10},{10,1... | collective-permute-start | bytes 196616 | tf_op jit(solution)/shard_map/ppermute | solution.py:299
  36.7 4.9 %copy-start.5 = (bf16[256,128]{1,0:T(8,128)(2,1)S(1)}, bf16[256,128]{1,0:T(8,128)(2,1)}, u32[]{:S(2)}) copy-start(bf16[256,128]{1,0:T(8,128)(2,1)} %node_in.4) | copy-start | bytes 196612
  36.7 4.9 %copy-start.8 = (bf16[128,128]{1,0:T(8,128)(2,1)S(1)}, bf16[128,128]{1,0:T(8,128)(2,1)}, u32[]{:S(2)}) copy-start(bf16[128,128]{1,0:T(8,128)(2,1)} %edge_out.4) | copy-start | bytes 98308
  36.8 4.9 %copy-start.9 = (bf16[128,128]{1,0:T(8,128)(2,1)S(1)}, bf16[128,128]{1,0:T(8,128)(2,1)}, u32[]{:S(2)}) copy-start(bf16[128,128]{1,0:T(8,128)(2,1)} %node_out.4) | copy-start | bytes 98308
  38.6 12.0 %copy-start.6 = (bf16[256,128]{1,0:T(8,128)(2,1)S(1)}, bf16[256,128]{1,0:T(8,128)(2,1)}, u32[]{:S(2)}) copy-start(bf16[256,128]{1,0:T(8,128)(2,1)} %first.6) | copy-start | bytes 196612
  38.6 12.0 %copy-start.10 = (bf16[128,128]{1,0:T(8,128)(2,1)S(1)}, bf16[128,128]{1,0:T(8,128)(2,1)}, u32[]{:S(2)}) copy-start(bf16[128,128]{1,0:T(8,128)(2,1)} %second.1) | copy-start | bytes 98308
  45.7 1.9 %collective-permute-start.13 = (bf16[256,128]{1,0:T(8,128)(2,1)S(1)}, bf16[256,128]{1,0:T(8,128)(2,1)S(1)}, u32[]{:S(2)}, u32[]{:S(2)}) collective-permute-start(bf16[256,128]{1,0:T(8,128)(2,1)S(1)} %coarse.1.own), channel_id=1, source_target_pairs={{1,0},{2,1},{3,2},{4,3},{5,4},{6,5},{7,6},{8,7},{9,8},{10,9},{11,1... | collective-permute-start | bytes 196616 | tf_op jit(solution)/shard_map/ppermute | solution.py:300
  45.7 4.9 %collective-permute-start.12 = (bf16[256,128]{1,0:T(8,128)(2,1)S(1)}, bf16[256,128]{1,0:T(8,128)(2,1)S(1)}, u32[]{:S(2)}, u32[]{:S(2)}) collective-permute-start(bf16[256,128]{1,0:T(8,128)(2,1)S(1)} %coarse.1.own), channel_id=1, source_target_pairs={{0,1},{1,2},{2,3},{3,4},{4,5},{5,6},{6,7},{7,8},{8,9},{9,10},{10,1... | collective-permute-start | bytes 196616 | tf_op jit(solution)/shard_map/ppermute | solution.py:299
  54.7 9.8 %collective-permute-start.18 = (bf16[256,128]{1,0:T(8,128)(2,1)S(1)}, bf16[256,128]{1,0:T(8,128)(2,1)S(1)}, u32[]{:S(2)}, u32[]{:S(2)}) collective-permute-start(bf16[256,128]{1,0:T(8,128)(2,1)S(1)} %get-tuple-element.17), channel_id=1, source_target_pairs={{48,64},{64,48},{112,128},{128,112},{176,192},{192,176},{240,256},... | collective-permute-start | bytes 196616 | tf_op jit(solution)/shard_map/ppermute | solution.py:293
  55.4 9.1 %collective-permute-start.17 = (bf16[256,128]{1,0:T(8,128)(2,1)S(1)}, bf16[256,128]{1,0:T(8,128)(2,1)S(1)}, u32[]{:S(2)}, u32[]{:S(2)}) collective-permute-start(bf16[256,128]{1,0:T(8,128)(2,1)S(1)} %get-tuple-element.17), channel_id=1, source_target_pairs={{16,0},{0,1},{18,2},{2,3},{20,4},{4,5},{22,6},{6,7},{24,8},{8,9},{... | collective-permute-start | bytes 196616 | tf_op jit(solution)/shard_map/ppermute | solution.py:292
  55.4 9.1 %collective-permute-start.16 = (bf16[256,128]{1,0:T(8,128)(2,1)S(1)}, bf16[256,128]{1,0:T(8,128)(2,1)S(1)}, u32[]{:S(2)}, u32[]{:S(2)}) collective-permute-start(bf16[256,128]{1,0:T(8,128)(2,1)S(1)} %get-tuple-element.17), channel_id=1, source_target_pairs={{0,16},{1,0},{2,18},{3,2},{4,20},{5,4},{6,22},{7,6},{8,24},{9,8},{... | collective-permute-start | bytes 196616 | tf_op jit(solution)/shard_map/ppermute | solution.py:291
  61.4 3.1 %collective-permute-start.15 = (bf16[256,128]{1,0:T(8,128)(2,1)S(1)}, bf16[256,128]{1,0:T(8,128)(2,1)S(1)}, u32[]{:S(2)}, u32[]{:S(2)}) collective-permute-start(bf16[256,128]{1,0:T(8,128)(2,1)S(1)} %get-tuple-element.17), channel_id=1, source_target_pairs={{1,0},{2,1},{3,2},{4,3},{5,4},{6,5},{7,6},{8,7},{9,8},{10,9},{11,1... | collective-permute-start | bytes 196616 | tf_op jit(solution)/shard_map/ppermute | solution.py:300
  61.4 4.9 %collective-permute-start.14 = (bf16[256,128]{1,0:T(8,128)(2,1)S(1)}, bf16[256,128]{1,0:T(8,128)(2,1)S(1)}, u32[]{:S(2)}, u32[]{:S(2)}) collective-permute-start(bf16[256,128]{1,0:T(8,128)(2,1)S(1)} %get-tuple-element.17), channel_id=1, source_target_pairs={{0,1},{1,2},{2,3},{3,4},{4,5},{5,6},{6,7},{7,8},{8,9},{9,10},{10,1... | collective-permute-start | bytes 196616 | tf_op jit(solution)/shard_map/ppermute | solution.py:299

commit v2 on v1

v2 whole, which is shorter than its diff:
```python
import functools

import jax
import jax.numpy as jnp
from jax import lax
from jax.experimental import pallas as pl
from jax.experimental.pallas import tpu as pltpu
from jax.sharding import PartitionSpec as P

LATENT = 128
CELLS = 2048
EDGES = 1024
RIM = 256
CLUS = 256
CEDGES = 1024
FAN = 8
ROWS = 4
CELL_PARTS = 2
BF16 = jnp.bfloat16
F32 = jnp.float32
VMEM = pl.BlockSpec(memory_space=pltpu.VMEM)
ANY = pl.BlockSpec(memory_space=pl.ANY)
SMEM = pl.BlockSpec(memory_space=pltpu.SMEM)
PARAMS = pltpu.CompilerParams(vmem_limit_bytes=24 * 1024 * 1024)


def cost(flops, moved):
    return pl.CostEstimate(flops=flops, bytes_accessed=moved, transcendentals=0)


def dot(a, b):
    return jnp.dot(a, b, preferred_element_type=F32)


def column(ref, start, count):
    parts = []
    for k in range(count):
        row = ref[pl.ds(start + k, 1), :]
        parts.append(jnp.transpose(jnp.broadcast_to(row, (128, 128))))
    return jnp.concatenate(parts, axis=0)


def pick_rows(code, depth, low):
    code = code.astype(F32).astype(BF16)
    blocks = []
    for b in range(depth // 128):
        lane = lax.broadcasted_iota(jnp.int32, code.shape, 1) + (low + 128 * b)
        hit = code == lane.astype(F32).astype(BF16)
        blocks.append(jnp.where(hit, jnp.ones_like(code), jnp.zeros_like(code)))
    return jnp.concatenate(blocks, axis=1)


def pick_columns(ref, code_of, depth, low, count):
    row = lax.broadcasted_iota(jnp.int32, (depth, 128), 0) + low
    row = row.astype(F32).astype(BF16)
    blocks = []
    for c in range(count):
        code = code_of(ref[pl.ds(c, 1), :]).astype(F32).astype(BF16)
        hit = jnp.broadcast_to(code, (depth, 128)) == row
        blocks.append(jnp.where(hit, jnp.ones_like(row), jnp.zeros_like(row)))
    return jnp.concatenate(blocks, axis=1)


def side_by_side(table, folds):
    depth = table.shape[0] // folds
    return jnp.concatenate([table[f * depth : (f + 1) * depth] for f in range(folds)], axis=1)


def choose(wide, which, folds):
    out = wide[:, :LATENT]
    for f in range(1, folds):
        out = jnp.where(which == f, wide[:, f * LATENT : (f + 1) * LATENT], out)
    return out


def centred_layer(second):
    exact = second.astype(F32)
    exact = exact - jnp.mean(exact, axis=-1, keepdims=True)
    high = exact.astype(BF16)
    low = (exact - high.astype(F32)).astype(BF16)
    return jnp.concatenate([high, low], axis=0)


def finish(pre, second):
    hidden = jnp.maximum(pre, 0.0).astype(BF16)
    centred = dot(jnp.concatenate([hidden, hidden], axis=1), second)
    spread = jnp.mean(centred * centred, axis=-1, keepdims=True)
    return centred * lax.rsqrt(spread + 1e-05)


def from_cells(table, index):
    code = jnp.where(index < CELLS, (index & 511) - 256, 512)
    wide = dot(pick_rows(code, 512, -256), table)
    return choose(wide, index >> 9, 4).astype(BF16)


def from_halo(table, index):
    code = jnp.where(index >= 0, index & 255, 512)
    wide = dot(pick_rows(code, 256, 0), table)
    return choose(wide, index >> 8, 4).astype(BF16)


def halo_table(flags, first, second, right, left, cross):
    a, b, c = first[...], second[...], cross[...]
    zero = jnp.zeros_like(a)
    up = jnp.where(flags[0] == 0, a, jnp.where(flags[0] == 1, b, jnp.where(flags[0] == 2, c, zero)))
    down = jnp.where(flags[1] == 0, a, jnp.where(flags[1] == 1, b, jnp.where(flags[1] == 2, c, zero)))
    west = jnp.where(flags[2] == 0, zero, left[...])
    east = jnp.where(flags[3] == 0, zero, right[...])
    return jnp.concatenate([up, down, west, east], axis=1)


def outgoing_kernel(nodes, rows, out):
    table = side_by_side(nodes[...], 4)
    out[...] = from_cells(table, column(rows, 0, 2) - 1)


def fine_local_kernel(nodes, edges, senders, receivers, first, out):
    table = side_by_side(nodes[...], 4)

    near = from_cells(table, jnp.concatenate([column(senders, 0, 8), column(receivers, 0, 8)], axis=0))
    out[...] = dot(jnp.concatenate([edges[...], near[:EDGES], near[EDGES:]], axis=1), first[...])


def edge_part(flags, pre, edges, senders, receivers, halo, edge_in, edge_out, new_edges, wide, sums):
    far = from_halo(halo_table(flags, *halo), column(senders, 0, 8) - CELLS)
    message = finish(pre[...] + dot(far, edge_in[LATENT : 2 * LATENT, :]), centred_layer(edge_out[...]))
    new_edges[...] = (edges[...].astype(F32) + message).astype(BF16)
    quarter = column(receivers, 0, 8) >> 9
    wide[...] = jnp.concatenate([jnp.where(quarter == f, message, 0.0) for f in range(4)], axis=1).astype(BF16)
    spread = pick_columns(receivers, lambda r: (r & 511) - 256, 512, -256, 8)
    total = dot(spread, wide[...]).astype(BF16)
    for f in range(4):
        sums[pl.ds(512 * f, 512), :] = total[:, f * LATENT : (f + 1) * LATENT]


def cell_part(at, nodes, sums, node_in, second):
    cells = nodes[at, :]
    inputs = jnp.concatenate([cells, sums[at, :]], axis=1)
    return (cells.astype(F32) + finish(dot(inputs, node_in[...]), second)).astype(BF16)


def fine_pool_kernel(
    flags, pre, edges, nodes, senders, receivers, first, second, right, left, cross,
    edge_in, edge_out, node_in, node_out, labels,
    new_nodes, new_edges, own, to_left, to_right, wide, sums, masked,
):
    halo = (first, second, right, left, cross)
    edge_part(flags, pre, edges, senders, receivers, halo, edge_in, edge_out, new_edges, wide, sums)
    layer = centred_layer(node_out[...])
    cells = cell_part(pl.ds(0, CELLS), nodes, sums, node_in, layer)
    new_nodes[...] = cells
    block = (column(labels, 0, 16) - flags[4]) >> 8
    masked[...] = jnp.concatenate(
        [jnp.where(block == b, cells.astype(F32), 0.0) for b in range(3)], axis=1
    ).astype(BF16)
    total = dot(pick_columns(labels, lambda r: r & 255, 256, 0, 16), masked[...])
    to_left[...] = total[:, :LATENT].astype(BF16)
    own[...] = total[:, LATENT : 2 * LATENT]
    to_right[...] = total[:, 2 * LATENT :].astype(BF16)


def fine_last_kernel(
    flags, pre, edges, nodes, senders, receivers, first, second, right, left, cross,
    edge_in, edge_out, node_in, node_out,
    new_nodes, new_edges, wide, sums, held_nodes, held_edges, sent,
):
    halo = (first, second, right, left, cross)
    edge_part(flags, pre, edges, senders, receivers, halo, edge_in, edge_out, held_edges, wide, sums)
    puts = [pltpu.make_async_copy(held_edges, new_edges, sent.at[0])]
    puts[0].start()
    layer = centred_layer(node_out[...])
    size = CELLS // CELL_PARTS
    for f in range(CELL_PARTS):
        at = pl.ds(f * size, size)
        held_nodes[at, :] = cell_part(at, nodes, sums, node_in, layer)
        puts.append(pltpu.make_async_copy(held_nodes.at[at, :], new_nodes.at[at, :], sent.at[1 + f]))
        puts[-1].start()
    for put in puts:
        put.wait()


def coarse_local_kernel(pooled, senders, receivers, first, out):
    index = jnp.concatenate([column(senders, 0, 8), column(receivers, 0, 8)], axis=0)
    near = dot(pick_rows(jnp.where(index < CLUS, index, 512), 256, 0), pooled[...]).astype(BF16)
    out[...] = dot(jnp.concatenate([near[:CEDGES], near[CEDGES:]], axis=1), first[...])


def coarse_kernel(
    flags, pre, pooled, senders, receivers, first, second, right, left, cross,
    edge_in, edge_out, node_in, node_out, out,
):
    table = halo_table(flags, first, second, right, left, cross)
    far = from_halo(table, column(senders, 0, 8) - CLUS)
    message = finish(pre[...] + dot(far, edge_in[:LATENT, :]), centred_layer(edge_out[...])).astype(BF16)
    gathered = dot(pick_columns(receivers, lambda r: r, 256, 0, 8), message).astype(BF16)
    own = pooled[...]
    inputs = jnp.concatenate([own, gathered], axis=1)
    out[...] = (own.astype(F32) + finish(dot(inputs, node_in[...]), centred_layer(node_out[...]))).astype(BF16)


def prolong_kernel(flags, cells, labels, own, left, right, rows, first, second, new_cells, outgoing):
    table = jnp.concatenate([left[...], own[...], right[...]], axis=1)
    index = column(labels, 0, 16) - flags[4]
    looked = choose(dot(pick_rows(index & 255, 256, 0), table), index >> 8, 3).astype(BF16)
    old = cells[...]
    update = finish(dot(jnp.concatenate([old, looked], axis=1), first[...]), centred_layer(second[...]))
    new = (old.astype(F32) + update).astype(BF16)
    new_cells[...] = new
    outgoing[...] = from_cells(side_by_side(new, 4), column(rows, 0, 2) - 1)


def shape(*dims, dtype=BF16):
    return jax.ShapeDtypeStruct(dims, dtype)


def call(kernel, outs, ins, args, name, estimate, scratch=(), where=None):
    return pl.pallas_call(
        kernel,
        out_shape=outs,
        in_specs=ins,
        out_specs=where or jax.tree.map(lambda _: VMEM, outs),
        scratch_shapes=scratch,
        compiler_params=PARAMS,
        cost_estimate=estimate,
        name=name,
    )(*args)


def snake(count_x, count_y):
    pairs = []
    for i in range(count_x):
        for j in range(count_y):
            if j % 2 == 0:
                to = (i + 1, j) if i % ROWS < ROWS - 1 else (i, j + 1)
            else:
                to = (i - 1, j) if i % ROWS > 0 else (i, j - 1)
            pairs.append((i * count_y + j, to[0] * count_y + to[1]))
    return pairs


def exchange(block):
    count_x, count_y = lax.axis_size("px"), lax.axis_size("py")
    ring = snake(count_x, count_y)
    crossing = []
    for k in range(ROWS - 1, count_x - 1, ROWS):
        crossing += [(k, k + 1), (k + 1, k)]
    left, right = exchange_row(block, block)
    first = lax.ppermute(block, ("px", "py"), ring)
    second = lax.ppermute(block, ("px", "py"), [(b, a) for a, b in ring])
    cross = lax.ppermute(block, "px", crossing)
    return first, second, right, left, cross


def exchange_row(to_left, to_right):
    count = lax.axis_size("py")
    from_left = lax.ppermute(to_right, "py", [(i, (i + 1) % count) for i in range(count)])
    from_right = lax.ppermute(to_left, "py", [((i + 1) % count, i) for i in range(count)])
    return from_left, from_right


def on_device(
    node_latents, edge_latents, edge_senders, edge_receivers, send_rows, clusters, coarse_senders, coarse_receivers,
    fine_edge_in, fine_edge_out, fine_node_in, fine_node_out,
    coarse_edge_in, coarse_edge_out, coarse_node_in, coarse_node_out, prolong_in, prolong_out,
):
    nodes, edges = node_latents[0, 0], edge_latents[0, 0]
    senders, receivers = edge_senders.reshape(8, 128), edge_receivers.reshape(8, 128)
    rows, labels = send_rows.reshape(2, 128) + 1, clusters.reshape(16, 128)
    csenders, creceivers = coarse_senders.reshape(8, 128), coarse_receivers.reshape(8, 128)
    i, j = lax.axis_index("px"), lax.axis_index("py")
    last_i, last_j = lax.axis_size("px") - 1, lax.axis_size("py") - 1
    core, along = j % 2, i % ROWS
    up = jnp.where(along > 0, core, jnp.where(i > 0, 2, 3))
    down = jnp.where(along < ROWS - 1, 1 - core, jnp.where(i < last_i, 2, 3))
    flags = jnp.stack([up, down, j > 0, j < last_j, (j - 1) * CLUS]).astype(jnp.int32)

    def fine_local(nodes, edges):
        return call(
            fine_local_kernel, shape(EDGES, LATENT, dtype=F32), [VMEM] * 5,
            (nodes, edges, senders, receivers, fine_edge_in), "fine_local", cost(4_000_000_000, 2_000_000),
        )

    weights = (fine_edge_in, fine_edge_out, fine_node_in, fine_node_out)
    scratch = [pltpu.VMEM((EDGES, 512), BF16), pltpu.VMEM((CELLS, LATENT), BF16)]

    outgoing = call(outgoing_kernel, shape(RIM, LATENT), [VMEM] * 2, (nodes, rows), "outgoing", cost(10**9, 10**6))
    halo = exchange(outgoing)
    pre = fine_local(nodes, edges)
    cells, edges_one, own, to_left, to_right = call(
        fine_pool_kernel,
        [shape(CELLS, LATENT), shape(EDGES, LATENT), shape(CLUS, LATENT, dtype=F32)] + [shape(CLUS, LATENT)] * 2,
        [SMEM] + [VMEM] * 15,
        (flags, pre, edges, nodes, senders, receivers, *halo, *weights, labels),
        "fine_pool", cost(4_000_000_000, 2_000_000), scratch + [pltpu.VMEM((CELLS, 384), BF16)],
    )
    from_left, from_right = exchange_row(to_left, to_right)
    pooled = ((own + from_left + from_right) / FAN).astype(BF16)
    halo = exchange(pooled)
    pre = call(
        coarse_local_kernel, shape(CEDGES, LATENT, dtype=F32), [VMEM] * 4,
        (pooled, csenders, creceivers, coarse_edge_in), "coarse_local", cost(10**9, 10**6),
    )
    coarse = call(
        coarse_kernel, shape(CLUS, LATENT), [SMEM] + [VMEM] * 13,
        (flags, pre, pooled, csenders, creceivers, *halo,
         coarse_edge_in, coarse_edge_out, coarse_node_in, coarse_node_out),
        "coarse", cost(2 * 10**9, 10**6),
    )
    left, right = exchange_row(coarse, coarse)
    cells_two, outgoing = call(
        prolong_kernel, [shape(CELLS, LATENT), shape(RIM, LATENT)], [SMEM] + [VMEM] * 8,
        (flags, cells, labels, coarse, left, right, rows, prolong_in, prolong_out),
        "prolong", cost(2 * 10**9, 10**6),
    )
    halo = exchange(outgoing)
    pre = fine_local(cells_two, edges_one)
    node_out, edge_out = call(
        fine_last_kernel, [shape(CELLS, LATENT), shape(EDGES, LATENT)], [SMEM] + [VMEM] * 14,
        (flags, pre, edges_one, cells_two, senders, receivers, *halo, *weights),
        "fine_last", cost(4_000_000_000, 2_000_000),
        scratch + [
            pltpu.VMEM((CELLS, LATENT), BF16), pltpu.VMEM((EDGES, LATENT), BF16),
            pltpu.SemaphoreType.DMA((1 + CELL_PARTS,)),
        ],
        [ANY, ANY],
    )
    return node_out[None, None], edge_out[None, None]


def solution(mesh):
    split = P("px", "py", None)
    cells = P("px", "py", None, None)
    return jax.shard_map(
        on_device,
        mesh=mesh,
        in_specs=(cells, cells) + (split,) * 6 + (P(),) * 10,
        out_specs=(cells, cells),
        check_vma=False,
    )
```

time: 74 us -> 62.6 us (0.85)
  the two profiles are of different devices: /device:TPU:196 before, /device:TPU:223 now
where the time goes in v2:
time: 62.6 us; the launch traced here: 62.3 us
  starting transfers between devices  30.8 us (49%)
  Pallas kernels  15.7 us (25%)
  waiting for transfers between devices  12.7 us (20%)
  local copies, waits for them, and re-layouts  1.22 us (2%)
  between operations  1.1 us (2%)
  other arithmetic  0.72 us (1%)
    pallas_call x8, Pallas kernels, call(): pl.pallas_call(kernel, out_shape=outs, in_specs=ins, out_specs=where or j...  15.7 us
    ppermute x3, starting transfers between devices, exchange(): cross = lax.ppermute(block, 'px', crossing)  14 us
    ppermute x5, starting transfers between devices, exchange_row(): lax.ppermute(to_right, 'py', [(i, (i + 1) % count) for i in range(count)])  12.2 us
    ppermute x5, waiting for transfers between devices, exchange_row(): lax.ppermute(to_left, 'py', [((i + 1) % count, i) for i in range(count)])  9.56 us
    ppermute x3, starting transfers between devices, exchange(): first = lax.ppermute(block, ('px', 'py'), ring)  4.39 us
    ppermute x3, waiting for transfers between devices, exchange(): cross = lax.ppermute(block, 'px', crossing)  1.76 us
    ppermute x5, waiting for transfers between devices, exchange_row(): lax.ppermute(to_right, 'py', [(i, (i + 1) % count) for i in range(count)])  1.34 us
  transfers between devices with their start and end apart: 19, of which 7 were waited for; matrix products, arithmetic and copies ran while one was open for 0% of the time, Pallas kernels for 6%

profile of v2, /device:TPU:223, one launch (start us, length us, event | category | flops | bytes accessed | tf_op | source)
XLA Modules:
  0.0 62.3 jit_solution(11041608056638628825)
XLA Ops:
  0.6 0.7 %broadcast_add_fusion = s32[1,1,256]{2,1,0:T(1,128)S(1)} fusion(s32[1,1,256]{2,1,0:T(1,128)} %param.22), kind=kLoop, calls=%fused_computation.1 | loop fusion | flops 256 | bytes 2048 | tf_op jit(solution)/shard_map/add | solution.py:269
  1.3 1.0 %copy-done = bf16[1,1,2048,128]{3,2,1,0:T(8,128)(2,1)S(1)} copy-done((bf16[1,1,2048,128]{3,2,1,0:T(8,128)(2,1)S(1)}, bf16[1,1,2048,128]{3,2,1,0:T(8,128)(2,1)}, u32[]{:S(2)}) %copy-start) | copy-done | bytes 524312
  2.4 0.4 outgoing.1
  2.7 0.0 copy-start.16
  2.7 5.1 %collective-permute-start.4 = (bf16[256,128]{1,0:T(8,128)(2,1)S(1)}, bf16[256,128]{1,0:T(8,128)(2,1)S(1)}, u32[]{:S(2)}, u32[]{:S(2)}) collective-permute-start(bf16[256,128]{1,0:T(8,128)(2,1)S(1)} %outgoing.1), channel_id=1, source_target_pairs={{48,64},{64,48},{112,128},{128,112},{176,192},{192,176},{240,256},... | collective-permute-start | bytes 196616 | tf_op jit(solution)/shard_map/ppermute | solution.py:251
  7.9 3.4 %collective-permute-start.3 = (bf16[256,128]{1,0:T(8,128)(2,1)S(1)}, bf16[256,128]{1,0:T(8,128)(2,1)S(1)}, u32[]{:S(2)}, u32[]{:S(2)}) collective-permute-start(bf16[256,128]{1,0:T(8,128)(2,1)S(1)} %outgoing.1), channel_id=1, source_target_pairs={{0,1},{1,2},{2,3},{3,4},{4,5},{5,6},{6,7},{7,8},{8,9},{9,10},{10,1... | collective-permute-start | bytes 196616 | tf_op jit(solution)/shard_map/ppermute | solution.py:257
  11.2 0.0 collective-permute-start.2
  11.2 0.0 collective-permute-start.1
  11.2 1.5 %collective-permute-start = (bf16[256,128]{1,0:T(8,128)(2,1)S(1)}, bf16[256,128]{1,0:T(8,128)(2,1)S(1)}, u32[]{:S(2)}, u32[]{:S(2)}) collective-permute-start(bf16[256,128]{1,0:T(8,128)(2,1)S(1)} %outgoing.1), channel_id=1, source_target_pairs={{0,16},{1,0},{2,18},{3,2},{4,20},{5,4},{6,22},{7,6},{8,24},{9,8},{... | collective-permute-start | bytes 196616 | tf_op jit(solution)/shard_map/ppermute | solution.py:249
  12.7 0.0 copy-done.2
  12.7 0.0 copy-done.3
  12.7 0.0 copy-done.17
  12.7 0.0 copy-done.16
  12.7 0.0 copy-start.1
  12.7 0.0 copy-start.12
  12.7 0.0 copy-start.13
  12.7 1.6 %fine_local.2.pre = f32[1024,128]{1,0:T(8,128)S(1)} custom-call(bf16[2048,128]{1,0:T(8,128)(2,1)S(1)} %bitcast.18, bf16[1024,128]{1,0:T(8,128)(2,1)S(1)} %bitcast.20, s32[8,128]{1,0:T(8,128)S(1)} %bitcast.28, s32[8,128]{1,0:T(8,128)S(1)} %bitcast.32, bf16[384,128]{1,0:T(8,128)(2,1)S(1)} %copy-done.3), custom_call_target="tpu_custom_call" | custom-call | flops 4000000000 | bytes 2000000 | tf_op jit(solution)/shard_map/fine_local/pallas_call | solution.py:218
  14.3 0.0 copy-start.7
  14.3 0.0 copy-start.11
  14.4 0.1 stack.31.flags
  14.5 0.0 collective-permute-done.4.cross
  14.5 0.0 collective-permute-done.3.left
  14.5 1.7 %collective-permute-done.2.right = bf16[256,128]{1,0:T(8,128)(2,1)S(1)} collective-permute-done((bf16[256,128]{1,0:T(8,128)(2,1)S(1)}, bf16[256,128]{1,0:T(8,128)(2,1)S(1)}, u32[]{:S(2)}, u32[]{:S(2)}) %collective-permute-start.2) | collective-permute-done | bytes 65568 | tf_op jit(solution)/shard_map/ppermute | solution.py:258
  16.1 0.0 collective-permute-done.1.second
  16.1 0.0 collective-permute-done.first
  16.2 3.4 %fine_pool.1 = (bf16[2048,128]{1,0:T(8,128)(2,1)S(1)}, bf16[1024,128]{1,0:T(8,128)(2,1)S(1)}, f32[256,128]{1,0:T(8,128)S(1)}, bf16[256,128]{1,0:T(8,128)(2,1)S(1)}, bf16[256,128]{1,0:T(8,128)(2,1)S(1)}) custom-call(s32[5]{0:T(128)S(1)} %stack.31.flags, f32[1024,128]{1,0:T(8,128)S(1)} %fine_local.2.pre, bf16[1024,128]{1,0:T(8,128)(2,1)S(1)} %bitcast.21, ...), custom_call_target="tpu_custom_call" | custom-call | flops 4000000000 | bytes 2000000 | tf_op jit(solution)/shard_map/fine_pool/pallas_call | solution.py:218
  19.6 2.3 %collective-permute-start.5 = (bf16[256,128]{1,0:T(8,128)(2,1)S(1)}, bf16[256,128]{1,0:T(8,128)(2,1)S(1)}, u32[]{:S(2)}, u32[]{:S(2)}) collective-permute-start(bf16[256,128]{1,0:T(8,128)(2,1)S(1)} %get-tuple-element.13), channel_id=1, source_target_pairs={{0,1},{1,2},{2,3},{3,4},{4,5},{5,6},{6,7},{7,8},{8,9},{9,10},{10,1... | collective-permute-start | bytes 196616 | tf_op jit(solution)/shard_map/ppermute | solution.py:257
  21.9 0.0 collective-permute-start.6
  21.9 1.3 %collective-permute-done.5 = bf16[256,128]{1,0:T(8,128)(2,1)S(1)} collective-permute-done((bf16[256,128]{1,0:T(8,128)(2,1)S(1)}, bf16[256,128]{1,0:T(8,128)(2,1)S(1)}, u32[]{:S(2)}, u32[]{:S(2)}) %collective-permute-start.5) | collective-permute-done | bytes 65568 | tf_op jit(solution)/shard_map/ppermute | solution.py:257
  23.2 3.6 %collective-permute-done.6 = bf16[256,128]{1,0:T(8,128)(2,1)S(1)} collective-permute-done((bf16[256,128]{1,0:T(8,128)(2,1)S(1)}, bf16[256,128]{1,0:T(8,128)(2,1)S(1)}, u32[]{:S(2)}, u32[]{:S(2)}) %collective-permute-start.6) | collective-permute-done | bytes 65568 | tf_op jit(solution)/shard_map/ppermute | solution.py:258
  26.8 3.8 %collective-permute-start.11 = (bf16[256,128]{1,0:T(8,128)(2,1)S(1)}, bf16[256,128]{1,0:T(8,128)(2,1)S(1)}, u32[]{:S(2)}, u32[]{:S(2)}) collective-permute-start(bf16[256,128]{1,0:T(8,128)(2,1)S(1)} %multiply_convert_fusion.pooled), channel_id=1, source_target_pairs={{48,64},{64,48},{112,128},{128,112},{176,192},{192,176},{240,256},... | collective-permute-start | bytes 196616 | tf_op jit(solution)/shard_map/ppermute | solution.py:251
  30.6 0.3 collective-permute-start.10
  30.9 0.2 collective-permute-start.9
  31.1 0.0 collective-permute-start.8
  31.1 1.5 %collective-permute-start.7 = (bf16[256,128]{1,0:T(8,128)(2,1)S(1)}, bf16[256,128]{1,0:T(8,128)(2,1)S(1)}, u32[]{:S(2)}, u32[]{:S(2)}) collective-permute-start(bf16[256,128]{1,0:T(8,128)(2,1)S(1)} %multiply_convert_fusion.pooled), channel_id=1, source_target_pairs={{0,16},{1,0},{2,18},{3,2},{4,20},{5,4},{6,22},{7,6},{8,24},{9,8},{... | collective-permute-start | bytes 196616 | tf_op jit(solution)/shard_map/ppermute | solution.py:249
  32.6 0.0 copy-start.8
  32.6 0.0 copy-start.9
  32.6 0.8 %coarse_local.1.pre = f32[1024,128]{1,0:T(8,128)S(1)} custom-call(bf16[256,128]{1,0:T(8,128)(2,1)S(1)} %multiply_convert_fusion.pooled, s32[8,128]{1,0:T(8,128)S(1)} %bitcast.24, s32[8,128]{1,0:T(8,128)S(1)} %bitcast.26, bf16[256,128]{1,0:T(8,128)(2,1)S(1)} %copy-done.4), custom_call_target="tpu_custom_call" | custom-call | flops 1000000000 | bytes 1000000 | tf_op jit(solution)/shard_map/coarse_local/pallas_call | solution.py:218
  33.5 0.0 copy-start.6
  33.5 0.0 copy-start.10
  33.5 1.8 %collective-permute-done.11.cross = bf16[256,128]{1,0:T(8,128)(2,1)S(1)} collective-permute-done((bf16[256,128]{1,0:T(8,128)(2,1)S(1)}, bf16[256,128]{1,0:T(8,128)(2,1)S(1)}, u32[]{:S(2)}, u32[]{:S(2)}) %collective-permute-start.11) | collective-permute-done | bytes 65568 | tf_op jit(solution)/shard_map/ppermute | solution.py:251
  35.3 0.0 collective-permute-done.10.left
  35.3 0.5 collective-permute-done.9.right
  35.8 0.0 collective-permute-done.8.second
  35.8 0.0 collective-permute-done.7.first
  35.8 2.0 %coarse.1.own = bf16[256,128]{1,0:T(8,128)(2,1)S(1)} custom-call(s32[5]{0:T(128)S(1)} %stack.31.flags, f32[1024,128]{1,0:T(8,128)S(1)} %coarse_local.1.pre, bf16[256,128]{1,0:T(8,128)(2,1)S(1)} %multiply_convert_fusion.pooled, s32[8,128]{1,0:T(8,128)S(1)} %bitcast.25, s32[8,128]{1,0:T(8,128)S(1)} %bitcast.27, ...), custom_call_target="tpu_custom_call" | custom-call | flops 2000000000 | bytes 1000000 | tf_op jit(solution)/shard_map/coarse/pallas_call | solution.py:218
  37.9 0.0 collective-permute-start.13
  37.9 2.9 %collective-permute-start.12 = (bf16[256,128]{1,0:T(8,128)(2,1)S(1)}, bf16[256,128]{1,0:T(8,128)(2,1)S(1)}, u32[]{:S(2)}, u32[]{:S(2)}) collective-permute-start(bf16[256,128]{1,0:T(8,128)(2,1)S(1)} %coarse.1.own), channel_id=1, source_target_pairs={{0,1},{1,2},{2,3},{3,4},{4,5},{5,6},{6,7},{7,8},{8,9},{9,10},{10,1... | collective-permute-start | bytes 196616 | tf_op jit(solution)/shard_map/ppermute | solution.py:257
  40.9 1.9 %collective-permute-done.13.right = bf16[256,128]{1,0:T(8,128)(2,1)S(1)} collective-permute-done((bf16[256,128]{1,0:T(8,128)(2,1)S(1)}, bf16[256,128]{1,0:T(8,128)(2,1)S(1)}, u32[]{:S(2)}, u32[]{:S(2)}) %collective-permute-start.13) | collective-permute-done | bytes 65568 | tf_op jit(solution)/shard_map/ppermute | solution.py:258
  42.8 0.0 collective-permute-done.12.left
  42.8 0.0 copy-done.6
  42.8 2.3 %prolong.1 = (bf16[2048,128]{1,0:T(8,128)(2,1)S(1)}, bf16[256,128]{1,0:T(8,128)(2,1)S(1)}) custom-call(s32[5]{0:T(128)S(1)} %stack.31.flags, bf16[2048,128]{1,0:T(8,128)(2,1)S(1)} %get-tuple-element.11.cells, s32[16,128]{1,0:T(8,128)S(1)} %bitcast.23, bf16[256,128]{1,0:T(8,128)(2,1)S(1)} %coarse.1.own, bf16[256,128]{1,0:T(8,128)(2,1)S(1)} %collective-permute-done.12.left, ...), custom_call_target="tpu_custom_call" | custom-call | flops 2000000000 | bytes 1000000 | tf_op jit(solution)/shard_map/prolong/pallas_call | solution.py:218
  45.2 5.1 %collective-permute-start.18 = (bf16[256,128]{1,0:T(8,128)(2,1)S(1)}, bf16[256,128]{1,0:T(8,128)(2,1)S(1)}, u32[]{:S(2)}, u32[]{:S(2)}) collective-permute-start(bf16[256,128]{1,0:T(8,128)(2,1)S(1)} %get-tuple-element.17), channel_id=1, source_target_pairs={{48,64},{64,48},{112,128},{128,112},{176,192},{192,176},{240,256},... | collective-permute-start | bytes 196616 | tf_op jit(solution)/shard_map/ppermute | solution.py:251
  50.3 3.2 %collective-permute-start.17 = (bf16[256,128]{1,0:T(8,128)(2,1)S(1)}, bf16[256,128]{1,0:T(8,128)(2,1)S(1)}, u32[]{:S(2)}, u32[]{:S(2)}) collective-permute-start(bf16[256,128]{1,0:T(8,128)(2,1)S(1)} %get-tuple-element.17), channel_id=1, source_target_pairs={{0,1},{1,2},{2,3},{3,4},{4,5},{5,6},{6,7},{7,8},{8,9},{9,10},{10,1... | collective-permute-start | bytes 196616 | tf_op jit(solution)/shard_map/ppermute | solution.py:257
  53.5 0.0 collective-permute-start.16
  53.5 0.0 collective-permute-start.15
  53.5 1.5 %collective-permute-start.14 = (bf16[256,128]{1,0:T(8,128)(2,1)S(1)}, bf16[256,128]{1,0:T(8,128)(2,1)S(1)}, u32[]{:S(2)}, u32[]{:S(2)}) collective-permute-start(bf16[256,128]{1,0:T(8,128)(2,1)S(1)} %get-tuple-element.17), channel_id=1, source_target_pairs={{0,16},{1,0},{2,18},{3,2},{4,20},{5,4},{6,22},{7,6},{8,24},{9,8},{... | collective-permute-start | bytes 196616 | tf_op jit(solution)/shard_map/ppermute | solution.py:249
  55.0 1.5 %fine_local.3.pre = f32[1024,128]{1,0:T(8,128)S(1)} custom-call(bf16[2048,128]{1,0:T(8,128)(2,1)S(1)} %get-tuple-element.15.nodes, bf16[1024,128]{1,0:T(8,128)(2,1)S(1)} %get-tuple-element.16.edges, s32[8,128]{1,0:T(8,128)S(1)} %bitcast.30, s32[8,128]{1,0:T(8,128)S(1)} %bitcast.34, bf16[384,128]{1,0:T(8,128)(2,1)S(1)} %copy-done.3), custom_call_target="tpu_custom_call" | custom-call | flops 4000000000 | bytes 2000000 | tf_op jit(solution)/shard_map/fine_local/pallas_call | solution.py:218
  56.6 0.0 collective-permute-done.18.cross
  56.6 0.0 collective-permute-done.17.left
  56.6 1.9 %collective-permute-done.16.right = bf16[256,128]{1,0:T(8,128)(2,1)S(1)} collective-permute-done((bf16[256,128]{1,0:T(8,128)(2,1)S(1)}, bf16[256,128]{1,0:T(8,128)(2,1)S(1)}, u32[]{:S(2)}, u32[]{:S(2)}) %collective-permute-start.16) | collective-permute-done | bytes 65568 | tf_op jit(solution)/shard_map/ppermute | solution.py:258
  58.4 0.0 collective-permute-done.15.second
  58.4 0.0 collective-permute-done.14.first
  58.4 3.7 %fine_last.1 = (bf16[2048,128]{1,0:T(8,128)(2,1)}, bf16[1024,128]{1,0:T(8,128)(2,1)}) custom-call(s32[5]{0:T(128)S(1)} %stack.31.flags, f32[1024,128]{1,0:T(8,128)S(1)} %fine_local.3.pre, bf16[1024,128]{1,0:T(8,128)(2,1)S(1)} %get-tuple-element.16.edges, bf16[2048,128]{1,0:T(8,128)(2,1)S(1)} %get-tuple-element.15.nodes, s32[8,128]{1,0:T(8,128)S(1)} %bitcast.31, ...), custom_call_target="tpu_custom_call" | custom-call | flops 4000000000 | bytes 2000000 | tf_op jit(solution)/shard_map/fine_last/pallas_call | solution.py:218
  (21 shorter events, 0.1 us)
Async XLA Ops:
  1.3 1.0 %copy-start = (bf16[1,1,2048,128]{3,2,1,0:T(8,128)(2,1)S(1)}, bf16[1,1,2048,128]{3,2,1,0:T(8,128)(2,1)}, u32[]{:S(2)}) copy-start(bf16[1,1,2048,128]{3,2,1,0:T(8,128)(2,1)} %param.18) | copy-start | bytes 1572868
  2.4 10.3 %copy-start.2 = (bf16[1,1,1024,128]{3,2,1,0:T(8,128)(2,1)S(1)}, bf16[1,1,1024,128]{3,2,1,0:T(8,128)(2,1)}, u32[]{:S(2)}) copy-start(bf16[1,1,1024,128]{3,2,1,0:T(8,128)(2,1)} %param.19) | copy-start | bytes 786436
  2.4 10.3 %copy-start.3 = (bf16[384,128]{1,0:T(8,128)(2,1)S(1)}, bf16[384,128]{1,0:T(8,128)(2,1)}, u32[]{:S(2)}) copy-start(bf16[384,128]{1,0:T(8,128)(2,1)} %edge_in.5) | copy-start | bytes 294916
  2.4 10.3 %copy-start.17 = (s32[1,1,1024]{2,1,0:T(1,128)S(1)}, s32[1,1,1024]{2,1,0:T(1,128)}, u32[]{:S(2)}) copy-start(s32[1,1,1024]{2,1,0:T(1,128)} %param.21) | copy-start | bytes 12292
  2.7 10.0 %copy-start.16 = (s32[1,1,1024]{2,1,0:T(1,128)S(1)}, s32[1,1,1024]{2,1,0:T(1,128)}, u32[]{:S(2)}) copy-start(s32[1,1,1024]{2,1,0:T(1,128)} %param.20) | copy-start | bytes 12292
  2.7 11.7 %collective-permute-start.4 = (bf16[256,128]{1,0:T(8,128)(2,1)S(1)}, bf16[256,128]{1,0:T(8,128)(2,1)S(1)}, u32[]{:S(2)}, u32[]{:S(2)}) collective-permute-start(bf16[256,128]{1,0:T(8,128)(2,1)S(1)} %outgoing.1), channel_id=1, source_target_pairs={{48,64},{64,48},{112,128},{128,112},{176,192},{192,176},{240,256},... | collective-permute-start | bytes 196616 | tf_op jit(solution)/shard_map/ppermute | solution.py:251
  7.9 6.6 %collective-permute-start.3 = (bf16[256,128]{1,0:T(8,128)(2,1)S(1)}, bf16[256,128]{1,0:T(8,128)(2,1)S(1)}, u32[]{:S(2)}, u32[]{:S(2)}) collective-permute-start(bf16[256,128]{1,0:T(8,128)(2,1)S(1)} %outgoing.1), channel_id=1, source_target_pairs={{0,1},{1,2},{2,3},{3,4},{4,5},{5,6},{6,7},{7,8},{8,9},{9,10},{10,1... | collective-permute-start | bytes 196616 | tf_op jit(solution)/shard_map/ppermute | solution.py:257
  11.2 4.9 %collective-permute-start.2 = (bf16[256,128]{1,0:T(8,128)(2,1)S(1)}, bf16[256,128]{1,0:T(8,128)(2,1)S(1)}, u32[]{:S(2)}, u32[]{:S(2)}) collective-permute-start(bf16[256,128]{1,0:T(8,128)(2,1)S(1)} %outgoing.1), channel_id=1, source_target_pairs={{1,0},{2,1},{3,2},{4,3},{5,4},{6,5},{7,6},{8,7},{9,8},{10,9},{11,1... | collective-permute-start | bytes 196616 | tf_op jit(solution)/shard_map/ppermute | solution.py:258
  11.2 4.9 %collective-permute-start.1 = (bf16[256,128]{1,0:T(8,128)(2,1)S(1)}, bf16[256,128]{1,0:T(8,128)(2,1)S(1)}, u32[]{:S(2)}, u32[]{:S(2)}) collective-permute-start(bf16[256,128]{1,0:T(8,128)(2,1)S(1)} %outgoing.1), channel_id=1, source_target_pairs={{16,0},{0,1},{18,2},{2,3},{20,4},{4,5},{22,6},{6,7},{24,8},{8,9},{... | collective-permute-start | bytes 196616 | tf_op jit(solution)/shard_map/ppermute | solution.py:250
  11.2 4.9 %collective-permute-start = (bf16[256,128]{1,0:T(8,128)(2,1)S(1)}, bf16[256,128]{1,0:T(8,128)(2,1)S(1)}, u32[]{:S(2)}, u32[]{:S(2)}) collective-permute-start(bf16[256,128]{1,0:T(8,128)(2,1)S(1)} %outgoing.1), channel_id=1, source_target_pairs={{0,16},{1,0},{2,18},{3,2},{4,20},{5,4},{6,22},{7,6},{8,24},{9,8},{... | collective-permute-start | bytes 196616 | tf_op jit(solution)/shard_map/ppermute | solution.py:249
  12.7 3.4 %copy-start.1 = (bf16[1,1,2048,128]{3,2,1,0:T(8,128)(2,1)S(1)}, bf16[1,1,2048,128]{3,2,1,0:T(8,128)(2,1)}, u32[]{:S(2)}) copy-start(bf16[1,1,2048,128]{3,2,1,0:T(8,128)(2,1)} %param.18) | copy-start | bytes 1572868
  12.7 3.4 %copy-start.12 = (bf16[128,128]{1,0:T(8,128)(2,1)S(1)}, bf16[128,128]{1,0:T(8,128)(2,1)}, u32[]{:S(2)}) copy-start(bf16[128,128]{1,0:T(8,128)(2,1)} %node_out.5) | copy-start | bytes 98308
  12.7 3.4 %copy-start.13 = (s32[1,1,2048]{2,1,0:T(1,128)S(1)}, s32[1,1,2048]{2,1,0:T(1,128)}, u32[]{:S(2)}) copy-start(s32[1,1,2048]{2,1,0:T(1,128)} %param.23) | copy-start | bytes 24580
  14.3 1.9 %copy-start.7 = (bf16[256,128]{1,0:T(8,128)(2,1)S(1)}, bf16[256,128]{1,0:T(8,128)(2,1)}, u32[]{:S(2)}) copy-start(bf16[256,128]{1,0:T(8,128)(2,1)} %node_in.5) | copy-start | bytes 196612
  14.3 1.8 %copy-start.11 = (bf16[128,128]{1,0:T(8,128)(2,1)S(1)}, bf16[128,128]{1,0:T(8,128)(2,1)}, u32[]{:S(2)}) copy-start(bf16[128,128]{1,0:T(8,128)(2,1)} %edge_out.5) | copy-start | bytes 98308
  19.6 3.6 %collective-permute-start.5 = (bf16[256,128]{1,0:T(8,128)(2,1)S(1)}, bf16[256,128]{1,0:T(8,128)(2,1)S(1)}, u32[]{:S(2)}, u32[]{:S(2)}) collective-permute-start(bf16[256,128]{1,0:T(8,128)(2,1)S(1)} %get-tuple-element.13), channel_id=1, source_target_pairs={{0,1},{1,2},{2,3},{3,4},{4,5},{5,6},{6,7},{7,8},{8,9},{9,10},{10,1... | collective-permute-start | bytes 196616 | tf_op jit(solution)/shard_map/ppermute | solution.py:257
  21.9 4.9 %collective-permute-start.6 = (bf16[256,128]{1,0:T(8,128)(2,1)S(1)}, bf16[256,128]{1,0:T(8,128)(2,1)S(1)}, u32[]{:S(2)}, u32[]{:S(2)}) collective-permute-start(bf16[256,128]{1,0:T(8,128)(2,1)S(1)} %get-tuple-element.14), channel_id=1, source_target_pairs={{1,0},{2,1},{3,2},{4,3},{5,4},{6,5},{7,6},{8,7},{9,8},{10,9},{11,1... | collective-permute-start | bytes 196616 | tf_op jit(solution)/shard_map/ppermute | solution.py:258
  26.8 5.8 %copy-start.4 = (bf16[256,128]{1,0:T(8,128)(2,1)S(1)}, bf16[256,128]{1,0:T(8,128)(2,1)}, u32[]{:S(2)}) copy-start(bf16[256,128]{1,0:T(8,128)(2,1)} %edge_in.4) | copy-start | bytes 196612
  26.8 5.8 %copy-start.14 = (s32[1,1,1024]{2,1,0:T(1,128)S(1)}, s32[1,1,1024]{2,1,0:T(1,128)}, u32[]{:S(2)}) copy-start(s32[1,1,1024]{2,1,0:T(1,128)} %param.24) | copy-start | bytes 12292
  26.8 5.8 %copy-start.15 = (s32[1,1,1024]{2,1,0:T(1,128)S(1)}, s32[1,1,1024]{2,1,0:T(1,128)}, u32[]{:S(2)}) copy-start(s32[1,1,1024]{2,1,0:T(1,128)} %param.25) | copy-start | bytes 12292
  26.8 8.5 %collective-permute-start.11 = (bf16[256,128]{1,0:T(8,128)(2,1)S(1)}, bf16[256,128]{1,0:T(8,128)(2,1)S(1)}, u32[]{:S(2)}, u32[]{:S(2)}) collective-permute-start(bf16[256,128]{1,0:T(8,128)(2,1)S(1)} %multiply_convert_fusion.pooled), channel_id=1, source_target_pairs={{48,64},{64,48},{112,128},{128,112},{176,192},{192,176},{240,256},... | collective-permute-start | bytes 196616 | tf_op jit(solution)/shard_map/ppermute | solution.py:251
  30.6 4.7 %collective-permute-start.10 = (bf16[256,128]{1,0:T(8,128)(2,1)S(1)}, bf16[256,128]{1,0:T(8,128)(2,1)S(1)}, u32[]{:S(2)}, u32[]{:S(2)}) collective-permute-start(bf16[256,128]{1,0:T(8,128)(2,1)S(1)} %multiply_convert_fusion.pooled), channel_id=1, source_target_pairs={{0,1},{1,2},{2,3},{3,4},{4,5},{5,6},{6,7},{7,8},{8,9},{9,10},{10,1... | collective-permute-start | bytes 196616 | tf_op jit(solution)/shard_map/ppermute | solution.py:257
  30.9 4.9 %collective-permute-start.9 = (bf16[256,128]{1,0:T(8,128)(2,1)S(1)}, bf16[256,128]{1,0:T(8,128)(2,1)S(1)}, u32[]{:S(2)}, u32[]{:S(2)}) collective-permute-start(bf16[256,128]{1,0:T(8,128)(2,1)S(1)} %multiply_convert_fusion.pooled), channel_id=1, source_target_pairs={{1,0},{2,1},{3,2},{4,3},{5,4},{6,5},{7,6},{8,7},{9,8},{10,9},{11,1... | collective-permute-start | bytes 196616 | tf_op jit(solution)/shard_map/ppermute | solution.py:258
  31.1 4.7 %collective-permute-start.8 = (bf16[256,128]{1,0:T(8,128)(2,1)S(1)}, bf16[256,128]{1,0:T(8,128)(2,1)S(1)}, u32[]{:S(2)}, u32[]{:S(2)}) collective-permute-start(bf16[256,128]{1,0:T(8,128)(2,1)S(1)} %multiply_convert_fusion.pooled), channel_id=1, source_target_pairs={{16,0},{0,1},{18,2},{2,3},{20,4},{4,5},{22,6},{6,7},{24,8},{8,9},{... | collective-permute-start | bytes 196616 | tf_op jit(solution)/shard_map/ppermute | solution.py:250
  31.1 4.7 %collective-permute-start.7 = (bf16[256,128]{1,0:T(8,128)(2,1)S(1)}, bf16[256,128]{1,0:T(8,128)(2,1)S(1)}, u32[]{:S(2)}, u32[]{:S(2)}) collective-permute-start(bf16[256,128]{1,0:T(8,128)(2,1)S(1)} %multiply_convert_fusion.pooled), channel_id=1, source_target_pairs={{0,16},{1,0},{2,18},{3,2},{4,20},{5,4},{6,22},{7,6},{8,24},{9,8},{... | collective-permute-start | bytes 196616 | tf_op jit(solution)/shard_map/ppermute | solution.py:249
  32.6 3.2 %copy-start.5 = (bf16[256,128]{1,0:T(8,128)(2,1)S(1)}, bf16[256,128]{1,0:T(8,128)(2,1)}, u32[]{:S(2)}) copy-start(bf16[256,128]{1,0:T(8,128)(2,1)} %node_in.4) | copy-start | bytes 196612
  32.6 3.2 %copy-start.8 = (bf16[128,128]{1,0:T(8,128)(2,1)S(1)}, bf16[128,128]{1,0:T(8,128)(2,1)}, u32[]{:S(2)}) copy-start(bf16[128,128]{1,0:T(8,128)(2,1)} %edge_out.4) | copy-start | bytes 98308
  32.6 3.2 %copy-start.9 = (bf16[128,128]{1,0:T(8,128)(2,1)S(1)}, bf16[128,128]{1,0:T(8,128)(2,1)}, u32[]{:S(2)}) copy-start(bf16[128,128]{1,0:T(8,128)(2,1)} %node_out.4) | copy-start | bytes 98308
  33.5 9.3 %copy-start.6 = (bf16[256,128]{1,0:T(8,128)(2,1)S(1)}, bf16[256,128]{1,0:T(8,128)(2,1)}, u32[]{:S(2)}) copy-start(bf16[256,128]{1,0:T(8,128)(2,1)} %first.6) | copy-start | bytes 196612
  33.5 9.3 %copy-start.10 = (bf16[128,128]{1,0:T(8,128)(2,1)S(1)}, bf16[128,128]{1,0:T(8,128)(2,1)}, u32[]{:S(2)}) copy-start(bf16[128,128]{1,0:T(8,128)(2,1)} %second.1) | copy-start | bytes 98308
  37.9 4.9 %collective-permute-start.13 = (bf16[256,128]{1,0:T(8,128)(2,1)S(1)}, bf16[256,128]{1,0:T(8,128)(2,1)S(1)}, u32[]{:S(2)}, u32[]{:S(2)}) collective-permute-start(bf16[256,128]{1,0:T(8,128)(2,1)S(1)} %coarse.1.own), channel_id=1, source_target_pairs={{1,0},{2,1},{3,2},{4,3},{5,4},{6,5},{7,6},{8,7},{9,8},{10,9},{11,1... | collective-permute-start | bytes 196616 | tf_op jit(solution)/shard_map/ppermute | solution.py:258
  37.9 4.9 %collective-permute-start.12 = (bf16[256,128]{1,0:T(8,128)(2,1)S(1)}, bf16[256,128]{1,0:T(8,128)(2,1)S(1)}, u32[]{:S(2)}, u32[]{:S(2)}) collective-permute-start(bf16[256,128]{1,0:T(8,128)(2,1)S(1)} %coarse.1.own), channel_id=1, source_target_pairs={{0,1},{1,2},{2,3},{3,4},{4,5},{5,6},{6,7},{7,8},{8,9},{9,10},{10,1... | collective-permute-start | bytes 196616 | tf_op jit(solution)/shard_map/ppermute | solution.py:257
  45.2 11.4 %collective-permute-start.18 = (bf16[256,128]{1,0:T(8,128)(2,1)S(1)}, bf16[256,128]{1,0:T(8,128)(2,1)S(1)}, u32[]{:S(2)}, u32[]{:S(2)}) collective-permute-start(bf16[256,128]{1,0:T(8,128)(2,1)S(1)} %get-tuple-element.17), channel_id=1, source_target_pairs={{48,64},{64,48},{112,128},{128,112},{176,192},{192,176},{240,256},... | collective-permute-start | bytes 196616 | tf_op jit(solution)/shard_map/ppermute | solution.py:251
  50.3 6.3 %collective-permute-start.17 = (bf16[256,128]{1,0:T(8,128)(2,1)S(1)}, bf16[256,128]{1,0:T(8,128)(2,1)S(1)}, u32[]{:S(2)}, u32[]{:S(2)}) collective-permute-start(bf16[256,128]{1,0:T(8,128)(2,1)S(1)} %get-tuple-element.17), channel_id=1, source_target_pairs={{0,1},{1,2},{2,3},{3,4},{4,5},{5,6},{6,7},{7,8},{8,9},{9,10},{10,1... | collective-permute-start | bytes 196616 | tf_op jit(solution)/shard_map/ppermute | solution.py:257
  53.5 4.9 %collective-permute-start.16 = (bf16[256,128]{1,0:T(8,128)(2,1)S(1)}, bf16[256,128]{1,0:T(8,128)(2,1)S(1)}, u32[]{:S(2)}, u32[]{:S(2)}) collective-permute-start(bf16[256,128]{1,0:T(8,128)(2,1)S(1)} %get-tuple-element.17), channel_id=1, source_target_pairs={{1,0},{2,1},{3,2},{4,3},{5,4},{6,5},{7,6},{8,7},{9,8},{10,9},{11,1... | collective-permute-start | bytes 196616 | tf_op jit(solution)/shard_map/ppermute | solution.py:258
  53.5 4.9 %collective-permute-start.15 = (bf16[256,128]{1,0:T(8,128)(2,1)S(1)}, bf16[256,128]{1,0:T(8,128)(2,1)S(1)}, u32[]{:S(2)}, u32[]{:S(2)}) collective-permute-start(bf16[256,128]{1,0:T(8,128)(2,1)S(1)} %get-tuple-element.17), channel_id=1, source_target_pairs={{16,0},{0,1},{18,2},{2,3},{20,4},{4,5},{22,6},{6,7},{24,8},{8,9},{... | collective-permute-start | bytes 196616 | tf_op jit(solution)/shard_map/ppermute | solution.py:250
  53.5 4.9 %collective-permute-start.14 = (bf16[256,128]{1,0:T(8,128)(2,1)S(1)}, bf16[256,128]{1,0:T(8,128)(2,1)S(1)}, u32[]{:S(2)}, u32[]{:S(2)}) collective-permute-start(bf16[256,128]{1,0:T(8,128)(2,1)S(1)} %get-tuple-element.17), channel_id=1, source_target_pairs={{0,16},{1,0},{2,18},{3,2},{4,20},{5,4},{6,22},{7,6},{8,24},{9,8},{... | collective-permute-start | bytes 196616 | tf_op jit(solution)/shard_map/ppermute | solution.py:249

commit v3 on v2

--- a/solution.py
+++ b/solution.py
@@ -115,11 +115,13 @@
     out[...] = from_cells(table, column(rows, 0, 2) - 1)
 
 
+def local_product(table, edges, senders, receivers, first):
+    near = from_cells(table, jnp.concatenate([column(senders, 0, 8), column(receivers, 0, 8)], axis=0))
+    return dot(jnp.concatenate([edges[...], near[:EDGES], near[EDGES:]], axis=1), first[...])
+
+
 def fine_local_kernel(nodes, edges, senders, receivers, first, out):
-    table = side_by_side(nodes[...], 4)
-
-    near = from_cells(table, jnp.concatenate([column(senders, 0, 8), column(receivers, 0, 8)], axis=0))
-    out[...] = dot(jnp.concatenate([edges[...], near[:EDGES], near[EDGES:]], axis=1), first[...])
+    out[...] = local_product(side_by_side(nodes[...], 4), edges, senders, receivers, first)
 
 
 def edge_part(flags, pre, edges, senders, receivers, halo, edge_in, edge_out, new_edges, wide, sums):
@@ -199,15 +201,33 @@
     out[...] = (own.astype(F32) + finish(dot(inputs, node_in[...]), centred_layer(node_out[...]))).astype(BF16)
 
 
-def prolong_kernel(flags, cells, labels, own, left, right, rows, first, second, new_cells, outgoing):
+def rim_kernel(flags, cells, labels, rows, rim, rim_labels):
+    index = column(rows, 0, 2) - 1
+    label = column(labels, 0, 16) - flags[4]
+    rim[...] = from_cells(side_by_side(cells[...], 4), index)
+    low = from_cells(side_by_side((label & 255).astype(F32).astype(BF16), 4), index)
+    block = from_cells(side_by_side((label >> 8).astype(F32).astype(BF16), 4), index)
+    rim_labels[...] = low.astype(F32).astype(jnp.int32) + 256 * block.astype(F32).astype(jnp.int32)
+
+
+def lift(old, label, own, left, right, first, second):
     table = jnp.concatenate([left[...], own[...], right[...]], axis=1)
-    index = column(labels, 0, 16) - flags[4]
-    looked = choose(dot(pick_rows(index & 255, 256, 0), table), index >> 8, 3).astype(BF16)
-    old = cells[...]
+    looked = choose(dot(pick_rows(label & 255, 256, 0), table), label >> 8, 3).astype(BF16)
     update = finish(dot(jnp.concatenate([old, looked], axis=1), first[...]), centred_layer(second[...]))
-    new = (old.astype(F32) + update).astype(BF16)
+    return (old.astype(F32) + update).astype(BF16)
+
+
+def lift_rim_kernel(rim, rim_labels, own, left, right, first, second, out):
+    out[...] = lift(rim[...], rim_labels[...], own, left, right, first, second)
+
+
+def lift_local_kernel(
+    flags, cells, labels, own, left, right, first, second, edges, senders, receivers, edge_in, new_cells, out
+):
+    label = column(labels, 0, 16) - flags[4]
+    new = lift(cells[...], label, own, left, right, first, second)
     new_cells[...] = new
-    outgoing[...] = from_cells(side_by_side(new, 4), column(rows, 0, 2) - 1)
+    out[...] = local_product(side_by_side(new, 4), edges, senders, receivers, edge_in)
 
 
 def shape(*dims, dtype=BF16):
@@ -275,18 +295,15 @@
     down = jnp.where(along < ROWS - 1, 1 - core, jnp.where(i < last_i, 2, 3))
     flags = jnp.stack([up, down, j > 0, j < last_j, (j - 1) * CLUS]).astype(jnp.int32)
 
-    def fine_local(nodes, edges):
-        return call(
-            fine_local_kernel, shape(EDGES, LATENT, dtype=F32), [VMEM] * 5,
-            (nodes, edges, senders, receivers, fine_edge_in), "fine_local", cost(4_000_000_000, 2_000_000),
-        )
-
     weights = (fine_edge_in, fine_edge_out, fine_node_in, fine_node_out)
     scratch = [pltpu.VMEM((EDGES, 512), BF16), pltpu.VMEM((CELLS, LATENT), BF16)]
 
     outgoing = call(outgoing_kernel, shape(RIM, LATENT), [VMEM] * 2, (nodes, rows), "outgoing", cost(10**9, 10**6))
     halo = exchange(outgoing)
-    pre = fine_local(nodes, edges)
+    pre = call(
+        fine_local_kernel, shape(EDGES, LATENT, dtype=F32), [VMEM] * 5,
+        (nodes, edges, senders, receivers, fine_edge_in), "fine_local", cost(4 * 10**9, 2 * 10**6),
+    )
     cells, edges_one, own, to_left, to_right = call(
         fine_pool_kernel,
         [shape(CELLS, LATENT), shape(EDGES, LATENT), shape(CLUS, LATENT, dtype=F32)] + [shape(CLUS, LATENT)] * 2,
@@ -307,14 +324,22 @@
          coarse_edge_in, coarse_edge_out, coarse_node_in, coarse_node_out),
         "coarse", cost(2 * 10**9, 10**6),
     )
+    rim, rim_labels = call(
+        rim_kernel, [shape(RIM, LATENT), shape(RIM, LATENT, dtype=jnp.int32)], [SMEM] + [VMEM] * 3,
+        (flags, cells, labels, rows), "rim", cost(10**9, 10**6),
+    )
     left, right = exchange_row(coarse, coarse)
-    cells_two, outgoing = call(
-        prolong_kernel, [shape(CELLS, LATENT), shape(RIM, LATENT)], [SMEM] + [VMEM] * 8,
-        (flags, cells, labels, coarse, left, right, rows, prolong_in, prolong_out),
-        "prolong", cost(2 * 10**9, 10**6),
+    outgoing = call(
+        lift_rim_kernel, shape(RIM, LATENT), [VMEM] * 7,
+        (rim, rim_labels, coarse, left, right, prolong_in, prolong_out), "lift_rim", cost(10**8, 10**5),
     )
     halo = exchange(outgoing)
-    pre = fine_local(cells_two, edges_one)
+    cells_two, pre = call(
+        lift_local_kernel, [shape(CELLS, LATENT), shape(EDGES, LATENT, dtype=F32)], [SMEM] + [VMEM] * 11,
+        (flags, cells, labels, coarse, left, right, prolong_in, prolong_out,
+         edges_one, senders, receivers, fine_edge_in),
+        "lift_local", cost(4 * 10**9, 10**6),
+    )
     node_out, edge_out = call(
         fine_last_kernel, [shape(CELLS, LATENT), shape(EDGES, LATENT)], [SMEM] + [VMEM] * 14,
         (flags, pre, edges_one, cells_two, senders, receivers, *halo, *weights),

time: 62.6 us -> 60.8 us (0.971)
  waiting for transfers between devices: 12.7 us -> 9.59 us
  Pallas kernels: 15.7 us -> 17 us
    ppermute x5, waiting for transfers between devices: 9.56 us -> 6.45 us  [exchange_row(): lax.ppermute(to_left, 'py', [((i + 1) % count, i) for i in range(count)])]
    pallas_call x8 -> x9, Pallas kernels: 15.7 us -> 17 us  [call(): pl.pallas_call(kernel, out_shape=outs, in_specs=ins, out_specs=where or j...]
  transfers between devices with their start and end apart: 19 -> 19, of which waited for: 7 -> 6; matrix products, arithmetic and copies ran while one was open for 0% -> 0% of each run, Pallas kernels for 6% -> 12%
where the time goes in v3:
time: 60.8 us; the launch traced here: 60.5 us
  starting transfers between devices  30.8 us (51%)
  Pallas kernels  17 us (28%)
  waiting for transfers between devices  9.59 us (16%)
  local copies, waits for them, and re-layouts  1.21 us (2%)
  between operations  1.08 us (2%)
  other arithmetic  0.72 us (1%)
    pallas_call x9, Pallas kernels, call(): pl.pallas_call(kernel, out_shape=outs, in_specs=ins, out_specs=where or j...  17 us
    ppermute x3, starting transfers between devices, exchange(): cross = lax.ppermute(block, 'px', crossing)  14 us
    ppermute x5, starting transfers between devices, exchange_row(): lax.ppermute(to_right, 'py', [(i, (i + 1) % count) for i in range(count)])  12.2 us
    ppermute x5, waiting for transfers between devices, exchange_row(): lax.ppermute(to_left, 'py', [((i + 1) % count, i) for i in range(count)])  6.45 us
    ppermute x3, starting transfers between devices, exchange(): first = lax.ppermute(block, ('px', 'py'), ring)  4.39 us
    ppermute x3, waiting for transfers between devices, exchange(): cross = lax.ppermute(block, 'px', crossing)  1.79 us
    ppermute x5, waiting for transfers between devices, exchange_row(): lax.ppermute(to_right, 'py', [(i, (i + 1) % count) for i in range(count)])  1.34 us
  transfers between devices with their start and end apart: 19, of which 6 were waited for; matrix products, arithmetic and copies ran while one was open for 0% of the time, Pallas kernels for 12%

profile of v3, /device:TPU:223, one launch (start us, length us, event | category | flops | bytes accessed | tf_op | source)
XLA Modules:
  0.0 60.5 jit_solution(15077498205973696181)
XLA Ops:
  0.6 0.7 %broadcast_add_fusion = s32[1,1,256]{2,1,0:T(1,128)S(1)} fusion(s32[1,1,256]{2,1,0:T(1,128)} %param.22), kind=kLoop, calls=%fused_computation.1 | loop fusion | flops 256 | bytes 2048 | tf_op jit(solution)/shard_map/add | solution.py:289
  1.3 1.0 %copy-done.2 = bf16[1,1,2048,128]{3,2,1,0:T(8,128)(2,1)S(1)} copy-done((bf16[1,1,2048,128]{3,2,1,0:T(8,128)(2,1)S(1)}, bf16[1,1,2048,128]{3,2,1,0:T(8,128)(2,1)}, u32[]{:S(2)}) %copy-start.2) | copy-done | bytes 524312
  2.4 0.4 outgoing.1
  2.7 0.0 copy-start.16
  2.7 5.1 %collective-permute-start.4 = (bf16[256,128]{1,0:T(8,128)(2,1)S(1)}, bf16[256,128]{1,0:T(8,128)(2,1)S(1)}, u32[]{:S(2)}, u32[]{:S(2)}) collective-permute-start(bf16[256,128]{1,0:T(8,128)(2,1)S(1)} %outgoing.1), channel_id=1, source_target_pairs={{48,64},{64,48},{112,128},{128,112},{176,192},{192,176},{240,256},... | collective-permute-start | bytes 196616 | tf_op jit(solution)/shard_map/ppermute | solution.py:271
  7.9 3.4 %collective-permute-start.3 = (bf16[256,128]{1,0:T(8,128)(2,1)S(1)}, bf16[256,128]{1,0:T(8,128)(2,1)S(1)}, u32[]{:S(2)}, u32[]{:S(2)}) collective-permute-start(bf16[256,128]{1,0:T(8,128)(2,1)S(1)} %outgoing.1), channel_id=1, source_target_pairs={{0,1},{1,2},{2,3},{3,4},{4,5},{5,6},{6,7},{7,8},{8,9},{9,10},{10,1... | collective-permute-start | bytes 196616 | tf_op jit(solution)/shard_map/ppermute | solution.py:277
  11.2 0.0 collective-permute-start.2
  11.2 0.0 collective-permute-start.1
  11.2 1.5 %collective-permute-start = (bf16[256,128]{1,0:T(8,128)(2,1)S(1)}, bf16[256,128]{1,0:T(8,128)(2,1)S(1)}, u32[]{:S(2)}, u32[]{:S(2)}) collective-permute-start(bf16[256,128]{1,0:T(8,128)(2,1)S(1)} %outgoing.1), channel_id=1, source_target_pairs={{0,16},{1,0},{2,18},{3,2},{4,20},{5,4},{6,22},{7,6},{8,24},{9,8},{... | collective-permute-start | bytes 196616 | tf_op jit(solution)/shard_map/ppermute | solution.py:269
  12.7 0.0 copy-done.4
  12.7 0.0 copy-done.5
  12.7 0.0 copy-done.16
  12.7 0.0 copy-start.3
  12.7 0.0 copy-start.12
  12.7 0.0 copy-start.13
  12.7 1.6 %fine_local.1.pre = f32[1024,128]{1,0:T(8,128)S(1)} custom-call(bf16[2048,128]{1,0:T(8,128)(2,1)S(1)} %bitcast.18, bf16[1024,128]{1,0:T(8,128)(2,1)S(1)} %bitcast.20, s32[8,128]{1,0:T(8,128)S(1)} %bitcast.29, s32[8,128]{1,0:T(8,128)S(1)} %bitcast.33, bf16[384,128]{1,0:T(8,128)(2,1)S(1)} %copy-done.5), custom_call_target="tpu_custom_call" | custom-call | flops 4000000000 | bytes 2000000 | tf_op jit(solution)/shard_map/fine_local/pallas_call | solution.py:238
  14.3 0.0 copy-start.8
  14.3 0.0 copy-start.11
  14.4 0.1 stack.31.flags
  14.5 0.0 collective-permute-done.4.cross
  14.5 0.0 collective-permute-done.3.left
  14.5 1.7 %collective-permute-done.2.right = bf16[256,128]{1,0:T(8,128)(2,1)S(1)} collective-permute-done((bf16[256,128]{1,0:T(8,128)(2,1)S(1)}, bf16[256,128]{1,0:T(8,128)(2,1)S(1)}, u32[]{:S(2)}, u32[]{:S(2)}) %collective-permute-start.2) | collective-permute-done | bytes 65568 | tf_op jit(solution)/shard_map/ppermute | solution.py:278
  16.1 0.0 collective-permute-done.1.second
  16.1 0.0 collective-permute-done.first
  16.2 3.4 %fine_pool.1 = (bf16[2048,128]{1,0:T(8,128)(2,1)S(1)}, bf16[1024,128]{1,0:T(8,128)(2,1)S(1)}, f32[256,128]{1,0:T(8,128)S(1)}, bf16[256,128]{1,0:T(8,128)(2,1)S(1)}, bf16[256,128]{1,0:T(8,128)(2,1)S(1)}) custom-call(s32[5]{0:T(128)S(1)} %stack.31.flags, f32[1024,128]{1,0:T(8,128)S(1)} %fine_local.1.pre, bf16[1024,128]{1,0:T(8,128)(2,1)S(1)} %bitcast.21, ...), custom_call_target="tpu_custom_call" | custom-call | flops 4000000000 | bytes 2000000 | tf_op jit(solution)/shard_map/fine_pool/pallas_call | solution.py:238
  19.6 2.3 %collective-permute-start.5 = (bf16[256,128]{1,0:T(8,128)(2,1)S(1)}, bf16[256,128]{1,0:T(8,128)(2,1)S(1)}, u32[]{:S(2)}, u32[]{:S(2)}) collective-permute-start(bf16[256,128]{1,0:T(8,128)(2,1)S(1)} %get-tuple-element.15), channel_id=1, source_target_pairs={{0,1},{1,2},{2,3},{3,4},{4,5},{5,6},{6,7},{7,8},{8,9},{9,10},{10,1... | collective-permute-start | bytes 196616 | tf_op jit(solution)/shard_map/ppermute | solution.py:277
  21.9 0.0 collective-permute-start.6
  21.9 1.3 %collective-permute-done.5 = bf16[256,128]{1,0:T(8,128)(2,1)S(1)} collective-permute-done((bf16[256,128]{1,0:T(8,128)(2,1)S(1)}, bf16[256,128]{1,0:T(8,128)(2,1)S(1)}, u32[]{:S(2)}, u32[]{:S(2)}) %collective-permute-start.5) | collective-permute-done | bytes 65568 | tf_op jit(solution)/shard_map/ppermute | solution.py:277
  23.2 3.6 %collective-permute-done.6 = bf16[256,128]{1,0:T(8,128)(2,1)S(1)} collective-permute-done((bf16[256,128]{1,0:T(8,128)(2,1)S(1)}, bf16[256,128]{1,0:T(8,128)(2,1)S(1)}, u32[]{:S(2)}, u32[]{:S(2)}) %collective-permute-start.6) | collective-permute-done | bytes 65568 | tf_op jit(solution)/shard_map/ppermute | solution.py:278
  26.8 3.8 %collective-permute-start.11 = (bf16[256,128]{1,0:T(8,128)(2,1)S(1)}, bf16[256,128]{1,0:T(8,128)(2,1)S(1)}, u32[]{:S(2)}, u32[]{:S(2)}) collective-permute-start(bf16[256,128]{1,0:T(8,128)(2,1)S(1)} %multiply_convert_fusion.pooled), channel_id=1, source_target_pairs={{48,64},{64,48},{112,128},{128,112},{176,192},{192,176},{240,256},... | collective-permute-start | bytes 196616 | tf_op jit(solution)/shard_map/ppermute | solution.py:271
  30.6 0.3 collective-permute-start.10
  30.9 0.2 collective-permute-start.9
  31.1 0.0 collective-permute-start.8
  31.1 1.5 %collective-permute-start.7 = (bf16[256,128]{1,0:T(8,128)(2,1)S(1)}, bf16[256,128]{1,0:T(8,128)(2,1)S(1)}, u32[]{:S(2)}, u32[]{:S(2)}) collective-permute-start(bf16[256,128]{1,0:T(8,128)(2,1)S(1)} %multiply_convert_fusion.pooled), channel_id=1, source_target_pairs={{0,16},{1,0},{2,18},{3,2},{4,20},{5,4},{6,22},{7,6},{8,24},{9,8},{... | collective-permute-start | bytes 196616 | tf_op jit(solution)/shard_map/ppermute | solution.py:269
  32.6 0.0 copy-done.14
  32.6 0.0 copy-start.9
  32.6 0.0 copy-start.10
  32.6 0.8 %coarse_local.1.pre = f32[1024,128]{1,0:T(8,128)S(1)} custom-call(bf16[256,128]{1,0:T(8,128)(2,1)S(1)} %multiply_convert_fusion.pooled, s32[8,128]{1,0:T(8,128)S(1)} %bitcast.25, s32[8,128]{1,0:T(8,128)S(1)} %bitcast.27, bf16[256,128]{1,0:T(8,128)(2,1)S(1)} %copy-done.6), custom_call_target="tpu_custom_call" | custom-call | flops 1000000000 | bytes 1000000 | tf_op jit(solution)/shard_map/coarse_local/pallas_call | solution.py:238
  33.5 1.8 %collective-permute-done.11.cross = bf16[256,128]{1,0:T(8,128)(2,1)S(1)} collective-permute-done((bf16[256,128]{1,0:T(8,128)(2,1)S(1)}, bf16[256,128]{1,0:T(8,128)(2,1)S(1)}, u32[]{:S(2)}, u32[]{:S(2)}) %collective-permute-start.11) | collective-permute-done | bytes 65568 | tf_op jit(solution)/shard_map/ppermute | solution.py:271
  35.3 0.0 collective-permute-done.10.left
  35.3 0.5 collective-permute-done.9.right
  35.8 0.0 collective-permute-done.8.second
  35.8 0.0 collective-permute-done.7.first
  35.8 0.0 copy-done.9
  35.8 0.0 copy-done.10
  35.8 2.0 %coarse.1.own = bf16[256,128]{1,0:T(8,128)(2,1)S(1)} custom-call(s32[5]{0:T(128)S(1)} %stack.31.flags, f32[1024,128]{1,0:T(8,128)S(1)} %coarse_local.1.pre, bf16[256,128]{1,0:T(8,128)(2,1)S(1)} %multiply_convert_fusion.pooled, s32[8,128]{1,0:T(8,128)S(1)} %bitcast.26, s32[8,128]{1,0:T(8,128)S(1)} %bitcast.28, ...), custom_call_target="tpu_custom_call" | custom-call | flops 2000000000 | bytes 1000000 | tf_op jit(solution)/shard_map/coarse/pallas_call | solution.py:238
  37.9 0.0 collective-permute-start.13
  37.9 2.9 %collective-permute-start.12 = (bf16[256,128]{1,0:T(8,128)(2,1)S(1)}, bf16[256,128]{1,0:T(8,128)(2,1)S(1)}, u32[]{:S(2)}, u32[]{:S(2)}) collective-permute-start(bf16[256,128]{1,0:T(8,128)(2,1)S(1)} %coarse.1.own), channel_id=1, source_target_pairs={{0,1},{1,2},{2,3},{3,4},{4,5},{5,6},{6,7},{7,8},{8,9},{9,10},{10,1... | collective-permute-start | bytes 196616 | tf_op jit(solution)/shard_map/ppermute | solution.py:277
  40.9 1.3 %rim.1 = (bf16[256,128]{1,0:T(8,128)(2,1)S(1)}, s32[256,128]{1,0:T(8,128)S(1)}) custom-call(s32[5]{0:T(128)S(1)} %stack.31.flags, bf16[2048,128]{1,0:T(8,128)(2,1)S(1)} %get-tuple-element.13.cells, s32[16,128]{1,0:T(8,128)S(1)} %bitcast.23, s32[2,128]{1,0:T(2,128)S(1)} %bitcast.16), custom_call_target="tpu_custom_call" | custom-call | flops 1000000000 | bytes 1000000 | tf_op jit(solution)/shard_map/rim/pallas_call | solution.py:238
  42.2 0.6 %collective-permute-done.13.right = bf16[256,128]{1,0:T(8,128)(2,1)S(1)} collective-permute-done((bf16[256,128]{1,0:T(8,128)(2,1)S(1)}, bf16[256,128]{1,0:T(8,128)(2,1)S(1)}, u32[]{:S(2)}, u32[]{:S(2)}) %collective-permute-start.13) | collective-permute-done | bytes 65568 | tf_op jit(solution)/shard_map/ppermute | solution.py:278
  42.8 0.0 collective-permute-done.12.left
  42.8 0.6 lift_rim.1
  43.4 5.1 %collective-permute-start.18 = (bf16[256,128]{1,0:T(8,128)(2,1)S(1)}, bf16[256,128]{1,0:T(8,128)(2,1)S(1)}, u32[]{:S(2)}, u32[]{:S(2)}) collective-permute-start(bf16[256,128]{1,0:T(8,128)(2,1)S(1)} %lift_rim.1), channel_id=1, source_target_pairs={{48,64},{64,48},{112,128},{128,112},{176,192},{192,176},{240,256},... | collective-permute-start | bytes 196616 | tf_op jit(solution)/shard_map/ppermute | solution.py:271
  48.5 3.2 %collective-permute-start.17 = (bf16[256,128]{1,0:T(8,128)(2,1)S(1)}, bf16[256,128]{1,0:T(8,128)(2,1)S(1)}, u32[]{:S(2)}, u32[]{:S(2)}) collective-permute-start(bf16[256,128]{1,0:T(8,128)(2,1)S(1)} %lift_rim.1), channel_id=1, source_target_pairs={{0,1},{1,2},{2,3},{3,4},{4,5},{5,6},{6,7},{7,8},{8,9},{9,10},{10,1... | collective-permute-start | bytes 196616 | tf_op jit(solution)/shard_map/ppermute | solution.py:277
  51.7 0.0 collective-permute-start.16
  51.8 0.0 collective-permute-start.15
  51.8 1.5 %collective-permute-start.14 = (bf16[256,128]{1,0:T(8,128)(2,1)S(1)}, bf16[256,128]{1,0:T(8,128)(2,1)S(1)}, u32[]{:S(2)}, u32[]{:S(2)}) collective-permute-start(bf16[256,128]{1,0:T(8,128)(2,1)S(1)} %lift_rim.1), channel_id=1, source_target_pairs={{0,16},{1,0},{2,18},{3,2},{4,20},{5,4},{6,22},{7,6},{8,24},{9,8},{... | collective-permute-start | bytes 196616 | tf_op jit(solution)/shard_map/ppermute | solution.py:269
  53.2 3.4 %lift_local.1 = (bf16[2048,128]{1,0:T(8,128)(2,1)S(1)}, f32[1024,128]{1,0:T(8,128)S(1)}) custom-call(s32[5]{0:T(128)S(1)} %stack.31.flags, bf16[2048,128]{1,0:T(8,128)(2,1)S(1)} %get-tuple-element.13.cells, s32[16,128]{1,0:T(8,128)S(1)} %bitcast.24, bf16[256,128]{1,0:T(8,128)(2,1)S(1)} %coarse.1.own, bf16[256,128]{1,0:T(8,128)(2,1)S(1)} %collective-permute-done.12.left, ...), custom_call_target="tpu_custom_call" | custom-call | flops 4000000000 | bytes 1000000 | tf_op jit(solution)/shard_map/lift_local/pallas_call | solution.py:238
  56.6 0.0 collective-permute-done.18.cross
  56.6 0.0 collective-permute-done.17.left
  56.6 0.0 collective-permute-done.16.right
  56.6 0.0 collective-permute-done.15.second
  56.7 0.0 collective-permute-done.14.first
  56.7 3.6 %fine_last.1 = (bf16[2048,128]{1,0:T(8,128)(2,1)}, bf16[1024,128]{1,0:T(8,128)(2,1)}) custom-call(s32[5]{0:T(128)S(1)} %stack.31.flags, f32[1024,128]{1,0:T(8,128)S(1)} %get-tuple-element.18.pre, bf16[1024,128]{1,0:T(8,128)(2,1)S(1)} %get-tuple-element.17.edges, bf16[2048,128]{1,0:T(8,128)(2,1)S(1)} %get-tuple-element.19.nodes, s32[8,128]{1,0:T(8,128)S(1)} %bitcast.32, ...), custom_call_target="tpu_custom_call" | custom-call | flops 4000000000 | bytes 2000000 | tf_op jit(solution)/shard_map/fine_last/pallas_call | solution.py:238
  (22 shorter events, 0.1 us)
Async XLA Ops:
  1.3 1.0 %copy-start.2 = (bf16[1,1,2048,128]{3,2,1,0:T(8,128)(2,1)S(1)}, bf16[1,1,2048,128]{3,2,1,0:T(8,128)(2,1)}, u32[]{:S(2)}) copy-start(bf16[1,1,2048,128]{3,2,1,0:T(8,128)(2,1)} %param.18) | copy-start | bytes 1572868
  2.4 10.3 %copy-start.4 = (bf16[1,1,1024,128]{3,2,1,0:T(8,128)(2,1)S(1)}, bf16[1,1,1024,128]{3,2,1,0:T(8,128)(2,1)}, u32[]{:S(2)}) copy-start(bf16[1,1,1024,128]{3,2,1,0:T(8,128)(2,1)} %param.19) | copy-start | bytes 786436
  2.4 10.3 %copy-start.5 = (bf16[384,128]{1,0:T(8,128)(2,1)S(1)}, bf16[384,128]{1,0:T(8,128)(2,1)}, u32[]{:S(2)}) copy-start(bf16[384,128]{1,0:T(8,128)(2,1)} %edge_in.7) | copy-start | bytes 294916
  2.4 10.3 %copy-start.17 = (s32[1,1,1024]{2,1,0:T(1,128)S(1)}, s32[1,1,1024]{2,1,0:T(1,128)}, u32[]{:S(2)}) copy-start(s32[1,1,1024]{2,1,0:T(1,128)} %param.21) | copy-start | bytes 12292
  2.7 10.0 %copy-start.16 = (s32[1,1,1024]{2,1,0:T(1,128)S(1)}, s32[1,1,1024]{2,1,0:T(1,128)}, u32[]{:S(2)}) copy-start(s32[1,1,1024]{2,1,0:T(1,128)} %param.20) | copy-start | bytes 12292
  2.7 11.7 %collective-permute-start.4 = (bf16[256,128]{1,0:T(8,128)(2,1)S(1)}, bf16[256,128]{1,0:T(8,128)(2,1)S(1)}, u32[]{:S(2)}, u32[]{:S(2)}) collective-permute-start(bf16[256,128]{1,0:T(8,128)(2,1)S(1)} %outgoing.1), channel_id=1, source_target_pairs={{48,64},{64,48},{112,128},{128,112},{176,192},{192,176},{240,256},... | collective-permute-start | bytes 196616 | tf_op jit(solution)/shard_map/ppermute | solution.py:271
  7.9 6.6 %collective-permute-start.3 = (bf16[256,128]{1,0:T(8,128)(2,1)S(1)}, bf16[256,128]{1,0:T(8,128)(2,1)S(1)}, u32[]{:S(2)}, u32[]{:S(2)}) collective-permute-start(bf16[256,128]{1,0:T(8,128)(2,1)S(1)} %outgoing.1), channel_id=1, source_target_pairs={{0,1},{1,2},{2,3},{3,4},{4,5},{5,6},{6,7},{7,8},{8,9},{9,10},{10,1... | collective-permute-start | bytes 196616 | tf_op jit(solution)/shard_map/ppermute | solution.py:277
  11.2 4.9 %collective-permute-start.2 = (bf16[256,128]{1,0:T(8,128)(2,1)S(1)}, bf16[256,128]{1,0:T(8,128)(2,1)S(1)}, u32[]{:S(2)}, u32[]{:S(2)}) collective-permute-start(bf16[256,128]{1,0:T(8,128)(2,1)S(1)} %outgoing.1), channel_id=1, source_target_pairs={{1,0},{2,1},{3,2},{4,3},{5,4},{6,5},{7,6},{8,7},{9,8},{10,9},{11,1... | collective-permute-start | bytes 196616 | tf_op jit(solution)/shard_map/ppermute | solution.py:278
  11.2 4.9 %collective-permute-start.1 = (bf16[256,128]{1,0:T(8,128)(2,1)S(1)}, bf16[256,128]{1,0:T(8,128)(2,1)S(1)}, u32[]{:S(2)}, u32[]{:S(2)}) collective-permute-start(bf16[256,128]{1,0:T(8,128)(2,1)S(1)} %outgoing.1), channel_id=1, source_target_pairs={{16,0},{0,1},{18,2},{2,3},{20,4},{4,5},{22,6},{6,7},{24,8},{8,9},{... | collective-permute-start | bytes 196616 | tf_op jit(solution)/shard_map/ppermute | solution.py:270
  11.2 4.9 %collective-permute-start = (bf16[256,128]{1,0:T(8,128)(2,1)S(1)}, bf16[256,128]{1,0:T(8,128)(2,1)S(1)}, u32[]{:S(2)}, u32[]{:S(2)}) collective-permute-start(bf16[256,128]{1,0:T(8,128)(2,1)S(1)} %outgoing.1), channel_id=1, source_target_pairs={{0,16},{1,0},{2,18},{3,2},{4,20},{5,4},{6,22},{7,6},{8,24},{9,8},{... | collective-permute-start | bytes 196616 | tf_op jit(solution)/shard_map/ppermute | solution.py:269
  12.7 3.4 %copy-start.3 = (bf16[1,1,2048,128]{3,2,1,0:T(8,128)(2,1)S(1)}, bf16[1,1,2048,128]{3,2,1,0:T(8,128)(2,1)}, u32[]{:S(2)}) copy-start(bf16[1,1,2048,128]{3,2,1,0:T(8,128)(2,1)} %param.18) | copy-start | bytes 1572868
  12.7 3.4 %copy-start.12 = (bf16[128,128]{1,0:T(8,128)(2,1)S(1)}, bf16[128,128]{1,0:T(8,128)(2,1)}, u32[]{:S(2)}) copy-start(bf16[128,128]{1,0:T(8,128)(2,1)} %node_out.5) | copy-start | bytes 98308
  12.7 3.4 %copy-start.13 = (s32[1,1,2048]{2,1,0:T(1,128)S(1)}, s32[1,1,2048]{2,1,0:T(1,128)}, u32[]{:S(2)}) copy-start(s32[1,1,2048]{2,1,0:T(1,128)} %param.23) | copy-start | bytes 24580
  14.3 1.9 %copy-start.8 = (bf16[256,128]{1,0:T(8,128)(2,1)S(1)}, bf16[256,128]{1,0:T(8,128)(2,1)}, u32[]{:S(2)}) copy-start(bf16[256,128]{1,0:T(8,128)(2,1)} %node_in.5) | copy-start | bytes 196612
  14.3 1.8 %copy-start.11 = (bf16[128,128]{1,0:T(8,128)(2,1)S(1)}, bf16[128,128]{1,0:T(8,128)(2,1)}, u32[]{:S(2)}) copy-start(bf16[128,128]{1,0:T(8,128)(2,1)} %edge_out.5) | copy-start | bytes 98308
  19.6 3.6 %collective-permute-start.5 = (bf16[256,128]{1,0:T(8,128)(2,1)S(1)}, bf16[256,128]{1,0:T(8,128)(2,1)S(1)}, u32[]{:S(2)}, u32[]{:S(2)}) collective-permute-start(bf16[256,128]{1,0:T(8,128)(2,1)S(1)} %get-tuple-element.15), channel_id=1, source_target_pairs={{0,1},{1,2},{2,3},{3,4},{4,5},{5,6},{6,7},{7,8},{8,9},{9,10},{10,1... | collective-permute-start | bytes 196616 | tf_op jit(solution)/shard_map/ppermute | solution.py:277
  21.9 4.9 %collective-permute-start.6 = (bf16[256,128]{1,0:T(8,128)(2,1)S(1)}, bf16[256,128]{1,0:T(8,128)(2,1)S(1)}, u32[]{:S(2)}, u32[]{:S(2)}) collective-permute-start(bf16[256,128]{1,0:T(8,128)(2,1)S(1)} %get-tuple-element.16), channel_id=1, source_target_pairs={{1,0},{2,1},{3,2},{4,3},{5,4},{6,5},{7,6},{8,7},{9,8},{10,9},{11,1... | collective-permute-start | bytes 196616 | tf_op jit(solution)/shard_map/ppermute | solution.py:278
  26.8 5.8 %copy-start.6 = (bf16[256,128]{1,0:T(8,128)(2,1)S(1)}, bf16[256,128]{1,0:T(8,128)(2,1)}, u32[]{:S(2)}) copy-start(bf16[256,128]{1,0:T(8,128)(2,1)} %edge_in.5) | copy-start | bytes 196612
  26.8 5.8 %copy-start.14 = (s32[1,1,1024]{2,1,0:T(1,128)S(1)}, s32[1,1,1024]{2,1,0:T(1,128)}, u32[]{:S(2)}) copy-start(s32[1,1,1024]{2,1,0:T(1,128)} %param.24) | copy-start | bytes 12292
  26.8 5.8 %copy-start.15 = (s32[1,1,1024]{2,1,0:T(1,128)S(1)}, s32[1,1,1024]{2,1,0:T(1,128)}, u32[]{:S(2)}) copy-start(s32[1,1,1024]{2,1,0:T(1,128)} %param.25) | copy-start | bytes 12292
  26.8 8.5 %collective-permute-start.11 = (bf16[256,128]{1,0:T(8,128)(2,1)S(1)}, bf16[256,128]{1,0:T(8,128)(2,1)S(1)}, u32[]{:S(2)}, u32[]{:S(2)}) collective-permute-start(bf16[256,128]{1,0:T(8,128)(2,1)S(1)} %multiply_convert_fusion.pooled), channel_id=1, source_target_pairs={{48,64},{64,48},{112,128},{128,112},{176,192},{192,176},{240,256},... | collective-permute-start | bytes 196616 | tf_op jit(solution)/shard_map/ppermute | solution.py:271
  30.6 4.7 %collective-permute-start.10 = (bf16[256,128]{1,0:T(8,128)(2,1)S(1)}, bf16[256,128]{1,0:T(8,128)(2,1)S(1)}, u32[]{:S(2)}, u32[]{:S(2)}) collective-permute-start(bf16[256,128]{1,0:T(8,128)(2,1)S(1)} %multiply_convert_fusion.pooled), channel_id=1, source_target_pairs={{0,1},{1,2},{2,3},{3,4},{4,5},{5,6},{6,7},{7,8},{8,9},{9,10},{10,1... | collective-permute-start | bytes 196616 | tf_op jit(solution)/shard_map/ppermute | solution.py:277
  30.9 4.9 %collective-permute-start.9 = (bf16[256,128]{1,0:T(8,128)(2,1)S(1)}, bf16[256,128]{1,0:T(8,128)(2,1)S(1)}, u32[]{:S(2)}, u32[]{:S(2)}) collective-permute-start(bf16[256,128]{1,0:T(8,128)(2,1)S(1)} %multiply_convert_fusion.pooled), channel_id=1, source_target_pairs={{1,0},{2,1},{3,2},{4,3},{5,4},{6,5},{7,6},{8,7},{9,8},{10,9},{11,1... | collective-permute-start | bytes 196616 | tf_op jit(solution)/shard_map/ppermute | solution.py:278
  31.1 4.7 %collective-permute-start.8 = (bf16[256,128]{1,0:T(8,128)(2,1)S(1)}, bf16[256,128]{1,0:T(8,128)(2,1)S(1)}, u32[]{:S(2)}, u32[]{:S(2)}) collective-permute-start(bf16[256,128]{1,0:T(8,128)(2,1)S(1)} %multiply_convert_fusion.pooled), channel_id=1, source_target_pairs={{16,0},{0,1},{18,2},{2,3},{20,4},{4,5},{22,6},{6,7},{24,8},{8,9},{... | collective-permute-start | bytes 196616 | tf_op jit(solution)/shard_map/ppermute | solution.py:270
  31.1 4.7 %collective-permute-start.7 = (bf16[256,128]{1,0:T(8,128)(2,1)S(1)}, bf16[256,128]{1,0:T(8,128)(2,1)S(1)}, u32[]{:S(2)}, u32[]{:S(2)}) collective-permute-start(bf16[256,128]{1,0:T(8,128)(2,1)S(1)} %multiply_convert_fusion.pooled), channel_id=1, source_target_pairs={{0,16},{1,0},{2,18},{3,2},{4,20},{5,4},{6,22},{7,6},{8,24},{9,8},{... | collective-permute-start | bytes 196616 | tf_op jit(solution)/shard_map/ppermute | solution.py:269
  32.6 3.2 %copy-start.7 = (bf16[256,128]{1,0:T(8,128)(2,1)S(1)}, bf16[256,128]{1,0:T(8,128)(2,1)}, u32[]{:S(2)}) copy-start(bf16[256,128]{1,0:T(8,128)(2,1)} %node_in.4) | copy-start | bytes 196612
  32.6 3.2 %copy-start.9 = (bf16[128,128]{1,0:T(8,128)(2,1)S(1)}, bf16[128,128]{1,0:T(8,128)(2,1)}, u32[]{:S(2)}) copy-start(bf16[128,128]{1,0:T(8,128)(2,1)} %edge_out.4) | copy-start | bytes 98308
  32.6 3.2 %copy-start.10 = (bf16[128,128]{1,0:T(8,128)(2,1)S(1)}, bf16[128,128]{1,0:T(8,128)(2,1)}, u32[]{:S(2)}) copy-start(bf16[128,128]{1,0:T(8,128)(2,1)} %node_out.4) | copy-start | bytes 98308
  37.9 4.9 %collective-permute-start.13 = (bf16[256,128]{1,0:T(8,128)(2,1)S(1)}, bf16[256,128]{1,0:T(8,128)(2,1)S(1)}, u32[]{:S(2)}, u32[]{:S(2)}) collective-permute-start(bf16[256,128]{1,0:T(8,128)(2,1)S(1)} %coarse.1.own), channel_id=1, source_target_pairs={{1,0},{2,1},{3,2},{4,3},{5,4},{6,5},{7,6},{8,7},{9,8},{10,9},{11,1... | collective-permute-start | bytes 196616 | tf_op jit(solution)/shard_map/ppermute | solution.py:278
  37.9 4.9 %collective-permute-start.12 = (bf16[256,128]{1,0:T(8,128)(2,1)S(1)}, bf16[256,128]{1,0:T(8,128)(2,1)S(1)}, u32[]{:S(2)}, u32[]{:S(2)}) collective-permute-start(bf16[256,128]{1,0:T(8,128)(2,1)S(1)} %coarse.1.own), channel_id=1, source_target_pairs={{0,1},{1,2},{2,3},{3,4},{4,5},{5,6},{6,7},{7,8},{8,9},{9,10},{10,1... | collective-permute-start | bytes 196616 | tf_op jit(solution)/shard_map/ppermute | solution.py:277
  40.9 1.9 %copy-start = (bf16[256,128]{1,0:T(8,128)(2,1)S(1)}, bf16[256,128]{1,0:T(8,128)(2,1)}, u32[]{:S(2)}) copy-start(bf16[256,128]{1,0:T(8,128)(2,1)} %first.7) | copy-start | bytes 196612
  40.9 2.0 %copy-start.1 = (bf16[128,128]{1,0:T(8,128)(2,1)S(1)}, bf16[128,128]{1,0:T(8,128)(2,1)}, u32[]{:S(2)}) copy-start(bf16[128,128]{1,0:T(8,128)(2,1)} %second.3) | copy-start | bytes 98308
  43.4 13.2 %collective-permute-start.18 = (bf16[256,128]{1,0:T(8,128)(2,1)S(1)}, bf16[256,128]{1,0:T(8,128)(2,1)S(1)}, u32[]{:S(2)}, u32[]{:S(2)}) collective-permute-start(bf16[256,128]{1,0:T(8,128)(2,1)S(1)} %lift_rim.1), channel_id=1, source_target_pairs={{48,64},{64,48},{112,128},{128,112},{176,192},{192,176},{240,256},... | collective-permute-start | bytes 196616 | tf_op jit(solution)/shard_map/ppermute | solution.py:271
  48.5 8.1 %collective-permute-start.17 = (bf16[256,128]{1,0:T(8,128)(2,1)S(1)}, bf16[256,128]{1,0:T(8,128)(2,1)S(1)}, u32[]{:S(2)}, u32[]{:S(2)}) collective-permute-start(bf16[256,128]{1,0:T(8,128)(2,1)S(1)} %lift_rim.1), channel_id=1, source_target_pairs={{0,1},{1,2},{2,3},{3,4},{4,5},{5,6},{6,7},{7,8},{8,9},{9,10},{10,1... | collective-permute-start | bytes 196616 | tf_op jit(solution)/shard_map/ppermute | solution.py:277
  51.7 4.9 %collective-permute-start.16 = (bf16[256,128]{1,0:T(8,128)(2,1)S(1)}, bf16[256,128]{1,0:T(8,128)(2,1)S(1)}, u32[]{:S(2)}, u32[]{:S(2)}) collective-permute-start(bf16[256,128]{1,0:T(8,128)(2,1)S(1)} %lift_rim.1), channel_id=1, source_target_pairs={{1,0},{2,1},{3,2},{4,3},{5,4},{6,5},{7,6},{8,7},{9,8},{10,9},{11,1... | collective-permute-start | bytes 196616 | tf_op jit(solution)/shard_map/ppermute | solution.py:278
  51.8 4.9 %collective-permute-start.15 = (bf16[256,128]{1,0:T(8,128)(2,1)S(1)}, bf16[256,128]{1,0:T(8,128)(2,1)S(1)}, u32[]{:S(2)}, u32[]{:S(2)}) collective-permute-start(bf16[256,128]{1,0:T(8,128)(2,1)S(1)} %lift_rim.1), channel_id=1, source_target_pairs={{16,0},{0,1},{18,2},{2,3},{20,4},{4,5},{22,6},{6,7},{24,8},{8,9},{... | collective-permute-start | bytes 196616 | tf_op jit(solution)/shard_map/ppermute | solution.py:270
  51.8 4.9 %collective-permute-start.14 = (bf16[256,128]{1,0:T(8,128)(2,1)S(1)}, bf16[256,128]{1,0:T(8,128)(2,1)S(1)}, u32[]{:S(2)}, u32[]{:S(2)}) collective-permute-start(bf16[256,128]{1,0:T(8,128)(2,1)S(1)} %lift_rim.1), channel_id=1, source_target_pairs={{0,16},{1,0},{2,18},{3,2},{4,20},{5,4},{6,22},{7,6},{8,24},{9,8},{... | collective-permute-start | bytes 196616 | tf_op jit(solution)/shard_map/ppermute | solution.py:269

commit v4 on v3

--- a/solution.py
+++ b/solution.py
@@ -163,7 +163,7 @@
 
 
 def fine_last_kernel(
-    flags, pre, edges, nodes, senders, receivers, first, second, right, left, cross,
+    flags, pre, edges, nodes, senders, receivers, first, second, cross, right, left,
     edge_in, edge_out, node_in, node_out,
     new_nodes, new_edges, wide, sums, held_nodes, held_edges, sent,
 ):
@@ -342,7 +342,7 @@
     )
     node_out, edge_out = call(
         fine_last_kernel, [shape(CELLS, LATENT), shape(EDGES, LATENT)], [SMEM] + [VMEM] * 14,
-        (flags, pre, edges_one, cells_two, senders, receivers, *halo, *weights),
+        (flags, pre, edges_one, cells_two, senders, receivers, *[halo[k] for k in (0, 1, 4, 2, 3)], *weights),
         "fine_last", cost(4_000_000_000, 2_000_000),
         scratch + [
             pltpu.VMEM((CELLS, LATENT), BF16), pltpu.VMEM((EDGES, LATENT), BF16),

time: 60.8 us -> 60.5 us (level)
  no operation moved by 1% of the time
where the time goes in v4:
time: 60.5 us; the launch traced here: 60.2 us
  starting transfers between devices  30.6 us (51%)
  Pallas kernels  17 us (28%)
  waiting for transfers between devices  9.55 us (16%)
  local copies, waits for them, and re-layouts  1.21 us (2%)
  between operations  1.11 us (2%)
  other arithmetic  0.72 us (1%)
    pallas_call x9, Pallas kernels, call(): pl.pallas_call(kernel, out_shape=outs, in_specs=ins, out_specs=where or j...  17 us
    ppermute x3, starting transfers between devices, exchange(): cross = lax.ppermute(block, 'px', crossing)  14 us
    ppermute x5, starting transfers between devices, exchange_row(): lax.ppermute(to_right, 'py', [(i, (i + 1) % count) for i in range(count)])  11.9 us
    ppermute x5, waiting for transfers between devices, exchange_row(): lax.ppermute(to_left, 'py', [((i + 1) % count, i) for i in range(count)])  6.41 us
    ppermute x3, starting transfers between devices, exchange(): first = lax.ppermute(block, ('px', 'py'), ring)  4.38 us
    ppermute x3, waiting for transfers between devices, exchange(): cross = lax.ppermute(block, 'px', crossing)  1.79 us
    ppermute x5, waiting for transfers between devices, exchange_row(): lax.ppermute(to_right, 'py', [(i, (i + 1) % count) for i in range(count)])  1.34 us
  transfers between devices with their start and end apart: 19, of which 6 were waited for; matrix products, arithmetic and copies ran while one was open for 0% of the time, Pallas kernels for 12%

profile of v4, /device:TPU:223, one launch (start us, length us, event | category | flops | bytes accessed | tf_op | source)
XLA Modules:
  0.0 60.2 jit_solution(3624241877532205564)
XLA Ops:
  0.6 0.7 %broadcast_add_fusion = s32[1,1,256]{2,1,0:T(1,128)S(1)} fusion(s32[1,1,256]{2,1,0:T(1,128)} %param.22), kind=kLoop, calls=%fused_computation.1 | loop fusion | flops 256 | bytes 2048 | tf_op jit(solution)/shard_map/add | solution.py:289
  1.3 1.0 %copy-done.2 = bf16[1,1,2048,128]{3,2,1,0:T(8,128)(2,1)S(1)} copy-done((bf16[1,1,2048,128]{3,2,1,0:T(8,128)(2,1)S(1)}, bf16[1,1,2048,128]{3,2,1,0:T(8,128)(2,1)}, u32[]{:S(2)}) %copy-start.2) | copy-done | bytes 524312
  2.4 0.4 outgoing.1
  2.7 0.0 copy-start.16
  2.7 5.1 %collective-permute-start.4 = (bf16[256,128]{1,0:T(8,128)(2,1)S(1)}, bf16[256,128]{1,0:T(8,128)(2,1)S(1)}, u32[]{:S(2)}, u32[]{:S(2)}) collective-permute-start(bf16[256,128]{1,0:T(8,128)(2,1)S(1)} %outgoing.1), channel_id=1, source_target_pairs={{48,64},{64,48},{112,128},{128,112},{176,192},{192,176},{240,256},... | collective-permute-start | bytes 196616 | tf_op jit(solution)/shard_map/ppermute | solution.py:271
  7.9 3.4 %collective-permute-start.3 = (bf16[256,128]{1,0:T(8,128)(2,1)S(1)}, bf16[256,128]{1,0:T(8,128)(2,1)S(1)}, u32[]{:S(2)}, u32[]{:S(2)}) collective-permute-start(bf16[256,128]{1,0:T(8,128)(2,1)S(1)} %outgoing.1), channel_id=1, source_target_pairs={{0,1},{1,2},{2,3},{3,4},{4,5},{5,6},{6,7},{7,8},{8,9},{9,10},{10,1... | collective-permute-start | bytes 196616 | tf_op jit(solution)/shard_map/ppermute | solution.py:277
  11.2 0.0 collective-permute-start.2
  11.2 0.0 collective-permute-start.1
  11.2 1.5 %collective-permute-start = (bf16[256,128]{1,0:T(8,128)(2,1)S(1)}, bf16[256,128]{1,0:T(8,128)(2,1)S(1)}, u32[]{:S(2)}, u32[]{:S(2)}) collective-permute-start(bf16[256,128]{1,0:T(8,128)(2,1)S(1)} %outgoing.1), channel_id=1, source_target_pairs={{0,16},{1,0},{2,18},{3,2},{4,20},{5,4},{6,22},{7,6},{8,24},{9,8},{... | collective-permute-start | bytes 196616 | tf_op jit(solution)/shard_map/ppermute | solution.py:269
  12.7 0.0 copy-done.4
  12.7 0.0 copy-done.5
  12.7 0.0 copy-done.17
  12.7 0.0 copy-start.3
  12.7 0.0 copy-start.12
  12.7 0.0 copy-start.13
  12.7 1.6 %fine_local.1.pre = f32[1024,128]{1,0:T(8,128)S(1)} custom-call(bf16[2048,128]{1,0:T(8,128)(2,1)S(1)} %bitcast.18, bf16[1024,128]{1,0:T(8,128)(2,1)S(1)} %bitcast.20, s32[8,128]{1,0:T(8,128)S(1)} %bitcast.29, s32[8,128]{1,0:T(8,128)S(1)} %bitcast.33, bf16[384,128]{1,0:T(8,128)(2,1)S(1)} %copy-done.5), custom_call_target="tpu_custom_call" | custom-call | flops 4000000000 | bytes 2000000 | tf_op jit(solution)/shard_map/fine_local/pallas_call | solution.py:238
  14.3 0.0 copy-start.8
  14.3 0.0 copy-start.11
  14.4 0.1 stack.31.flags
  14.5 0.0 collective-permute-done.4.cross
  14.5 0.0 collective-permute-done.3.left
  14.5 1.7 %collective-permute-done.2.right = bf16[256,128]{1,0:T(8,128)(2,1)S(1)} collective-permute-done((bf16[256,128]{1,0:T(8,128)(2,1)S(1)}, bf16[256,128]{1,0:T(8,128)(2,1)S(1)}, u32[]{:S(2)}, u32[]{:S(2)}) %collective-permute-start.2) | collective-permute-done | bytes 65568 | tf_op jit(solution)/shard_map/ppermute | solution.py:278
  16.1 0.0 collective-permute-done.1.second
  16.1 0.0 collective-permute-done.first
  16.1 0.0 copy-done.3
  16.2 3.4 %fine_pool.1 = (bf16[2048,128]{1,0:T(8,128)(2,1)S(1)}, bf16[1024,128]{1,0:T(8,128)(2,1)S(1)}, f32[256,128]{1,0:T(8,128)S(1)}, bf16[256,128]{1,0:T(8,128)(2,1)S(1)}, bf16[256,128]{1,0:T(8,128)(2,1)S(1)}) custom-call(s32[5]{0:T(128)S(1)} %stack.31.flags, f32[1024,128]{1,0:T(8,128)S(1)} %fine_local.1.pre, bf16[1024,128]{1,0:T(8,128)(2,1)S(1)} %bitcast.21, ...), custom_call_target="tpu_custom_call" | custom-call | flops 4000000000 | bytes 2000000 | tf_op jit(solution)/shard_map/fine_pool/pallas_call | solution.py:238
  19.6 2.3 %collective-permute-start.5 = (bf16[256,128]{1,0:T(8,128)(2,1)S(1)}, bf16[256,128]{1,0:T(8,128)(2,1)S(1)}, u32[]{:S(2)}, u32[]{:S(2)}) collective-permute-start(bf16[256,128]{1,0:T(8,128)(2,1)S(1)} %get-tuple-element.15), channel_id=1, source_target_pairs={{0,1},{1,2},{2,3},{3,4},{4,5},{5,6},{6,7},{7,8},{8,9},{9,10},{10,1... | collective-permute-start | bytes 196616 | tf_op jit(solution)/shard_map/ppermute | solution.py:277
  21.9 0.0 collective-permute-start.6
  21.9 1.3 %collective-permute-done.5 = bf16[256,128]{1,0:T(8,128)(2,1)S(1)} collective-permute-done((bf16[256,128]{1,0:T(8,128)(2,1)S(1)}, bf16[256,128]{1,0:T(8,128)(2,1)S(1)}, u32[]{:S(2)}, u32[]{:S(2)}) %collective-permute-start.5) | collective-permute-done | bytes 65568 | tf_op jit(solution)/shard_map/ppermute | solution.py:277
  23.2 3.6 %collective-permute-done.6 = bf16[256,128]{1,0:T(8,128)(2,1)S(1)} collective-permute-done((bf16[256,128]{1,0:T(8,128)(2,1)S(1)}, bf16[256,128]{1,0:T(8,128)(2,1)S(1)}, u32[]{:S(2)}, u32[]{:S(2)}) %collective-permute-start.6) | collective-permute-done | bytes 65568 | tf_op jit(solution)/shard_map/ppermute | solution.py:278
  26.8 3.8 %collective-permute-start.11 = (bf16[256,128]{1,0:T(8,128)(2,1)S(1)}, bf16[256,128]{1,0:T(8,128)(2,1)S(1)}, u32[]{:S(2)}, u32[]{:S(2)}) collective-permute-start(bf16[256,128]{1,0:T(8,128)(2,1)S(1)} %multiply_convert_fusion.pooled), channel_id=1, source_target_pairs={{48,64},{64,48},{112,128},{128,112},{176,192},{192,176},{240,256},... | collective-permute-start | bytes 196616 | tf_op jit(solution)/shard_map/ppermute | solution.py:271
  30.6 0.3 collective-permute-start.10
  30.9 0.2 collective-permute-start.9
  31.1 0.0 collective-permute-start.8
  31.1 1.5 %collective-permute-start.7 = (bf16[256,128]{1,0:T(8,128)(2,1)S(1)}, bf16[256,128]{1,0:T(8,128)(2,1)S(1)}, u32[]{:S(2)}, u32[]{:S(2)}) collective-permute-start(bf16[256,128]{1,0:T(8,128)(2,1)S(1)} %multiply_convert_fusion.pooled), channel_id=1, source_target_pairs={{0,16},{1,0},{2,18},{3,2},{4,20},{5,4},{6,22},{7,6},{8,24},{9,8},{... | collective-permute-start | bytes 196616 | tf_op jit(solution)/shard_map/ppermute | solution.py:269
  32.6 0.0 copy-done.14
  32.6 0.0 copy-start.9
  32.6 0.0 copy-start.10
  32.6 0.8 %coarse_local.1.pre = f32[1024,128]{1,0:T(8,128)S(1)} custom-call(bf16[256,128]{1,0:T(8,128)(2,1)S(1)} %multiply_convert_fusion.pooled, s32[8,128]{1,0:T(8,128)S(1)} %bitcast.25, s32[8,128]{1,0:T(8,128)S(1)} %bitcast.27, bf16[256,128]{1,0:T(8,128)(2,1)S(1)} %copy-done.6), custom_call_target="tpu_custom_call" | custom-call | flops 1000000000 | bytes 1000000 | tf_op jit(solution)/shard_map/coarse_local/pallas_call | solution.py:238
  33.5 1.8 %collective-permute-done.11.cross = bf16[256,128]{1,0:T(8,128)(2,1)S(1)} collective-permute-done((bf16[256,128]{1,0:T(8,128)(2,1)S(1)}, bf16[256,128]{1,0:T(8,128)(2,1)S(1)}, u32[]{:S(2)}, u32[]{:S(2)}) %collective-permute-start.11) | collective-permute-done | bytes 65568 | tf_op jit(solution)/shard_map/ppermute | solution.py:271
  35.3 0.0 collective-permute-done.10.left
  35.3 0.5 collective-permute-done.9.right
  35.8 0.0 collective-permute-done.8.second
  35.8 0.0 collective-permute-done.7.first
  35.8 2.0 %coarse.1.own = bf16[256,128]{1,0:T(8,128)(2,1)S(1)} custom-call(s32[5]{0:T(128)S(1)} %stack.31.flags, f32[1024,128]{1,0:T(8,128)S(1)} %coarse_local.1.pre, bf16[256,128]{1,0:T(8,128)(2,1)S(1)} %multiply_convert_fusion.pooled, s32[8,128]{1,0:T(8,128)S(1)} %bitcast.26, s32[8,128]{1,0:T(8,128)S(1)} %bitcast.28, ...), custom_call_target="tpu_custom_call" | custom-call | flops 2000000000 | bytes 1000000 | tf_op jit(solution)/shard_map/coarse/pallas_call | solution.py:238
  37.9 0.0 collective-permute-start.13
  37.9 2.9 %collective-permute-start.12 = (bf16[256,128]{1,0:T(8,128)(2,1)S(1)}, bf16[256,128]{1,0:T(8,128)(2,1)S(1)}, u32[]{:S(2)}, u32[]{:S(2)}) collective-permute-start(bf16[256,128]{1,0:T(8,128)(2,1)S(1)} %coarse.1.own), channel_id=1, source_target_pairs={{0,1},{1,2},{2,3},{3,4},{4,5},{5,6},{6,7},{7,8},{8,9},{9,10},{10,1... | collective-permute-start | bytes 196616 | tf_op jit(solution)/shard_map/ppermute | solution.py:277
  40.9 1.3 %rim.1 = (bf16[256,128]{1,0:T(8,128)(2,1)S(1)}, s32[256,128]{1,0:T(8,128)S(1)}) custom-call(s32[5]{0:T(128)S(1)} %stack.31.flags, bf16[2048,128]{1,0:T(8,128)(2,1)S(1)} %get-tuple-element.13.cells, s32[16,128]{1,0:T(8,128)S(1)} %bitcast.23, s32[2,128]{1,0:T(2,128)S(1)} %bitcast.16), custom_call_target="tpu_custom_call" | custom-call | flops 1000000000 | bytes 1000000 | tf_op jit(solution)/shard_map/rim/pallas_call | solution.py:238
  42.2 0.6 %collective-permute-done.13.right = bf16[256,128]{1,0:T(8,128)(2,1)S(1)} collective-permute-done((bf16[256,128]{1,0:T(8,128)(2,1)S(1)}, bf16[256,128]{1,0:T(8,128)(2,1)S(1)}, u32[]{:S(2)}, u32[]{:S(2)}) %collective-permute-start.13) | collective-permute-done | bytes 65568 | tf_op jit(solution)/shard_map/ppermute | solution.py:278
  42.8 0.0 collective-permute-done.12.left
  42.8 0.0 copy-done
  42.8 0.6 lift_rim.1
  43.4 3.0 %collective-permute-start.18 = (bf16[256,128]{1,0:T(8,128)(2,1)S(1)}, bf16[256,128]{1,0:T(8,128)(2,1)S(1)}, u32[]{:S(2)}, u32[]{:S(2)}) collective-permute-start(bf16[256,128]{1,0:T(8,128)(2,1)S(1)} %lift_rim.1), channel_id=1, source_target_pairs={{0,1},{1,2},{2,3},{3,4},{4,5},{5,6},{6,7},{7,8},{8,9},{9,10},{10,1... | collective-permute-start | bytes 196616 | tf_op jit(solution)/shard_map/ppermute | solution.py:277
  46.3 0.0 collective-permute-start.17
  46.3 5.1 %collective-permute-start.16 = (bf16[256,128]{1,0:T(8,128)(2,1)S(1)}, bf16[256,128]{1,0:T(8,128)(2,1)S(1)}, u32[]{:S(2)}, u32[]{:S(2)}) collective-permute-start(bf16[256,128]{1,0:T(8,128)(2,1)S(1)} %lift_rim.1), channel_id=1, source_target_pairs={{48,64},{64,48},{112,128},{128,112},{176,192},{192,176},{240,256},... | collective-permute-start | bytes 196616 | tf_op jit(solution)/shard_map/ppermute | solution.py:271
  51.5 0.0 collective-permute-start.15
  51.5 1.5 %collective-permute-start.14 = (bf16[256,128]{1,0:T(8,128)(2,1)S(1)}, bf16[256,128]{1,0:T(8,128)(2,1)S(1)}, u32[]{:S(2)}, u32[]{:S(2)}) collective-permute-start(bf16[256,128]{1,0:T(8,128)(2,1)S(1)} %lift_rim.1), channel_id=1, source_target_pairs={{0,16},{1,0},{2,18},{3,2},{4,20},{5,4},{6,22},{7,6},{8,24},{9,8},{... | collective-permute-start | bytes 196616 | tf_op jit(solution)/shard_map/ppermute | solution.py:269
  52.9 3.4 %lift_local.1 = (bf16[2048,128]{1,0:T(8,128)(2,1)S(1)}, f32[1024,128]{1,0:T(8,128)S(1)}) custom-call(s32[5]{0:T(128)S(1)} %stack.31.flags, bf16[2048,128]{1,0:T(8,128)(2,1)S(1)} %get-tuple-element.13.cells, s32[16,128]{1,0:T(8,128)S(1)} %bitcast.24, bf16[256,128]{1,0:T(8,128)(2,1)S(1)} %coarse.1.own, bf16[256,128]{1,0:T(8,128)(2,1)S(1)} %collective-permute-done.12.left, ...), custom_call_target="tpu_custom_call" | custom-call | flops 4000000000 | bytes 1000000 | tf_op jit(solution)/shard_map/lift_local/pallas_call | solution.py:238
  56.3 0.0 collective-permute-done.18.left
  56.3 0.0 collective-permute-done.17.right
  56.3 0.0 collective-permute-done.16.cross
  56.3 0.0 collective-permute-done.15.second
  56.4 0.0 collective-permute-done.14.first
  56.4 3.6 %fine_last.1 = (bf16[2048,128]{1,0:T(8,128)(2,1)}, bf16[1024,128]{1,0:T(8,128)(2,1)}) custom-call(s32[5]{0:T(128)S(1)} %stack.31.flags, f32[1024,128]{1,0:T(8,128)S(1)} %get-tuple-element.18.pre, bf16[1024,128]{1,0:T(8,128)(2,1)S(1)} %get-tuple-element.17.edges, bf16[2048,128]{1,0:T(8,128)(2,1)S(1)} %get-tuple-element.19.nodes, s32[8,128]{1,0:T(8,128)S(1)} %bitcast.32, ...), custom_call_target="tpu_custom_call" | custom-call | flops 4000000000 | bytes 2000000 | tf_op jit(solution)/shard_map/fine_last/pallas_call | solution.py:238
  (22 shorter events, 0.1 us)
Async XLA Ops:
  1.3 1.0 %copy-start.2 = (bf16[1,1,2048,128]{3,2,1,0:T(8,128)(2,1)S(1)}, bf16[1,1,2048,128]{3,2,1,0:T(8,128)(2,1)}, u32[]{:S(2)}) copy-start(bf16[1,1,2048,128]{3,2,1,0:T(8,128)(2,1)} %param.18) | copy-start | bytes 1572868
  2.4 10.3 %copy-start.4 = (bf16[1,1,1024,128]{3,2,1,0:T(8,128)(2,1)S(1)}, bf16[1,1,1024,128]{3,2,1,0:T(8,128)(2,1)}, u32[]{:S(2)}) copy-start(bf16[1,1,1024,128]{3,2,1,0:T(8,128)(2,1)} %param.19) | copy-start | bytes 786436
  2.4 10.3 %copy-start.5 = (bf16[384,128]{1,0:T(8,128)(2,1)S(1)}, bf16[384,128]{1,0:T(8,128)(2,1)}, u32[]{:S(2)}) copy-start(bf16[384,128]{1,0:T(8,128)(2,1)} %edge_in.7) | copy-start | bytes 294916
  2.4 10.3 %copy-start.17 = (s32[1,1,1024]{2,1,0:T(1,128)S(1)}, s32[1,1,1024]{2,1,0:T(1,128)}, u32[]{:S(2)}) copy-start(s32[1,1,1024]{2,1,0:T(1,128)} %param.21) | copy-start | bytes 12292
  2.7 10.0 %copy-start.16 = (s32[1,1,1024]{2,1,0:T(1,128)S(1)}, s32[1,1,1024]{2,1,0:T(1,128)}, u32[]{:S(2)}) copy-start(s32[1,1,1024]{2,1,0:T(1,128)} %param.20) | copy-start | bytes 12292
  2.7 11.7 %collective-permute-start.4 = (bf16[256,128]{1,0:T(8,128)(2,1)S(1)}, bf16[256,128]{1,0:T(8,128)(2,1)S(1)}, u32[]{:S(2)}, u32[]{:S(2)}) collective-permute-start(bf16[256,128]{1,0:T(8,128)(2,1)S(1)} %outgoing.1), channel_id=1, source_target_pairs={{48,64},{64,48},{112,128},{128,112},{176,192},{192,176},{240,256},... | collective-permute-start | bytes 196616 | tf_op jit(solution)/shard_map/ppermute | solution.py:271
  7.9 6.6 %collective-permute-start.3 = (bf16[256,128]{1,0:T(8,128)(2,1)S(1)}, bf16[256,128]{1,0:T(8,128)(2,1)S(1)}, u32[]{:S(2)}, u32[]{:S(2)}) collective-permute-start(bf16[256,128]{1,0:T(8,128)(2,1)S(1)} %outgoing.1), channel_id=1, source_target_pairs={{0,1},{1,2},{2,3},{3,4},{4,5},{5,6},{6,7},{7,8},{8,9},{9,10},{10,1... | collective-permute-start | bytes 196616 | tf_op jit(solution)/shard_map/ppermute | solution.py:277
  11.2 4.9 %collective-permute-start.2 = (bf16[256,128]{1,0:T(8,128)(2,1)S(1)}, bf16[256,128]{1,0:T(8,128)(2,1)S(1)}, u32[]{:S(2)}, u32[]{:S(2)}) collective-permute-start(bf16[256,128]{1,0:T(8,128)(2,1)S(1)} %outgoing.1), channel_id=1, source_target_pairs={{1,0},{2,1},{3,2},{4,3},{5,4},{6,5},{7,6},{8,7},{9,8},{10,9},{11,1... | collective-permute-start | bytes 196616 | tf_op jit(solution)/shard_map/ppermute | solution.py:278
  11.2 4.9 %collective-permute-start.1 = (bf16[256,128]{1,0:T(8,128)(2,1)S(1)}, bf16[256,128]{1,0:T(8,128)(2,1)S(1)}, u32[]{:S(2)}, u32[]{:S(2)}) collective-permute-start(bf16[256,128]{1,0:T(8,128)(2,1)S(1)} %outgoing.1), channel_id=1, source_target_pairs={{16,0},{0,1},{18,2},{2,3},{20,4},{4,5},{22,6},{6,7},{24,8},{8,9},{... | collective-permute-start | bytes 196616 | tf_op jit(solution)/shard_map/ppermute | solution.py:270
  11.2 4.9 %collective-permute-start = (bf16[256,128]{1,0:T(8,128)(2,1)S(1)}, bf16[256,128]{1,0:T(8,128)(2,1)S(1)}, u32[]{:S(2)}, u32[]{:S(2)}) collective-permute-start(bf16[256,128]{1,0:T(8,128)(2,1)S(1)} %outgoing.1), channel_id=1, source_target_pairs={{0,16},{1,0},{2,18},{3,2},{4,20},{5,4},{6,22},{7,6},{8,24},{9,8},{... | collective-permute-start | bytes 196616 | tf_op jit(solution)/shard_map/ppermute | solution.py:269
  12.7 3.4 %copy-start.3 = (bf16[1,1,2048,128]{3,2,1,0:T(8,128)(2,1)S(1)}, bf16[1,1,2048,128]{3,2,1,0:T(8,128)(2,1)}, u32[]{:S(2)}) copy-start(bf16[1,1,2048,128]{3,2,1,0:T(8,128)(2,1)} %param.18) | copy-start | bytes 1572868
  12.7 3.4 %copy-start.12 = (bf16[128,128]{1,0:T(8,128)(2,1)S(1)}, bf16[128,128]{1,0:T(8,128)(2,1)}, u32[]{:S(2)}) copy-start(bf16[128,128]{1,0:T(8,128)(2,1)} %node_out.5) | copy-start | bytes 98308
  12.7 3.4 %copy-start.13 = (s32[1,1,2048]{2,1,0:T(1,128)S(1)}, s32[1,1,2048]{2,1,0:T(1,128)}, u32[]{:S(2)}) copy-start(s32[1,1,2048]{2,1,0:T(1,128)} %param.23) | copy-start | bytes 24580
  14.3 1.9 %copy-start.8 = (bf16[256,128]{1,0:T(8,128)(2,1)S(1)}, bf16[256,128]{1,0:T(8,128)(2,1)}, u32[]{:S(2)}) copy-start(bf16[256,128]{1,0:T(8,128)(2,1)} %node_in.5) | copy-start | bytes 196612
  14.3 1.8 %copy-start.11 = (bf16[128,128]{1,0:T(8,128)(2,1)S(1)}, bf16[128,128]{1,0:T(8,128)(2,1)}, u32[]{:S(2)}) copy-start(bf16[128,128]{1,0:T(8,128)(2,1)} %edge_out.5) | copy-start | bytes 98308
  19.6 3.6 %collective-permute-start.5 = (bf16[256,128]{1,0:T(8,128)(2,1)S(1)}, bf16[256,128]{1,0:T(8,128)(2,1)S(1)}, u32[]{:S(2)}, u32[]{:S(2)}) collective-permute-start(bf16[256,128]{1,0:T(8,128)(2,1)S(1)} %get-tuple-element.15), channel_id=1, source_target_pairs={{0,1},{1,2},{2,3},{3,4},{4,5},{5,6},{6,7},{7,8},{8,9},{9,10},{10,1... | collective-permute-start | bytes 196616 | tf_op jit(solution)/shard_map/ppermute | solution.py:277
  21.9 4.9 %collective-permute-start.6 = (bf16[256,128]{1,0:T(8,128)(2,1)S(1)}, bf16[256,128]{1,0:T(8,128)(2,1)S(1)}, u32[]{:S(2)}, u32[]{:S(2)}) collective-permute-start(bf16[256,128]{1,0:T(8,128)(2,1)S(1)} %get-tuple-element.16), channel_id=1, source_target_pairs={{1,0},{2,1},{3,2},{4,3},{5,4},{6,5},{7,6},{8,7},{9,8},{10,9},{11,1... | collective-permute-start | bytes 196616 | tf_op jit(solution)/shard_map/ppermute | solution.py:278
  26.8 5.8 %copy-start.6 = (bf16[256,128]{1,0:T(8,128)(2,1)S(1)}, bf16[256,128]{1,0:T(8,128)(2,1)}, u32[]{:S(2)}) copy-start(bf16[256,128]{1,0:T(8,128)(2,1)} %edge_in.5) | copy-start | bytes 196612
  26.8 5.8 %copy-start.14 = (s32[1,1,1024]{2,1,0:T(1,128)S(1)}, s32[1,1,1024]{2,1,0:T(1,128)}, u32[]{:S(2)}) copy-start(s32[1,1,1024]{2,1,0:T(1,128)} %param.24) | copy-start | bytes 12292
  26.8 5.8 %copy-start.15 = (s32[1,1,1024]{2,1,0:T(1,128)S(1)}, s32[1,1,1024]{2,1,0:T(1,128)}, u32[]{:S(2)}) copy-start(s32[1,1,1024]{2,1,0:T(1,128)} %param.25) | copy-start | bytes 12292
  26.8 8.5 %collective-permute-start.11 = (bf16[256,128]{1,0:T(8,128)(2,1)S(1)}, bf16[256,128]{1,0:T(8,128)(2,1)S(1)}, u32[]{:S(2)}, u32[]{:S(2)}) collective-permute-start(bf16[256,128]{1,0:T(8,128)(2,1)S(1)} %multiply_convert_fusion.pooled), channel_id=1, source_target_pairs={{48,64},{64,48},{112,128},{128,112},{176,192},{192,176},{240,256},... | collective-permute-start | bytes 196616 | tf_op jit(solution)/shard_map/ppermute | solution.py:271
  30.6 4.7 %collective-permute-start.10 = (bf16[256,128]{1,0:T(8,128)(2,1)S(1)}, bf16[256,128]{1,0:T(8,128)(2,1)S(1)}, u32[]{:S(2)}, u32[]{:S(2)}) collective-permute-start(bf16[256,128]{1,0:T(8,128)(2,1)S(1)} %multiply_convert_fusion.pooled), channel_id=1, source_target_pairs={{0,1},{1,2},{2,3},{3,4},{4,5},{5,6},{6,7},{7,8},{8,9},{9,10},{10,1... | collective-permute-start | bytes 196616 | tf_op jit(solution)/shard_map/ppermute | solution.py:277
  30.9 4.9 %collective-permute-start.9 = (bf16[256,128]{1,0:T(8,128)(2,1)S(1)}, bf16[256,128]{1,0:T(8,128)(2,1)S(1)}, u32[]{:S(2)}, u32[]{:S(2)}) collective-permute-start(bf16[256,128]{1,0:T(8,128)(2,1)S(1)} %multiply_convert_fusion.pooled), channel_id=1, source_target_pairs={{1,0},{2,1},{3,2},{4,3},{5,4},{6,5},{7,6},{8,7},{9,8},{10,9},{11,1... | collective-permute-start | bytes 196616 | tf_op jit(solution)/shard_map/ppermute | solution.py:278
  31.1 4.7 %collective-permute-start.8 = (bf16[256,128]{1,0:T(8,128)(2,1)S(1)}, bf16[256,128]{1,0:T(8,128)(2,1)S(1)}, u32[]{:S(2)}, u32[]{:S(2)}) collective-permute-start(bf16[256,128]{1,0:T(8,128)(2,1)S(1)} %multiply_convert_fusion.pooled), channel_id=1, source_target_pairs={{16,0},{0,1},{18,2},{2,3},{20,4},{4,5},{22,6},{6,7},{24,8},{8,9},{... | collective-permute-start | bytes 196616 | tf_op jit(solution)/shard_map/ppermute | solution.py:270
  31.1 4.7 %collective-permute-start.7 = (bf16[256,128]{1,0:T(8,128)(2,1)S(1)}, bf16[256,128]{1,0:T(8,128)(2,1)S(1)}, u32[]{:S(2)}, u32[]{:S(2)}) collective-permute-start(bf16[256,128]{1,0:T(8,128)(2,1)S(1)} %multiply_convert_fusion.pooled), channel_id=1, source_target_pairs={{0,16},{1,0},{2,18},{3,2},{4,20},{5,4},{6,22},{7,6},{8,24},{9,8},{... | collective-permute-start | bytes 196616 | tf_op jit(solution)/shard_map/ppermute | solution.py:269
  32.6 3.2 %copy-start.7 = (bf16[256,128]{1,0:T(8,128)(2,1)S(1)}, bf16[256,128]{1,0:T(8,128)(2,1)}, u32[]{:S(2)}) copy-start(bf16[256,128]{1,0:T(8,128)(2,1)} %node_in.4) | copy-start | bytes 196612
  32.6 3.2 %copy-start.9 = (bf16[128,128]{1,0:T(8,128)(2,1)S(1)}, bf16[128,128]{1,0:T(8,128)(2,1)}, u32[]{:S(2)}) copy-start(bf16[128,128]{1,0:T(8,128)(2,1)} %edge_out.4) | copy-start | bytes 98308
  32.6 3.2 %copy-start.10 = (bf16[128,128]{1,0:T(8,128)(2,1)S(1)}, bf16[128,128]{1,0:T(8,128)(2,1)}, u32[]{:S(2)}) copy-start(bf16[128,128]{1,0:T(8,128)(2,1)} %node_out.4) | copy-start | bytes 98308
  37.9 4.9 %collective-permute-start.13 = (bf16[256,128]{1,0:T(8,128)(2,1)S(1)}, bf16[256,128]{1,0:T(8,128)(2,1)S(1)}, u32[]{:S(2)}, u32[]{:S(2)}) collective-permute-start(bf16[256,128]{1,0:T(8,128)(2,1)S(1)} %coarse.1.own), channel_id=1, source_target_pairs={{1,0},{2,1},{3,2},{4,3},{5,4},{6,5},{7,6},{8,7},{9,8},{10,9},{11,1... | collective-permute-start | bytes 196616 | tf_op jit(solution)/shard_map/ppermute | solution.py:278
  37.9 4.9 %collective-permute-start.12 = (bf16[256,128]{1,0:T(8,128)(2,1)S(1)}, bf16[256,128]{1,0:T(8,128)(2,1)S(1)}, u32[]{:S(2)}, u32[]{:S(2)}) collective-permute-start(bf16[256,128]{1,0:T(8,128)(2,1)S(1)} %coarse.1.own), channel_id=1, source_target_pairs={{0,1},{1,2},{2,3},{3,4},{4,5},{5,6},{6,7},{7,8},{8,9},{9,10},{10,1... | collective-permute-start | bytes 196616 | tf_op jit(solution)/shard_map/ppermute | solution.py:277
  40.9 1.9 %copy-start = (bf16[256,128]{1,0:T(8,128)(2,1)S(1)}, bf16[256,128]{1,0:T(8,128)(2,1)}, u32[]{:S(2)}) copy-start(bf16[256,128]{1,0:T(8,128)(2,1)} %first.7) | copy-start | bytes 196612
  40.9 2.0 %copy-start.1 = (bf16[128,128]{1,0:T(8,128)(2,1)S(1)}, bf16[128,128]{1,0:T(8,128)(2,1)}, u32[]{:S(2)}) copy-start(bf16[128,128]{1,0:T(8,128)(2,1)} %second.3) | copy-start | bytes 98308
  43.4 12.9 %collective-permute-start.18 = (bf16[256,128]{1,0:T(8,128)(2,1)S(1)}, bf16[256,128]{1,0:T(8,128)(2,1)S(1)}, u32[]{:S(2)}, u32[]{:S(2)}) collective-permute-start(bf16[256,128]{1,0:T(8,128)(2,1)S(1)} %lift_rim.1), channel_id=1, source_target_pairs={{0,1},{1,2},{2,3},{3,4},{4,5},{5,6},{6,7},{7,8},{8,9},{9,10},{10,1... | collective-permute-start | bytes 196616 | tf_op jit(solution)/shard_map/ppermute | solution.py:277
  46.3 10.0 %collective-permute-start.17 = (bf16[256,128]{1,0:T(8,128)(2,1)S(1)}, bf16[256,128]{1,0:T(8,128)(2,1)S(1)}, u32[]{:S(2)}, u32[]{:S(2)}) collective-permute-start(bf16[256,128]{1,0:T(8,128)(2,1)S(1)} %lift_rim.1), channel_id=1, source_target_pairs={{1,0},{2,1},{3,2},{4,3},{5,4},{6,5},{7,6},{8,7},{9,8},{10,9},{11,1... | collective-permute-start | bytes 196616 | tf_op jit(solution)/shard_map/ppermute | solution.py:278
  46.3 10.0 %collective-permute-start.16 = (bf16[256,128]{1,0:T(8,128)(2,1)S(1)}, bf16[256,128]{1,0:T(8,128)(2,1)S(1)}, u32[]{:S(2)}, u32[]{:S(2)}) collective-permute-start(bf16[256,128]{1,0:T(8,128)(2,1)S(1)} %lift_rim.1), channel_id=1, source_target_pairs={{48,64},{64,48},{112,128},{128,112},{176,192},{192,176},{240,256},... | collective-permute-start | bytes 196616 | tf_op jit(solution)/shard_map/ppermute | solution.py:271
  51.5 4.9 %collective-permute-start.15 = (bf16[256,128]{1,0:T(8,128)(2,1)S(1)}, bf16[256,128]{1,0:T(8,128)(2,1)S(1)}, u32[]{:S(2)}, u32[]{:S(2)}) collective-permute-start(bf16[256,128]{1,0:T(8,128)(2,1)S(1)} %lift_rim.1), channel_id=1, source_target_pairs={{16,0},{0,1},{18,2},{2,3},{20,4},{4,5},{22,6},{6,7},{24,8},{8,9},{... | collective-permute-start | bytes 196616 | tf_op jit(solution)/shard_map/ppermute | solution.py:270
  51.5 4.9 %collective-permute-start.14 = (bf16[256,128]{1,0:T(8,128)(2,1)S(1)}, bf16[256,128]{1,0:T(8,128)(2,1)S(1)}, u32[]{:S(2)}, u32[]{:S(2)}) collective-permute-start(bf16[256,128]{1,0:T(8,128)(2,1)S(1)} %lift_rim.1), channel_id=1, source_target_pairs={{0,16},{1,0},{2,18},{3,2},{4,20},{5,4},{6,22},{7,6},{8,24},{9,8},{... | collective-permute-start | bytes 196616 | tf_op jit(solution)/shard_map/ppermute | solution.py:269
